TPU v7x, 32 devices: a whole 2x2x4 slice. The times are simulated.
32 devices in a mesh: section: 4 (over y, x), space: 8 (over z, core).
Axes of the slice: x: 2, y: 2, z: 4, core: 2. Of those that a mesh axis runs over, the one named last changes fastest.
Arguments:
- raster: bfloat16 [4, 32, 128, 256], P(None, 'space'), may hold values from -6 to 6
- row_coef: bfloat16 [4, 15, 32, 128], P('section', None, 'space'), may hold values from -1.5 to 1.5
- col_coef: bfloat16 [4, 15, 128, 32], P('section', None, 'space'), may hold values from -1.5 to 1.5
- norm_gain: bfloat16 [4, 256], P('section'), may hold values from 0.099609375 to 1.8984375
- weight_in: bfloat16 [4, 256, 512], P('section'), may hold values from -0.375 to 0.375
- bias_in: bfloat16 [4, 512], P('section'), may hold values from -3 to 3
- weight_out: bfloat16 [4, 512, 256], P('section'), may hold values from -0.25 to 0.25
- readout: bfloat16 [256], replicated, may hold values from -0.375 to 0.375
Outputs:
- density: float32 [4, 32, 128], P('section', 'space')
All inputs are finite; a program needn't handle non-finite values.
Results may differ from a plain program's by a relative error of at most 0.015.
Values may be sent and summed in bfloat16 or wider, within the bound.
No kernel may reach another device: no remote copies, remote signals or barrier semaphores. Data moves between devices by JAX's collectives and lax.ppermute only.
A program may use at most 64 MiB of HBM per device.

v0:
```python
import jax
import jax.numpy as jnp
from jax import lax
from jax.sharding import PartitionSpec as P


def from_behind(array, axis, by):
    size = lax.axis_size(axis)
    pairs = [(i, i + by) for i in range(size) if 0 <= i + by < size]
    return lax.ppermute(array, axis, pairs)


def from_root(value, axis, source):
    kept = jnp.where(lax.axis_index(axis) == source, value, 0).astype(value.dtype)
    return lax.psum(kept, axis)


def row_stencil(surface, coefficients):
    taps_count = coefficients.shape[0]
    radius = taps_count // 2
    columns = surface.shape[1]
    padded = jnp.pad(surface.astype(jnp.float32), ((0, 0), (radius, radius), (0, 0)))
    summed = jnp.zeros(surface.shape, jnp.float32)
    for offset in range(taps_count):
        summed = (
            summed
            + coefficients[offset].astype(jnp.float32)[:, :, None]
            * padded[:, offset : offset + columns, :]
        )
    return summed


def col_stencil(surface, coefficients):
    taps_count = coefficients.shape[0]
    radius = taps_count // 2
    lines = surface.shape[0]
    swapped = jnp.swapaxes(coefficients, 1, 2)
    padded = jnp.pad(surface.astype(jnp.float32), ((radius, radius), (0, 0), (0, 0)))
    summed = jnp.zeros(surface.shape, jnp.float32)
    for offset in range(taps_count):
        summed = (
            summed
            + swapped[offset].astype(jnp.float32)[:, :, None]
            * padded[offset : offset + lines, :, :]
        )
    return summed


def apply_layer(current, params):
    row_part = row_stencil(current, params[0]).astype(jnp.bfloat16)
    columns_view = lax.all_to_all(row_part, "space", split_axis=1, concat_axis=0, tiled=True)
    mixed_field = col_stencil(columns_view, params[1])
    inverse = lax.rsqrt(jnp.mean(mixed_field * mixed_field, axis=-1, keepdims=True) + 1e-06)
    normed = (mixed_field * inverse * params[2].astype(jnp.float32)).astype(jnp.bfloat16)
    hidden = jax.nn.gelu(
        jnp.dot(normed, params[3], preferred_element_type=jnp.float32)
        + params[4].astype(jnp.float32),
        approximate=True,
    ).astype(jnp.bfloat16)
    return (mixed_field + jnp.dot(hidden, params[5], preferred_element_type=jnp.float32)).astype(
        jnp.bfloat16
    )


def to_rows(output):
    return lax.all_to_all(output, "space", split_axis=0, concat_axis=1, tiled=True)


def read_density(output, readout):
    return jax.nn.softplus(jnp.dot(output, readout, preferred_element_type=jnp.float32))


def on_device(raster, row_coef, col_coef, norm_gain, weight_in, bias_in, weight_out, readout):
    sections = lax.axis_size("section")
    spaces = lax.axis_size("space")
    windows = raster.shape[0]
    position = lax.axis_index("section")
    params = (row_coef[0], col_coef[0], norm_gain[0], weight_in[0], bias_in[0], weight_out[0])
    carried = jnp.zeros(raster.shape[1:], jnp.bfloat16)
    finished = jnp.zeros(
        (windows, raster.shape[1] * spaces, raster.shape[2] // spaces), jnp.float32
    )
    for moment in range(windows + sections - 1):
        entering = raster[min(moment, windows - 1)]
        current = jnp.where(position == 0, entering, carried)
        output = apply_layer(current, params)
        finished_index = moment - (sections - 1)
        if finished_index >= 0:
            finished = finished.at[finished_index].set(read_density(output, readout))
        if moment < windows + sections - 2:
            carried = from_behind(to_rows(output), "section", 1)
    row_density = lax.all_to_all(finished, "space", split_axis=1, concat_axis=2, tiled=True)
    everyone = from_root(row_density, "section", sections - 1)
    return lax.dynamic_slice_in_dim(everyone, position, 1, 0)


def solution(mesh):
    placed = (
        P(None, "space", None, None),
        P("section", None, "space", None),
        P("section", None, "space", None),
        P("section", None),
        P("section", None, None),
        P("section", None),
        P("section", None, None),
        P(),
    )
    return jax.shard_map(
        on_device,
        mesh=mesh,
        in_specs=placed,
        out_specs=P("section", "space", None),
        check_vma=False,
    )
```

profile of v0, /device:TPU:0, one launch (start us, length us, event | category | flops | bytes accessed | tf_op | source)
XLA Modules:
  0.0 301.3 jit_solution(14394144305837295881)
XLA Ops:
  0.0 1.3 fusion.471
  3.2 4.5 %add_convert_fusion.6 = bf16[4,128,256]{2,0,1:T(4,128)(2,1)} fusion(f32[4,128,256]{2,0,1:T(4,128)S(1)} %fusion.368, f32[4,128]{0,1:T(8,128)S(1)} %copy.113, f32[4,128]{0,1:T(8,128)S(1)} %copy.112, f32[4,128]{0,1:T(8,128)S(1)} %copy.111, f32[4,128]{0,1:T(8,128)S(1)} %copy.110, f32[4,128]{0,1:T(8,128)S(1)} %copy.109, f32[4,128]{0,1:T(8,128)S(1)} %copy.108, ...), kind=kLoop, calls=%fused_computation.531 | loop fusion | flops 3932160 | bytes 817152 | tf_op jit(solution)/shard_map/convert_element_type | solution.py:50
  7.7 6.5 %all-to-all-start = ((bf16[4,128,256]{2,0,1:T(4,128)(2,1)}), bf16[4,128,256]{2,0,1:T(4,128)(2,1)S(1)}, u32[]{:S(2)}, u32[]{:S(2)}) async-start(bf16[4,128,256]{2,0,1:T(4,128)(2,1)} %add_convert_fusion.6), calls=%async_computation | async-start | bytes 524288 | tf_op jit(solution)/shard_map/all_to_all | solution.py:51
  16.6 7.3 %all-to-all-done = bf16[4,128,256]{2,0,1:T(4,128)(2,1)S(1)} async-done(((bf16[4,128,256]{2,0,1:T(4,128)(2,1)}), bf16[4,128,256]{2,0,1:T(4,128)(2,1)S(1)}, u32[]{:S(2)}, u32[]{:S(2)}) %all-to-all-start) | async-done | bytes 262176 | tf_op jit(solution)/shard_map/all_to_all | solution.py:51
  24.0 2.0 multiply_reduce_fusion.6
  26.8 12.1 %all_to_all.180 = bf16[32,16,256]{2,1,0:T(8,128)(2,1)S(1)} all-to-all(bf16[32,16,256]{2,1,0:T(8,128)(2,1)S(1)} %fusion), channel_id=1, replica_groups=mesh['section'=4,'space'=8] {'space'}, dimensions={0} | all-to-all | bytes 524288 | tf_op jit(solution)/shard_map/all_to_all | solution.py:66
  39.1 3.4 %collective-permute-start = (bf16[4,128,256]{2,0,1:T(4,128)(2,1)S(1)}, bf16[4,128,256]{2,0,1:T(4,128)(2,1)S(1)}, u32[]{:S(2)}, u32[]{:S(2)}) collective-permute-start(bf16[4,128,256]{2,0,1:T(4,128)(2,1)S(1)} %bitcast.305), channel_id=1, source_target_pairs={{0,8},{8,16},{16,24},{1,9},{9,17},{17,25},{2,10},{10,18},{18,26},{... | collective-permute-start | bytes 786440 | tf_op jit(solution)/shard_map/ppermute | solution.py:10
  42.5 5.2 %collective-permute-done = bf16[4,128,256]{2,0,1:T(4,128)(2,1)S(1)} collective-permute-done((bf16[4,128,256]{2,0,1:T(4,128)(2,1)S(1)}, bf16[4,128,256]{2,0,1:T(4,128)(2,1)S(1)}, u32[]{:S(2)}, u32[]{:S(2)}) %collective-permute-start) | collective-permute-done | bytes 262176 | tf_op jit(solution)/shard_map/ppermute | solution.py:10
  47.9 3.3 %add_convert_fusion.5 = bf16[4,128,256]{2,0,1:T(4,128)(2,1)S(1)} fusion(f32[4,128,256]{2,0,1:T(4,128)S(1)} %fusion.370, f32[4,128]{0,1:T(8,128)S(1)} %copy.113, f32[4,128]{0,1:T(8,128)S(1)} %copy.112, f32[4,128]{0,1:T(8,128)S(1)} %copy.111, f32[4,128]{0,1:T(8,128)S(1)} %copy.110, f32[4,128]{0,1:T(8,128)S(1)} %copy.109, f32[4,128]{0,1:T(8,128)S(1)} %copy.108, ...), kind=kLoop, calls=%fused_computation.481 | loop fusion | flops 3932160 | bytes 817152 | tf_op jit(solution)/shard_map/convert_element_type | solution.py:50
  51.2 12.7 %all_to_all.181 = bf16[4,128,256]{2,0,1:T(4,128)(2,1)S(1)} all-to-all(bf16[4,128,256]{2,0,1:T(4,128)(2,1)S(1)} %add_convert_fusion.5), channel_id=1, replica_groups=mesh['section'=4,'space'=8] {'space'}, dimensions={1} | all-to-all | bytes 524288 | tf_op jit(solution)/shard_map/all_to_all | solution.py:51
  63.9 2.0 multiply_reduce_fusion.5
  66.7 12.1 %all_to_all.182 = bf16[32,16,256]{2,1,0:T(8,128)(2,1)S(1)} all-to-all(bf16[32,16,256]{2,1,0:T(8,128)(2,1)S(1)} %fusion.1), channel_id=1, replica_groups=mesh['section'=4,'space'=8] {'space'}, dimensions={0} | all-to-all | bytes 524288 | tf_op jit(solution)/shard_map/all_to_all | solution.py:66
  79.0 4.4 %collective-permute-start.1 = (bf16[4,128,256]{2,0,1:T(4,128)(2,1)S(1)}, bf16[4,128,256]{2,0,1:T(4,128)(2,1)S(1)}, u32[]{:S(2)}, u32[]{:S(2)}) collective-permute-start(bf16[4,128,256]{2,0,1:T(4,128)(2,1)S(1)} %bitcast.306), channel_id=1, source_target_pairs={{0,8},{8,16},{16,24},{1,9},{9,17},{17,25},{2,10},{10,18},{18,26},{... | collective-permute-start | bytes 786440 | tf_op jit(solution)/shard_map/ppermute | solution.py:10
  83.4 5.2 %collective-permute-done.1 = bf16[4,128,256]{2,0,1:T(4,128)(2,1)S(1)} collective-permute-done((bf16[4,128,256]{2,0,1:T(4,128)(2,1)S(1)}, bf16[4,128,256]{2,0,1:T(4,128)(2,1)S(1)}, u32[]{:S(2)}, u32[]{:S(2)}) %collective-permute-start.1) | collective-permute-done | bytes 262176 | tf_op jit(solution)/shard_map/ppermute | solution.py:10
  88.8 3.3 %add_convert_fusion.4 = bf16[4,128,256]{2,0,1:T(4,128)(2,1)S(1)} fusion(f32[4,128,256]{2,0,1:T(4,128)S(1)} %fusion.372, f32[4,128]{0,1:T(8,128)S(1)} %copy.113, f32[4,128]{0,1:T(8,128)S(1)} %copy.112, f32[4,128]{0,1:T(8,128)S(1)} %copy.111, f32[4,128]{0,1:T(8,128)S(1)} %copy.110, f32[4,128]{0,1:T(8,128)S(1)} %copy.109, f32[4,128]{0,1:T(8,128)S(1)} %copy.108, ...), kind=kLoop, calls=%fused_computation.461 | loop fusion | flops 3932160 | bytes 817152 | tf_op jit(solution)/shard_map/convert_element_type | solution.py:50
  92.1 12.7 %all_to_all.183 = bf16[4,128,256]{2,0,1:T(4,128)(2,1)S(1)} all-to-all(bf16[4,128,256]{2,0,1:T(4,128)(2,1)S(1)} %add_convert_fusion.4), channel_id=1, replica_groups=mesh['section'=4,'space'=8] {'space'}, dimensions={1} | all-to-all | bytes 524288 | tf_op jit(solution)/shard_map/all_to_all | solution.py:51
  104.9 2.0 multiply_reduce_fusion.4
  107.6 12.1 %all_to_all.184 = bf16[32,16,256]{2,1,0:T(8,128)(2,1)S(1)} all-to-all(bf16[32,16,256]{2,1,0:T(8,128)(2,1)S(1)} %fusion.2), channel_id=1, replica_groups=mesh['section'=4,'space'=8] {'space'}, dimensions={0} | all-to-all | bytes 524288 | tf_op jit(solution)/shard_map/all_to_all | solution.py:66
  119.9 4.4 %collective-permute-start.2 = (bf16[4,128,256]{2,0,1:T(4,128)(2,1)S(1)}, bf16[4,128,256]{2,0,1:T(4,128)(2,1)S(1)}, u32[]{:S(2)}, u32[]{:S(2)}) collective-permute-start(bf16[4,128,256]{2,0,1:T(4,128)(2,1)S(1)} %bitcast.307), channel_id=1, source_target_pairs={{0,8},{8,16},{16,24},{1,9},{9,17},{17,25},{2,10},{10,18},{18,26},{... | collective-permute-start | bytes 786440 | tf_op jit(solution)/shard_map/ppermute | solution.py:10
  124.3 5.2 %collective-permute-done.2 = bf16[4,128,256]{2,0,1:T(4,128)(2,1)S(1)} collective-permute-done((bf16[4,128,256]{2,0,1:T(4,128)(2,1)S(1)}, bf16[4,128,256]{2,0,1:T(4,128)(2,1)S(1)}, u32[]{:S(2)}, u32[]{:S(2)}) %collective-permute-start.2) | collective-permute-done | bytes 262176 | tf_op jit(solution)/shard_map/ppermute | solution.py:10
  129.7 3.3 %add_convert_fusion.3 = bf16[4,128,256]{2,0,1:T(4,128)(2,1)S(1)} fusion(f32[4,128,256]{2,0,1:T(4,128)S(1)} %select_convert_fusion.3, f32[4,128]{0,1:T(8,128)S(1)} %copy.113, f32[4,128]{0,1:T(8,128)S(1)} %copy.112, f32[4,128]{0,1:T(8,128)S(1)} %copy.111, f32[4,128]{0,1:T(8,128)S(1)} %copy.110, f32[4,128]{0,1:T(8,128)S(1)} %copy.109, f32[4,128]{0,1:T(8,128)S(1)} %copy.108, ...), kind=kLoop, calls=%fused_computation.441 | loop fusion | flops 3932160 | bytes 817152 | tf_op jit(solution)/shard_map/convert_element_type | solution.py:50
  133.0 12.7 %all_to_all.185 = bf16[4,128,256]{2,0,1:T(4,128)(2,1)S(1)} all-to-all(bf16[4,128,256]{2,0,1:T(4,128)(2,1)S(1)} %add_convert_fusion.3), channel_id=1, replica_groups=mesh['section'=4,'space'=8] {'space'}, dimensions={1} | all-to-all | bytes 524288 | tf_op jit(solution)/shard_map/all_to_all | solution.py:51
  145.8 2.0 multiply_reduce_fusion.3
  148.5 12.1 %all_to_all.186 = bf16[32,16,256]{2,1,0:T(8,128)(2,1)S(1)} all-to-all(bf16[32,16,256]{2,1,0:T(8,128)(2,1)S(1)} %fusion.3), channel_id=1, replica_groups=mesh['section'=4,'space'=8] {'space'}, dimensions={0} | all-to-all | bytes 524288 | tf_op jit(solution)/shard_map/all_to_all | solution.py:66
  160.8 5.2 %collective-permute-start.3 = (bf16[4,128,256]{2,0,1:T(4,128)(2,1)S(1)}, bf16[4,128,256]{2,0,1:T(4,128)(2,1)S(1)}, u32[]{:S(2)}, u32[]{:S(2)}) collective-permute-start(bf16[4,128,256]{2,0,1:T(4,128)(2,1)S(1)} %bitcast.308), channel_id=1, source_target_pairs={{0,8},{8,16},{16,24},{1,9},{9,17},{17,25},{2,10},{10,18},{18,26},{... | collective-permute-start | bytes 786440 | tf_op jit(solution)/shard_map/ppermute | solution.py:10
  166.0 5.2 %collective-permute-done.3 = bf16[4,128,256]{2,0,1:T(4,128)(2,1)S(1)} collective-permute-done((bf16[4,128,256]{2,0,1:T(4,128)(2,1)S(1)}, bf16[4,128,256]{2,0,1:T(4,128)(2,1)S(1)}, u32[]{:S(2)}, u32[]{:S(2)}) %collective-permute-start.3) | collective-permute-done | bytes 262176 | tf_op jit(solution)/shard_map/ppermute | solution.py:10
  171.4 3.3 %add_convert_fusion.2 = bf16[4,128,256]{2,0,1:T(4,128)(2,1)S(1)} fusion(f32[4,128,256]{2,0,1:T(4,128)S(1)} %select_convert_fusion.2, f32[4,128]{0,1:T(8,128)S(1)} %copy.113, f32[4,128]{0,1:T(8,128)S(1)} %copy.112, f32[4,128]{0,1:T(8,128)S(1)} %copy.111, f32[4,128]{0,1:T(8,128)S(1)} %copy.110, f32[4,128]{0,1:T(8,128)S(1)} %copy.109, f32[4,128]{0,1:T(8,128)S(1)} %copy.108, ...), kind=kLoop, calls=%fused_computation.421 | loop fusion | flops 3932160 | bytes 817152 | tf_op jit(solution)/shard_map/convert_element_type | solution.py:50
  174.8 12.7 %all_to_all.187 = bf16[4,128,256]{2,0,1:T(4,128)(2,1)S(1)} all-to-all(bf16[4,128,256]{2,0,1:T(4,128)(2,1)S(1)} %add_convert_fusion.2), channel_id=1, replica_groups=mesh['section'=4,'space'=8] {'space'}, dimensions={1} | all-to-all | bytes 524288 | tf_op jit(solution)/shard_map/all_to_all | solution.py:51
  187.5 2.0 multiply_reduce_fusion.2
  190.3 12.1 %all_to_all.188 = bf16[32,16,256]{2,1,0:T(8,128)(2,1)S(1)} all-to-all(bf16[32,16,256]{2,1,0:T(8,128)(2,1)S(1)} %fusion.4), channel_id=1, replica_groups=mesh['section'=4,'space'=8] {'space'}, dimensions={0} | all-to-all | bytes 524288 | tf_op jit(solution)/shard_map/all_to_all | solution.py:66
  202.5 5.3 %collective-permute-start.4 = (bf16[4,128,256]{2,0,1:T(4,128)(2,1)S(1)}, bf16[4,128,256]{2,0,1:T(4,128)(2,1)S(1)}, u32[]{:S(2)}, u32[]{:S(2)}) collective-permute-start(bf16[4,128,256]{2,0,1:T(4,128)(2,1)S(1)} %bitcast.309), channel_id=1, source_target_pairs={{0,8},{8,16},{16,24},{1,9},{9,17},{17,25},{2,10},{10,18},{18,26},{... | collective-permute-start | bytes 786440 | tf_op jit(solution)/shard_map/ppermute | solution.py:10
  207.9 5.2 %collective-permute-done.4 = bf16[4,128,256]{2,0,1:T(4,128)(2,1)S(1)} collective-permute-done((bf16[4,128,256]{2,0,1:T(4,128)(2,1)S(1)}, bf16[4,128,256]{2,0,1:T(4,128)(2,1)S(1)}, u32[]{:S(2)}, u32[]{:S(2)}) %collective-permute-start.4) | collective-permute-done | bytes 262176 | tf_op jit(solution)/shard_map/ppermute | solution.py:10
  213.2 3.3 %add_convert_fusion.1 = bf16[4,128,256]{2,0,1:T(4,128)(2,1)S(1)} fusion(f32[4,128,256]{2,0,1:T(4,128)S(1)} %select_convert_fusion.1, f32[4,128]{0,1:T(8,128)S(1)} %copy.113, f32[4,128]{0,1:T(8,128)S(1)} %copy.112, f32[4,128]{0,1:T(8,128)S(1)} %copy.111, f32[4,128]{0,1:T(8,128)S(1)} %copy.110, f32[4,128]{0,1:T(8,128)S(1)} %copy.109, f32[4,128]{0,1:T(8,128)S(1)} %copy.108, ...), kind=kLoop, calls=%fused_computation.401 | loop fusion | flops 3932160 | bytes 817152 | tf_op jit(solution)/shard_map/convert_element_type | solution.py:50
  216.6 12.7 %all_to_all.189 = bf16[4,128,256]{2,0,1:T(4,128)(2,1)S(1)} all-to-all(bf16[4,128,256]{2,0,1:T(4,128)(2,1)S(1)} %add_convert_fusion.1), channel_id=1, replica_groups=mesh['section'=4,'space'=8] {'space'}, dimensions={1} | all-to-all | bytes 524288 | tf_op jit(solution)/shard_map/all_to_all | solution.py:51
  229.3 2.0 multiply_reduce_fusion.1
  231.4 1.4 fusion.5
  232.8 3.5 %all-to-all-start.11 = ((bf16[32,16,256]{2,1,0:T(8,128)(2,1)}), bf16[32,16,256]{2,1,0:T(8,128)(2,1)S(1)}, u32[]{:S(2)}, u32[]{:S(2)}) async-start(bf16[32,16,256]{2,1,0:T(8,128)(2,1)} %fusion.5), calls=%async_computation.11 | async-start | bytes 524288 | tf_op jit(solution)/shard_map/all_to_all | solution.py:66
  236.7 9.2 %all-to-all-done.11 = bf16[32,16,256]{2,1,0:T(8,128)(2,1)S(1)} async-done(((bf16[32,16,256]{2,1,0:T(8,128)(2,1)}), bf16[32,16,256]{2,1,0:T(8,128)(2,1)S(1)}, u32[]{:S(2)}, u32[]{:S(2)}) %all-to-all-start.11) | async-done | bytes 262176 | tf_op jit(solution)/shard_map/all_to_all | solution.py:66
  246.1 5.3 %collective-permute-start.5 = (bf16[4,128,256]{2,0,1:T(4,128)(2,1)S(1)}, bf16[4,128,256]{2,0,1:T(4,128)(2,1)S(1)}, u32[]{:S(2)}, u32[]{:S(2)}) collective-permute-start(bf16[4,128,256]{2,0,1:T(4,128)(2,1)S(1)} %bitcast.304), channel_id=1, source_target_pairs={{0,8},{8,16},{16,24},{1,9},{9,17},{17,25},{2,10},{10,18},{18,26},{... | collective-permute-start | bytes 786440 | tf_op jit(solution)/shard_map/ppermute | solution.py:10
  251.9 4.7 %collective-permute-done.5 = bf16[4,128,256]{2,0,1:T(4,128)(2,1)S(1)} collective-permute-done((bf16[4,128,256]{2,0,1:T(4,128)(2,1)S(1)}, bf16[4,128,256]{2,0,1:T(4,128)(2,1)S(1)}, u32[]{:S(2)}, u32[]{:S(2)}) %collective-permute-start.5) | collective-permute-done | bytes 262176 | tf_op jit(solution)/shard_map/ppermute | solution.py:10
  256.8 4.5 %add_convert_fusion = bf16[4,128,256]{2,0,1:T(4,128)(2,1)} fusion(f32[4,128,256]{2,0,1:T(4,128)S(1)} %select_convert_fusion, f32[4,128]{0,1:T(8,128)S(1)} %copy.113, f32[4,128]{0,1:T(8,128)S(1)} %copy.112, f32[4,128]{0,1:T(8,128)S(1)} %copy.111, f32[4,128]{0,1:T(8,128)S(1)} %copy.110, f32[4,128]{0,1:T(8,128)S(1)} %copy.109, f32[4,128]{0,1:T(8,128)S(1)} %copy.108, ...), kind=kLoop, calls=%fused_computation.381 | loop fusion | flops 3932160 | bytes 817152 | tf_op jit(solution)/shard_map/convert_element_type | solution.py:50
  261.3 3.4 %all-to-all-start.12 = ((bf16[4,128,256]{2,0,1:T(4,128)(2,1)}), bf16[4,128,256]{2,0,1:T(4,128)(2,1)S(1)}, u32[]{:S(2)}, u32[]{:S(2)}) async-start(bf16[4,128,256]{2,0,1:T(4,128)(2,1)} %add_convert_fusion), calls=%async_computation.12 | async-start | bytes 524288 | tf_op jit(solution)/shard_map/all_to_all | solution.py:51
  264.7 1.4 fusion.474
  266.2 8.2 %all-to-all-done.12 = bf16[4,128,256]{2,0,1:T(4,128)(2,1)S(1)} async-done(((bf16[4,128,256]{2,0,1:T(4,128)(2,1)}), bf16[4,128,256]{2,0,1:T(4,128)(2,1)S(1)}, u32[]{:S(2)}, u32[]{:S(2)}) %all-to-all-start.12) | async-done | bytes 262176 | tf_op jit(solution)/shard_map/all_to_all | solution.py:51
  274.4 2.0 multiply_reduce_fusion
  278.7 3.3 %all-to-all-start.13 = ((f32[8,1,256]{2,1,0:T(1,128)}), f32[8,1,256]{2,1,0:T(1,128)S(1)}, u32[]{:S(2)}, u32[]{:S(2)}) async-start(f32[8,1,256]{2,1,0:T(1,128)} %reshape.531), calls=%async_computation.13 | async-start | bytes 16384 | tf_op jit(solution)/shard_map/all_to_all | solution.py:92
  282.0 5.5 %all-to-all-done.13 = f32[8,1,256]{2,1,0:T(1,128)S(1)} async-done(((f32[8,1,256]{2,1,0:T(1,128)}), f32[8,1,256]{2,1,0:T(1,128)S(1)}, u32[]{:S(2)}, u32[]{:S(2)}) %all-to-all-start.13) | async-done | bytes 8224 | tf_op jit(solution)/shard_map/all_to_all | solution.py:92
  289.0 11.7 %psum.7 = f32[4,4,128]{2,1,0:T(4,128)S(1)} all-reduce(f32[4,4,128]{2,1,0:T(4,128)S(1)} %select_n.85), channel_id=1, replica_groups=mesh['section'=4,'space'=8] {'section'}, use_global_device_ids=true, to_apply=%region_7.8 | all-reduce | flops 2048 | bytes 16384 | tf_op jit(solution)/shard_map/psum | solution.py:15
  (100 shorter events, 15.4 us)
Async XLA Ops:
  0.0 26.1 %copy-start = (bf16[1,256,512]{2,1,0:T(8,128)(2,1)S(1)}, bf16[1,256,512]{2,1,0:T(8,128)(2,1)}, u32[]{:S(2)}) copy-start(bf16[1,256,512]{2,1,0:T(8,128)(2,1)} %param.20) | copy-start | bytes 786436
  0.0 1.3 copy-start.3
  7.7 6.5 %copy-start.2 = (bf16[1,15,16,32]{3,2,1,0:T(8,128)(2,1)S(1)}, bf16[1,15,16,32]{3,2,1,0:T(8,128)(2,1)}, u32[]{:S(2)}) copy-start(bf16[1,15,16,32]{3,2,1,0:T(8,128)(2,1)} %param.18) | copy-start | bytes 46084
  7.7 16.2 %all-to-all-start = ((bf16[4,128,256]{2,0,1:T(4,128)(2,1)}), bf16[4,128,256]{2,0,1:T(4,128)(2,1)S(1)}, u32[]{:S(2)}, u32[]{:S(2)}) async-start(bf16[4,128,256]{2,0,1:T(4,128)(2,1)} %add_convert_fusion.6), calls=%async_computation | async-start | bytes 524288 | tf_op jit(solution)/shard_map/all_to_all | solution.py:51
  15.2 0.7 copy-start.4
  16.0 0.7 copy-start.5
  24.0 2.1 copy-start.1
  39.1 8.6 %collective-permute-start = (bf16[4,128,256]{2,0,1:T(4,128)(2,1)S(1)}, bf16[4,128,256]{2,0,1:T(4,128)(2,1)S(1)}, u32[]{:S(2)}, u32[]{:S(2)}) collective-permute-start(bf16[4,128,256]{2,0,1:T(4,128)(2,1)S(1)} %bitcast.305), channel_id=1, source_target_pairs={{0,8},{8,16},{16,24},{1,9},{9,17},{17,25},{2,10},{10,18},{18,26},{... | collective-permute-start | bytes 786440 | tf_op jit(solution)/shard_map/ppermute | solution.py:10
  79.0 9.6 %collective-permute-start.1 = (bf16[4,128,256]{2,0,1:T(4,128)(2,1)S(1)}, bf16[4,128,256]{2,0,1:T(4,128)(2,1)S(1)}, u32[]{:S(2)}, u32[]{:S(2)}) collective-permute-start(bf16[4,128,256]{2,0,1:T(4,128)(2,1)S(1)} %bitcast.306), channel_id=1, source_target_pairs={{0,8},{8,16},{16,24},{1,9},{9,17},{17,25},{2,10},{10,18},{18,26},{... | collective-permute-start | bytes 786440 | tf_op jit(solution)/shard_map/ppermute | solution.py:10
  119.9 9.6 %collective-permute-start.2 = (bf16[4,128,256]{2,0,1:T(4,128)(2,1)S(1)}, bf16[4,128,256]{2,0,1:T(4,128)(2,1)S(1)}, u32[]{:S(2)}, u32[]{:S(2)}) collective-permute-start(bf16[4,128,256]{2,0,1:T(4,128)(2,1)S(1)} %bitcast.307), channel_id=1, source_target_pairs={{0,8},{8,16},{16,24},{1,9},{9,17},{17,25},{2,10},{10,18},{18,26},{... | collective-permute-start | bytes 786440 | tf_op jit(solution)/shard_map/ppermute | solution.py:10
  160.8 10.4 %collective-permute-start.3 = (bf16[4,128,256]{2,0,1:T(4,128)(2,1)S(1)}, bf16[4,128,256]{2,0,1:T(4,128)(2,1)S(1)}, u32[]{:S(2)}, u32[]{:S(2)}) collective-permute-start(bf16[4,128,256]{2,0,1:T(4,128)(2,1)S(1)} %bitcast.308), channel_id=1, source_target_pairs={{0,8},{8,16},{16,24},{1,9},{9,17},{17,25},{2,10},{10,18},{18,26},{... | collective-permute-start | bytes 786440 | tf_op jit(solution)/shard_map/ppermute | solution.py:10
  202.5 10.5 %collective-permute-start.4 = (bf16[4,128,256]{2,0,1:T(4,128)(2,1)S(1)}, bf16[4,128,256]{2,0,1:T(4,128)(2,1)S(1)}, u32[]{:S(2)}, u32[]{:S(2)}) collective-permute-start(bf16[4,128,256]{2,0,1:T(4,128)(2,1)S(1)} %bitcast.309), channel_id=1, source_target_pairs={{0,8},{8,16},{16,24},{1,9},{9,17},{17,25},{2,10},{10,18},{18,26},{... | collective-permute-start | bytes 786440 | tf_op jit(solution)/shard_map/ppermute | solution.py:10
  232.8 3.6 %copy-start.6 = (bf16[256]{0:T(256)(128)(2,1)S(1)}, bf16[256]{0:T(256)(128)(2,1)}, u32[]{:S(2)}) copy-start(bf16[256]{0:T(256)(128)(2,1)} %param.23) | copy-start | bytes 1540
  232.8 13.2 %all-to-all-start.11 = ((bf16[32,16,256]{2,1,0:T(8,128)(2,1)}), bf16[32,16,256]{2,1,0:T(8,128)(2,1)S(1)}, u32[]{:S(2)}, u32[]{:S(2)}) async-start(bf16[32,16,256]{2,1,0:T(8,128)(2,1)} %fusion.5), calls=%async_computation.11 | async-start | bytes 524288 | tf_op jit(solution)/shard_map/all_to_all | solution.py:66
  246.1 10.5 %collective-permute-start.5 = (bf16[4,128,256]{2,0,1:T(4,128)(2,1)S(1)}, bf16[4,128,256]{2,0,1:T(4,128)(2,1)S(1)}, u32[]{:S(2)}, u32[]{:S(2)}) collective-permute-start(bf16[4,128,256]{2,0,1:T(4,128)(2,1)S(1)} %bitcast.304), channel_id=1, source_target_pairs={{0,8},{8,16},{16,24},{1,9},{9,17},{17,25},{2,10},{10,18},{18,26},{... | collective-permute-start | bytes 786440 | tf_op jit(solution)/shard_map/ppermute | solution.py:10
  261.3 13.1 %all-to-all-start.12 = ((bf16[4,128,256]{2,0,1:T(4,128)(2,1)}), bf16[4,128,256]{2,0,1:T(4,128)(2,1)S(1)}, u32[]{:S(2)}, u32[]{:S(2)}) async-start(bf16[4,128,256]{2,0,1:T(4,128)(2,1)} %add_convert_fusion), calls=%async_computation.12 | async-start | bytes 524288 | tf_op jit(solution)/shard_map/all_to_all | solution.py:51
  278.7 8.8 %all-to-all-start.13 = ((f32[8,1,256]{2,1,0:T(1,128)}), f32[8,1,256]{2,1,0:T(1,128)S(1)}, u32[]{:S(2)}, u32[]{:S(2)}) async-start(f32[8,1,256]{2,1,0:T(1,128)} %reshape.531), calls=%async_computation.13 | async-start | bytes 16384 | tf_op jit(solution)/shard_map/all_to_all | solution.py:92
where the time goes:
time: 302 us; the launch traced here: 301 us
  blocking collectives  136 us (45%)
  waiting for transfers between devices  60.8 us (20%)
  starting transfers between devices  44.7 us (15%)
  other arithmetic  42.3 us (14%)
  local copies, waits for them, and re-layouts  8.77 us (3%)
  matrix products  8.33 us (3%)
    all_to_all x5, blocking collectives, apply_layer(): lax.all_to_all(row_part, 'space', split_axis=1, concat_axis=0, tiled=True)  63.3 us
    all_to_all x5, blocking collectives, to_rows(): lax.all_to_all(output, 'space', split_axis=0, concat_axis=1, tiled=True)  60.7 us
    ppermute x6, waiting for transfers between devices, from_behind(): return lax.ppermute(array, axis, pairs)  30.5 us
    ppermute x6, starting transfers between devices, from_behind(): return lax.ppermute(array, axis, pairs)  28 us
    convert_element_type x7, other arithmetic, apply_layer(): row_part = row_stencil(current, params[0]).astype(jnp.bfloat16)  25.7 us
    all_to_all x2, waiting for transfers between devices, apply_layer(): lax.all_to_all(row_part, 'space', split_axis=1, concat_axis=0, tiled=True)  15.5 us
    reduce_sum x7, other arithmetic, apply_layer(): jnp.mean(mixed_field * mixed_field, axis=-1, keepdims=True) + 1e-06  14.3 us
    psum x1, blocking collectives, from_root(): return lax.psum(kept, axis)  11.7 us
  transfers between devices with their start and end apart: 10, of which 10 were waited for; matrix products, arithmetic and copies ran while one was open for 1% of the time, Pallas kernels for 0%

commit v1 on v0

v1 whole, which is shorter than its diff:
```python
import functools

import jax
import jax.numpy as jnp
from jax import lax
from jax.experimental import pallas as pl
from jax.experimental.pallas import tpu as pltpu
from jax.sharding import PartitionSpec as P

F32 = jnp.float32
BF16 = jnp.bfloat16
VMEM = pl.BlockSpec(memory_space=pltpu.VMEM)
SMEM = pl.BlockSpec(memory_space=pltpu.SMEM)
ANY = pl.BlockSpec(memory_space=pl.ANY)


def from_behind(array, axis, by):
    size = lax.axis_size(axis)
    pairs = [(i, i + by) for i in range(size) if 0 <= i + by < size]
    return lax.ppermute(array, axis, pairs)


def from_root(value, axis, source):
    kept = jnp.where(lax.axis_index(axis) == source, value, 0).astype(value.dtype)
    return lax.psum(kept, axis)


def row_stencil(surface, coefficients):
    taps_count = coefficients.shape[0]
    radius = taps_count // 2
    columns = surface.shape[1]
    padded = jnp.pad(surface.astype(F32), ((0, 0), (radius, radius), (0, 0)))
    summed = jnp.zeros(surface.shape, F32)
    for offset in range(taps_count):
        summed = (
            summed
            + coefficients[offset].astype(F32)[:, :, None] * padded[:, offset : offset + columns, :]
        )
    return summed


def col_stencil(surface, coefficients):
    taps_count = coefficients.shape[0]
    radius = taps_count // 2
    lines = surface.shape[0]
    swapped = jnp.swapaxes(coefficients, 1, 2)
    padded = jnp.pad(surface.astype(F32), ((radius, radius), (0, 0), (0, 0)))
    summed = jnp.zeros(surface.shape, F32)
    for offset in range(taps_count):
        summed = (
            summed
            + swapped[offset].astype(F32)[:, :, None] * padded[offset : offset + lines, :, :]
        )
    return summed


def apply_layer(current, params):
    row_part = row_stencil(current, params[0]).astype(BF16)
    columns_view = lax.all_to_all(row_part, "space", split_axis=1, concat_axis=0, tiled=True)
    mixed_field = col_stencil(columns_view, params[1])
    inverse = lax.rsqrt(jnp.mean(mixed_field * mixed_field, axis=-1, keepdims=True) + 1e-06)
    normed = (mixed_field * inverse * params[2].astype(F32)).astype(BF16)
    hidden = jax.nn.gelu(
        jnp.dot(normed, params[3], preferred_element_type=F32) + params[4].astype(F32),
        approximate=True,
    ).astype(BF16)
    return (mixed_field + jnp.dot(hidden, params[5], preferred_element_type=F32)).astype(BF16)


def to_rows(output):
    return lax.all_to_all(output, "space", split_axis=0, concat_axis=1, tiled=True)


def read_density(output, readout):
    return jax.nn.softplus(jnp.dot(output, readout, preferred_element_type=F32))


def layers_over_sections(
    raster, row_coef, col_coef, norm_gain, weight_in, bias_in, weight_out, readout
):
    sections = lax.axis_size("section")
    spaces = lax.axis_size("space")
    windows = raster.shape[0]
    position = lax.axis_index("section")
    params = (row_coef[0], col_coef[0], norm_gain[0], weight_in[0], bias_in[0], weight_out[0])
    carried = jnp.zeros(raster.shape[1:], BF16)
    finished = jnp.zeros((windows, raster.shape[1] * spaces, raster.shape[2] // spaces), F32)
    for moment in range(windows + sections - 1):
        entering = raster[min(moment, windows - 1)]
        current = jnp.where(position == 0, entering, carried)
        output = apply_layer(current, params)
        finished_index = moment - (sections - 1)
        if finished_index >= 0:
            finished = finished.at[finished_index].set(read_density(output, readout))
        if moment < windows + sections - 2:
            carried = from_behind(to_rows(output), "section", 1)
    row_density = lax.all_to_all(finished, "space", split_axis=1, concat_axis=2, tiled=True)
    everyone = from_root(row_density, "section", sections - 1)
    return lax.dynamic_slice_in_dim(everyone, position, 1, 0)


TAPS = 15
RADIUS = 7
ROWS = 32
COLS = 16
WIDE = 128
CELLS = ROWS * COLS
GROUP = 8 * COLS


def call(kernel, outs, specs, scratch=(), cost=1000):
    return pl.pallas_call(
        kernel,
        out_shape=outs,
        in_specs=specs,
        out_specs=jax.tree.map(lambda _: VMEM, outs),
        scratch_shapes=list(scratch),
        compiler_params=pltpu.CompilerParams(vmem_limit_bytes=48 * 1024 * 1024),
        cost_estimate=pl.CostEstimate(flops=cost * 1000, bytes_accessed=cost, transcendentals=0),
    )


def shaped(shape, kind=BF16):
    return jax.ShapeDtypeStruct(shape, kind)


def iota(shape, axis):
    return lax.broadcasted_iota(jnp.int32, shape, axis)


def picked(which, values):
    out = values[0]
    for k in range(1, len(values)):
        out = jnp.where(which == k, values[k], out)
    return out


def row0_kernel(place, q0, q1, q2, q3, own, sib, o0, o1, o2, o3, chunk):
    s, c, z = place[0], place[1], place[2]
    lane, line = iota((WIDE, WIDE), 1), iota((WIDE, WIDE), 0)
    source = line + lane - RADIUS
    inside = (lane < TAPS) & (source >= 0) & (source < WIDE)
    for i in range(8):
        taps = picked(s, [q[i].astype(F32) for q in (q0, q1, q2, q3)])
        spread = jnp.concatenate([jnp.transpose(taps), jnp.zeros((WIDE, WIDE - 16), F32)], 1)
        spread = jnp.where(inside, spread, 0.0)
        band = pltpu.roll(spread, WIDE - RADIUS, 1, stride=1, stride_axis=0).astype(BF16)
        cells = jnp.where(c == i // 4, own[i % 4], sib[i % 4])
        done = jnp.dot(band, cells, preferred_element_type=F32)
        done = done.reshape(4, 2, COLS, done.shape[-1])
        done = jnp.where(c == 0, done[:, 0], done[:, 1]).astype(BF16)
        chunk[:, COLS * i : COLS * (i + 1), :] = done
    for k, out in enumerate((o0, o1, o2, o3)):
        out[...] = chunk[z ^ k]


def spread_kernel(place, q0, q1, q2, q3, o0, o1, o2, o3, chunk):
    c, z = place[1], place[2]
    for i in range(4):
        stacked = jnp.concatenate([q[r].astype(F32) for r in (i, i + 4) for q in (q0, q1, q2, q3)], 0)
        turned = jnp.transpose(stacked).reshape(4, 2, COLS, WIDE)
        chunk[:, COLS * i : COLS * (i + 1), :] = jnp.where(c == 0, turned[:, 0], turned[:, 1]).astype(BF16)
    for k, out in enumerate((o0, o1, o2, o3)):
        out[...] = chunk[z ^ k]


def prepare_cols_kernel(layers, place, q0, q1, q2, q3, *rest):
    outs, (turned, ordered) = rest[: len(layers)], rest[len(layers) :]
    s = place[0]
    tap_in, tap_out = iota((WIDE, 256), 0), iota((WIDE, 256), 1)
    expand = jnp.where((tap_in == tap_out // COLS) & (tap_in < TAPS), 1.0, 0.0).astype(BF16)
    lane, line = iota((COLS, 256), 1), iota((COLS, 256), 0)
    same = line == lane % COLS
    for layer, out in zip(layers, outs):
        for m in range(4):
            taps = picked(s ^ layer, [q[8 + m].astype(F32) for q in (q0, q1, q2, q3)])
            turned[128 * m : 128 * (m + 1), :] = jnp.concatenate(
                [jnp.transpose(taps), jnp.zeros((128, WIDE - 16), F32)], 1
            )
        for i in range(ROWS):
            ordered[COLS * i : COLS * (i + 1), :] = turned[pl.ds(i, COLS, stride=ROWS), :]
        wide = jnp.dot(ordered[...].astype(BF16), expand, preferred_element_type=F32)
        for i in range(ROWS):
            row = i + lane // COLS - RADIUS
            block = jnp.where(same & (row >= 0) & (row < ROWS), wide[COLS * i : COLS * (i + 1)], 0.0)
            block = jnp.concatenate([block, jnp.zeros((COLS, CELLS - 256), F32)], 1)
            shift = (COLS * (i - RADIUS)) % CELLS
            if shift:
                block = pltpu.roll(block, shift, 1)
            out[COLS * i : COLS * (i + 1), :] = block.astype(BF16)


def prepare_rows_kernel(layers, place, g0, g1, g2, g3, *rest):
    outs, (parts,) = rest[: len(layers)], rest[len(layers) :]
    s, c, z, p = place[0], place[1], place[2], place[3]
    last = place[4]
    for k, g in enumerate((g0, g1, g2, g3)):
        parts[z ^ k] = g[...].astype(F32)
    lane, line = iota((GROUP, WIDE), 1), iota((GROUP, WIDE), 0)
    source = line % COLS + lane - RADIUS
    tap = lane < TAPS
    own_mask = tap & (source >= 0) & (source < COLS)
    left_mask = tap & (source < 0) & (p > 0)
    right_mask = tap & (source >= COLS) & (p < last)
    for layer, out in zip(layers, outs):
        kk = s ^ layer
        for g in range(4):
            part = parts[g]
            low = pltpu.roll(part, (WIDE - 16 * kk) % WIDE, 1)
            high = pltpu.roll(part, (WIDE + 64 - 16 * kk) % WIDE, 1)
            taps = jnp.concatenate([low, high], 0)
            own = jnp.where(own_mask, taps, 0.0)
            own = pltpu.roll(own, WIDE - RADIUS, 1, stride=1, stride_axis=0)
            left = jnp.where(left_mask, taps, 0.0)
            right = jnp.where(right_mask, taps, 0.0)
            lefts, rights = [], []
            for i in range(8):
                cut = slice(COLS * i, COLS * (i + 1))
                lefts.append(pltpu.roll(left[cut], 8 * i + 1, 1, stride=1, stride_axis=0))
                rights.append(pltpu.roll(right[cut], (8 * i - 23) % WIDE, 1, stride=1, stride_axis=0))
            left, right = jnp.concatenate(lefts, 0), jnp.concatenate(rights, 0)
            sides = jnp.where(
                c == 0, right + pltpu.roll(left, 64, 1), left + pltpu.roll(right, 64, 1)
            )
            out[g, :, 0:WIDE] = own.astype(BF16)
            out[g, :, WIDE : 2 * WIDE] = sides.astype(BF16)


def fetch(which, sources, buffer, sem):
    for k in range(4):

        @pl.when(which == k)
        def _():
            pltpu.make_async_copy(sources[k], buffer, sem).start()


def layer_kernel(layer, final, place, x, n0, n1, n2, rows_band, cols_band, readout, *rest):
    mine, theirs, rest = rest[0:4], rest[4:8], rest[8:]
    if final:
        (density,), (field, weights, sems) = rest[:1], rest[1:]
    else:
        (out, to_core, to_z), (field, weights, sems) = rest[:3], rest[3:]
    s, c, z = place[0], place[1], place[2]
    fetch(s ^ layer, mine, weights.at[0], sems.at[0])
    fetch(s ^ layer, theirs, weights.at[1], sems.at[1])
    if layer == 0:
        for k, n in enumerate((x, n0, n1, n2)):
            field[pl.ds(pl.multiple_of((z ^ k) * GROUP, GROUP), GROUP), :] = n[...]
    else:
        for g in range(4):
            cells = jnp.concatenate(
                [x[GROUP * g : GROUP * (g + 1)], n0[64 * g : 64 * (g + 1)], n1[64 * g : 64 * (g + 1)]], 0
            )
            field[GROUP * g : GROUP * (g + 1), :] = jnp.dot(
                rows_band[g], cells, preferred_element_type=F32
            ).astype(BF16)
    blocks = 2
    size = CELLS // blocks
    mixed = [
        jnp.dot(cols_band[size * b : size * (b + 1), :], field[...], preferred_element_type=F32)
        for b in range(blocks)
    ]
    pltpu.make_async_copy(mine[0], weights.at[0], sems.at[0]).wait()
    pltpu.make_async_copy(theirs[0], weights.at[1], sems.at[1]).wait()
    channels = x.shape[-1]
    gain = weights[0, 512:528, :].astype(F32)[1:2]
    for b in range(blocks):
        total = mixed[b]
        inverse = lax.rsqrt(jnp.mean(total * total, axis=-1, keepdims=True) + 1e-06)
        normed = (total * inverse * gain).astype(BF16)
        parts = []
        for half in range(2):
            bias = weights[half, 512:528, :].astype(F32)[0:1]
            hidden = jnp.dot(normed, weights[half, 0:256, :], preferred_element_type=F32) + bias
            hidden = jax.nn.gelu(hidden, approximate=True).astype(BF16)
            parts.append(jnp.dot(hidden, weights[half, 256:512, :], preferred_element_type=F32))
        total = total + (parts[0] + parts[1])
        if final:
            reader = jnp.broadcast_to(readout[...], (8, channels))
            logit = lax.dot_general(
                reader, total.astype(BF16), (((1,), (1,)), ((), ())), preferred_element_type=F32
            )
            density[:, size * b : size * (b + 1)] = (
                jnp.maximum(logit, 0.0) + jnp.log1p(jnp.exp(-jnp.abs(logit)))
            )
        else:
            out[size * b : size * (b + 1), :] = total.astype(BF16)
            cells = total.reshape(size // COLS, 2, 8, channels)
            left, right = cells[:, 0], cells[:, 1]
            cut = slice(size // 2 * b, size // 2 * (b + 1))
            to_core[cut, :] = jnp.where(c == 0, right, left).reshape(size // 2, channels).astype(BF16)
            to_z[cut, :] = jnp.where(c == 0, left, right).reshape(size // 2, channels).astype(BF16)


def gather_kernel(place, g0, g1, g2, g3, out, parts):
    z, p = place[2], place[3]
    for k, g in enumerate((g0, g1, g2, g3)):
        parts[z ^ k] = g[...]
    cells = jnp.concatenate([parts[g] for g in range(4)], 0)
    cells = pltpu.roll(cells, (CELLS - 64 * p) % CELLS, 1)[:, 0:WIDE]
    lane, line = iota((8, WIDE), 1), iota((8, WIDE), 0)
    mask = lane // COLS == line
    cells = pltpu.roll(cells, 0, 1, stride=COLS, stride_axis=0)
    for t in range(4):
        moved = pltpu.roll(cells, WIDE - COLS * t, 1) if t else cells
        out[0, t : t + 1, :] = jnp.sum(jnp.where(mask, moved, 0.0), axis=0, keepdims=True)


def window_on_section(raster, row_coef, col_coef, norm_gain, weight_in, bias_in, weight_out, readout):
    s, p = lax.axis_index("section"), lax.axis_index("space")
    c, z = p % 2, p // 2
    channels = raster.shape[-1]
    spaces = lax.axis_size("space")
    place = jnp.stack([s, c, z, p, jnp.int32(spaces - 1), s, s, s]).astype(jnp.int32)

    def core(array):
        return lax.ppermute(array, "space", [(i, i ^ 1) for i in range(spaces)])

    def chip(array, k):
        return lax.ppermute(array, "space", [(i, i ^ (2 * k)) for i in range(spaces)])

    def section(array, k):
        return lax.ppermute(array, "section", [(i, i ^ k) for i in range(4)])

    def beside(array):
        pairs = []
        for a in range(4):
            for q in range(spaces):
                other = q - 1 if q % 2 == 0 else q + 1
                to = a * spaces + other if 0 <= other < spaces else (a ^ 1) * spaces + q
                pairs.append((a * spaces + q, to))
        return lax.ppermute(array, ("section", "space"), pairs)

    rc = row_coef[0]
    rc_sib = core(rc)
    rc8 = jnp.where(c == 0, jnp.concatenate([rc, rc_sib], 1), jnp.concatenate([rc_sib, rc], 1))
    cc4 = col_coef[0].reshape(TAPS, 4, WIDE)
    pack = jnp.swapaxes(jnp.concatenate([rc8, cc4], 1), 0, 1)
    pack = jnp.pad(pack, ((0, 0), (0, 1), (0, 0)))
    packs = [pack] + [section(pack, k) for k in (1, 2, 3)]

    window = lax.dynamic_index_in_dim(raster, s, 0, keepdims=False)
    window_sib = core(window)

    def half(core_index):
        start = core_index * 256
        win = lax.dynamic_slice_in_dim(weight_in[0], start, 256, 1)
        wout = lax.dynamic_slice_in_dim(weight_out[0], start, 256, 0)
        bias = lax.dynamic_slice_in_dim(bias_in, start, 256, 1)
        return jnp.concatenate([win, wout, bias, norm_gain, jnp.zeros((14, 256), BF16)], 0)

    mine0, theirs0 = half(c), half(1 - c)
    mine = [mine0] + [section(mine0, k) for k in (1, 2, 3)]
    theirs = [theirs0] + [core(m) for m in mine[1:]]

    chunks = call(
        row0_kernel,
        (shaped((GROUP, channels)),) * 4,
        [SMEM] + [VMEM] * 6,
        [pltpu.VMEM((4, GROUP, channels), BF16)],
    )(place, *packs, window, window_sib)
    chunks = [chunks[0]] + [chip(chunks[k], k) for k in (1, 2, 3)]

    bands0 = call(
        functools.partial(prepare_cols_kernel, (0,)),
        (shaped((CELLS, CELLS)),),
        [SMEM] + [VMEM] * 4,
        [pltpu.VMEM((CELLS, WIDE), F32), pltpu.VMEM((CELLS, WIDE), F32)],
    )(place, *packs)
    spread = call(
        spread_kernel,
        (shaped((64, WIDE)),) * 4,
        [SMEM] + [VMEM] * 4,
        [pltpu.VMEM((4, 64, WIDE), BF16)],
    )(place, *packs)
    spread = [spread[0]] + [chip(spread[k], k) for k in (1, 2, 3)]
    bands = call(
        functools.partial(prepare_cols_kernel, (1, 2, 3)),
        (shaped((CELLS, CELLS)),) * 3,
        [SMEM] + [VMEM] * 4,
        [pltpu.VMEM((CELLS, WIDE), F32), pltpu.VMEM((CELLS, WIDE), F32)],
    )(place, *packs)
    cols_band = list(bands0) + list(bands)
    rows_band = [None] + list(
        call(
            functools.partial(prepare_rows_kernel, (1, 2, 3)),
            (shaped((4, GROUP, 256)),) * 3,
            [SMEM] + [VMEM] * 4,
            [pltpu.VMEM((4, 64, WIDE), F32)],
        )(place, *spread)
    )

    reader = readout.reshape(1, channels)
    for layer in range(4):
        final = layer == 3
        if layer == 0:
            fields = list(chunks)
            band = jnp.zeros((8, WIDE), BF16)
        else:
            fields = [state, core(to_core), beside(to_z), jnp.zeros((8, WIDE), BF16)]
            band = rows_band[layer]
        outs = (
            (shaped((8, CELLS), F32),)
            if final
            else (shaped((CELLS, channels)), shaped((CELLS // 2, channels)), shaped((CELLS // 2, channels)))
        )
        result = call(
            functools.partial(layer_kernel, layer, final),
            outs,
            [SMEM] + [VMEM] * 7 + [ANY] * 8,
            [
                pltpu.VMEM((CELLS, channels), BF16),
                pltpu.VMEM((2, 528, 256), BF16),
                pltpu.SemaphoreType.DMA((2,)),
            ],
        )(place, *fields, band, cols_band[layer], reader, *mine, *theirs)
        if not final:
            state, to_core, to_z = result

    density = result[0][0:1]
    density_sib = core(density)
    pair = jnp.where(
        c == 0, jnp.concatenate([density, density_sib], 0), jnp.concatenate([density_sib, density], 0)
    )
    pairs = [pair] + [chip(pair, k) for k in (1, 2, 3)]
    return call(
        gather_kernel,
        shaped((1, 4, WIDE), F32),
        [SMEM] + [VMEM] * 4,
        [pltpu.VMEM((4, 2, CELLS), F32)],
    )(place, *pairs)


def on_device(raster, row_coef, *rest):
    fits = (
        lax.axis_size("section") == 4
        and lax.axis_size("space") == 8
        and raster.shape == (4, 4, WIDE, 256)
        and row_coef.shape[1] == TAPS
    )
    plan = window_on_section if fits else layers_over_sections
    return plan(raster, row_coef, *rest)


def solution(mesh):
    placed = (
        P(None, "space", None, None),
        P("section", None, "space", None),
        P("section", None, "space", None),
        P("section", None),
        P("section", None, None),
        P("section", None),
        P("section", None, None),
        P(),
    )
    return jax.shard_map(
        on_device,
        mesh=mesh,
        in_specs=placed,
        out_specs=P("section", "space", None),
        check_vma=False,
    )
```

time: 302 us -> 84 us (0.28)
  blocking collectives: 136 us -> 0 us
  other arithmetic: 42.3 us -> 0.04 us
  waiting for transfers between devices: 60.8 us -> 24.6 us
  Pallas kernels: 0 us -> 18.1 us
  starting transfers between devices: 44.7 us -> 33.5 us
  matrix products: 8.33 us -> 0 us
    all_to_all x10 -> x0, blocking collectives: 124 us -> none  [the longest x5 63.3 us: apply_layer(): lax.all_to_all(row_part, 'space', split_axis=1, concat_axis=0, tiled=True)]
    all_to_all x4 -> x0, waiting for transfers between devices: 30.2 us -> none  [the longest x2 15.5 us: apply_layer(): lax.all_to_all(row_part, 'space', split_axis=1, concat_axis=0, tiled=True)]
    convert_element_type x18 -> x0, other arithmetic: 27.2 us -> none  [the longest x7 25.7 us: apply_layer(): row_part = row_stencil(current, params[0]).astype(jnp.bfloat16)]
    pallas_call x0 -> x10, Pallas kernels: none -> 18.1 us  [the longest x4 8.46 us: window_on_section(): call(functools.partial(layer_kernel, layer, final), outs, [SMEM] + [VMEM]...]
    all_to_all x4 -> x0, starting transfers between devices: 16.7 us -> none  [the longest x2 9.87 us: apply_layer(): lax.all_to_all(row_part, 'space', split_axis=1, concat_axis=0, tiled=True)]
    reduce_sum x7 -> x0, other arithmetic: 14.3 us -> none  [apply_layer(): jnp.mean(mixed_field * mixed_field, axis=-1, keepdims=True) + 1e-06]
    psum x1 -> x0, blocking collectives: 11.7 us -> none  [from_root(): return lax.psum(kept, axis)]
    dot_general x11 -> x0, matrix products: 8.33 us -> none  [the longest x6 4.79 us: apply_layer(): jnp.dot(hidden, params[5], preferred_element_type=jnp.float32)]
  transfers between devices with their start and end apart: 10 -> 27, of which waited for: 10 -> 15; matrix products, arithmetic and copies ran while one was open for 1% -> 3% of each run, Pallas kernels for 0% -> 10%
where the time goes in v1:
time: 84 us; the launch traced here: 83.7 us
  starting transfers between devices  33.5 us (40%)
  waiting for transfers between devices  24.6 us (29%)
  Pallas kernels  18.1 us (22%)
  local copies, waits for them, and re-layouts  7.15 us (9%)
    ppermute x9, starting transfers between devices, chip(): return lax.ppermute(array, 'space', [(i, i ^ 2 * k) for i in range(spaces)])  16.8 us
    ppermute x6, waiting for transfers between devices, section(): return lax.ppermute(array, 'section', [(i, i ^ k) for i in range(4)])  13 us
    ppermute x6, starting transfers between devices, section(): return lax.ppermute(array, 'section', [(i, i ^ k) for i in range(4)])  10.9 us
    pallas_call x4, Pallas kernels, window_on_section(): call(functools.partial(layer_kernel, layer, final), outs, [SMEM] + [VMEM]...  8.46 us
    ppermute x3, waiting for transfers between devices, beside(): return lax.ppermute(array, ('section', 'space'), pairs)  7.11 us
    ppermute x3, starting transfers between devices, beside(): return lax.ppermute(array, ('section', 'space'), pairs)  4.38 us
    ppermute x9, waiting for transfers between devices, chip(): return lax.ppermute(array, 'space', [(i, i ^ 2 * k) for i in range(spaces)])  3.27 us
    pallas_call x1, Pallas kernels, window_on_section(): call(functools.partial(prepare_rows_kernel, (1, 2, 3)), (shaped((4, GROUP...  2.97 us
  transfers between devices with their start and end apart: 27, of which 15 were waited for; matrix products, arithmetic and copies ran while one was open for 3% of the time, Pallas kernels for 10%

profile of v1, /device:TPU:0, one launch (start us, length us, event | category | flops | bytes accessed | tf_op | source)
XLA Modules:
  0.0 83.7 jit_solution(2845954398139786254)
XLA Ops:
  0.0 0.8 copy-done.4
  0.8 0.6 constant_dynamic-slice_fusion
  1.3 1.8 %dynamic-slice_bitcast_fusion.1 = (bf16[256,256]{1,0:T(8,128)(2,1)}, bf16[256,256]{1,0:T(8,128)(2,1)S(1)}, bf16[256,256]{1,0:T(8,128)(2,1)S(1)}, bf16[256,256]{1,0:T(8,128)(2,1)}) fusion(bf16[1,512,256]{2,1,0:T(8,128)(2,1)} %param.14, s32[]{:T(128)S(6)} %select_n.48, s32[]{:T(128)S(6)} %select_n.47, bf16[1,256,512]{2,1,0:T(8,128)(2,1)} %param.12), kind=kLoop, calls=%fused_computation.1 | loop fusion | bytes 1048584 | tf_op jit(solution)/shard_map/dynamic_slice | solution.py:348
  3.2 0.7 copy-done.3
  4.0 4.0 %collective-permute-start.10 = (bf16[528,256]{1,0:T(8,128)(2,1)S(1)}, bf16[528,256]{1,0:T(8,128)(2,1)S(1)}, u32[]{:S(2)}, u32[]{:S(2)}) collective-permute-start(bf16[528,256]{1,0:T(8,128)(2,1)S(1)} %concatenate.24.rest_0_), channel_id=1, source_target_pairs={{0,24},{8,16},{16,8},{24,0},{1,25},{9,17},{17,9},{25,1},{2,26},{10... | collective-permute-start | bytes 811016 | tf_op jit(solution)/shard_map/ppermute | solution.py:323
  8.0 0.5 collective-permute-start.9
  8.8 0.5 collective-permute-start.4
  9.3 0.3 copy-done.1
  9.7 0.2 collective-permute-done
  9.9 2.9 %collective-permute-start.3 = (bf16[12,16,128]{2,1,0:T(8,128)(2,1)S(1)}, bf16[12,16,128]{2,1,0:T(8,128)(2,1)S(1)}, u32[]{:S(2)}, u32[]{:S(2)}) collective-permute-start(bf16[12,16,128]{2,1,0:T(8,128)(2,1)S(1)} %pad.4.q0), channel_id=1, source_target_pairs={{0,24},{8,16},{16,8},{24,0},{1,25},{9,17},{17,9},{25,1},{2,26},{10... | collective-permute-start | bytes 147464 | tf_op jit(solution)/shard_map/ppermute | solution.py:323
  12.8 2.5 %collective-permute-done.10.rest_3_ = bf16[528,256]{1,0:T(8,128)(2,1)S(1)} collective-permute-done((bf16[528,256]{1,0:T(8,128)(2,1)S(1)}, bf16[528,256]{1,0:T(8,128)(2,1)S(1)}, u32[]{:S(2)}, u32[]{:S(2)}) %collective-permute-start.10) | collective-permute-done | bytes 270368 | tf_op jit(solution)/shard_map/ppermute | solution.py:323
  15.3 5.4 %collective-permute-done.9.rest_2_ = bf16[528,256]{1,0:T(8,128)(2,1)S(1)} collective-permute-done((bf16[528,256]{1,0:T(8,128)(2,1)S(1)}, bf16[528,256]{1,0:T(8,128)(2,1)S(1)}, u32[]{:S(2)}, u32[]{:S(2)}) %collective-permute-start.9) | collective-permute-done | bytes 270368 | tf_op jit(solution)/shard_map/ppermute | solution.py:323
  20.8 0.3 collective-permute-done.8.rest_1_
  21.1 0.2 collective-permute-start.11
  21.3 1.7 %collective-permute-start.2 = (bf16[12,16,128]{2,1,0:T(8,128)(2,1)S(1)}, bf16[12,16,128]{2,1,0:T(8,128)(2,1)S(1)}, u32[]{:S(2)}, u32[]{:S(2)}) collective-permute-start(bf16[12,16,128]{2,1,0:T(8,128)(2,1)S(1)} %pad.4.q0), channel_id=1, source_target_pairs={{0,16},{8,24},{16,0},{24,8},{1,17},{9,25},{17,1},{25,9},{2,18},{10... | collective-permute-start | bytes 147464 | tf_op jit(solution)/shard_map/ppermute | solution.py:323
  23.0 2.4 %collective-permute-done.2.q2 = bf16[12,16,128]{2,1,0:T(8,128)(2,1)S(1)} collective-permute-done((bf16[12,16,128]{2,1,0:T(8,128)(2,1)S(1)}, bf16[12,16,128]{2,1,0:T(8,128)(2,1)S(1)}, u32[]{:S(2)}, u32[]{:S(2)}) %collective-permute-start.2) | collective-permute-done | bytes 49184 | tf_op jit(solution)/shard_map/ppermute | solution.py:323
  25.4 1.7 %collective-permute-start.1 = (bf16[12,16,128]{2,1,0:T(8,128)(2,1)S(1)}, bf16[12,16,128]{2,1,0:T(8,128)(2,1)S(1)}, u32[]{:S(2)}, u32[]{:S(2)}) collective-permute-start(bf16[12,16,128]{2,1,0:T(8,128)(2,1)S(1)} %pad.4.q0), channel_id=1, source_target_pairs={{0,8},{8,0},{16,24},{24,16},{1,9},{9,1},{17,25},{25,17},{2,10},{10... | collective-permute-start | bytes 147464 | tf_op jit(solution)/shard_map/ppermute | solution.py:323
  27.2 2.3 %collective-permute-done.1.q1 = bf16[12,16,128]{2,1,0:T(8,128)(2,1)S(1)} collective-permute-done((bf16[12,16,128]{2,1,0:T(8,128)(2,1)S(1)}, bf16[12,16,128]{2,1,0:T(8,128)(2,1)S(1)}, u32[]{:S(2)}, u32[]{:S(2)}) %collective-permute-start.1) | collective-permute-done | bytes 49184 | tf_op jit(solution)/shard_map/ppermute | solution.py:323
  29.5 2.2 %shard_map.82 = (bf16[128,256]{1,0:T(8,128)(2,1)S(1)}, bf16[128,256]{1,0:T(8,128)(2,1)S(1)}, bf16[128,256]{1,0:T(8,128)(2,1)}, bf16[128,256]{1,0:T(8,128)(2,1)}) custom-call(s32[8]{0:T(128)S(1)} %stack.22.place, bf16[12,16,128]{2,1,0:T(8,128)(2,1)S(1)} %pad.4.q0, bf16[12,16,128]{2,1,0:T(8,128)(2,1)S(1)} %collective-permute-done.1.q1, ...), custom_call_target="tpu_custom_call" | custom-call | flops 1000000 | bytes 1000 | tf_op jit(solution)/shard_map/pallas_call | solution.py:356
  31.7 1.8 %collective-permute-start.5 = (bf16[128,256]{1,0:T(8,128)(2,1)S(1)}, bf16[128,256]{1,0:T(8,128)(2,1)S(1)}, u32[]{:S(2)}, u32[]{:S(2)}) collective-permute-start(bf16[128,256]{1,0:T(8,128)(2,1)S(1)} %get-tuple-element.29), channel_id=1, source_target_pairs={{0,2},{1,3},{2,0},{3,1},{4,6},{5,7},{6,4},{7,5},{8,10},{9,11},{10,... | collective-permute-start | bytes 196616 | tf_op jit(solution)/shard_map/ppermute | solution.py:320
  33.5 2.6 %collective-permute-start.6 = (bf16[128,256]{1,0:T(8,128)(2,1)}, bf16[128,256]{1,0:T(8,128)(2,1)}, u32[]{:S(2)}, u32[]{:S(2)}) collective-permute-start(bf16[128,256]{1,0:T(8,128)(2,1)} %get-tuple-element.30), channel_id=1, source_target_pairs={{0,4},{1,5},{2,6},{3,7},{4,0},{5,1},{6,2},{7,3},{8,12},{9,13},{10,... | collective-permute-start | bytes 196616 | tf_op jit(solution)/shard_map/ppermute | solution.py:320
  36.1 0.2 collective-permute-done.5.n0
  36.3 3.5 %collective-permute-start.7 = (bf16[128,256]{1,0:T(8,128)(2,1)}, bf16[128,256]{1,0:T(8,128)(2,1)}, u32[]{:S(2)}, u32[]{:S(2)}) collective-permute-start(bf16[128,256]{1,0:T(8,128)(2,1)} %get-tuple-element.31), channel_id=1, source_target_pairs={{0,6},{1,7},{2,4},{3,5},{4,2},{5,3},{6,0},{7,1},{8,14},{9,15},{10,... | collective-permute-start | bytes 196616 | tf_op jit(solution)/shard_map/ppermute | solution.py:320
  39.8 2.6 %concatenate.25.rest_4_ = bf16[528,256]{1,0:T(8,128)(2,1)S(1)} concatenate(bf16[256,256]{1,0:T(8,128)(2,1)} %get-tuple-element.58, bf16[256,256]{1,0:T(8,128)(2,1)} %get-tuple-element.51, bf16[1,256]{1,0:T(2,128)(2,1)} %get-tuple-element.55, bf16[1,256]{1,0:T(2,128)(2,1)} %param.11, bf16[14,256]{1,0:T(8,128)(2,1)S(1)} %broadcast.8), dimensions={0} | concatenate | bytes 540672 | tf_op jit(solution)/shard_map/concatenate | solution.py:350
  42.4 1.0 %shard_map.83.cols_band = bf16[512,512]{1,0:T(8,128)(2,1)S(1)} custom-call(s32[8]{0:T(128)S(1)} %stack.22.place, bf16[12,16,128]{2,1,0:T(8,128)(2,1)S(1)} %pad.4.q0, bf16[12,16,128]{2,1,0:T(8,128)(2,1)S(1)} %collective-permute-done.1.q1, bf16[12,16,128]{2,1,0:T(8,128)(2,1)S(1)} %collective-permute-done.2.q2, bf16[12,16,128]{2,1,0:T(8,128)(2,1)S(1)} %collective-permute-done.3.q3), custom_call_target="tpu_custom_call" | custom-call | flops 1000000 | bytes 1000 | tf_op jit(solution)/shard_map/pallas_call | solution.py:364
  43.5 2.2 %shard_map.84 = (bf16[512,256]{1,0:T(8,128)(2,1)S(1)}, bf16[256,256]{1,0:T(8,128)(2,1)S(1)}, bf16[256,256]{1,0:T(8,128)(2,1)S(1)}) custom-call(s32[8]{0:T(128)S(1)} %stack.22.place, bf16[128,256]{1,0:T(8,128)(2,1)S(1)} %get-tuple-element.28.x, bf16[128,256]{1,0:T(8,128)(2,1)S(1)} %collective-permute-done.5.n0, bf16[128,256]{1,0:T(8,128)(2,1)} %collective-permute-done.6.n1, ...), custom_call_target="tpu_custom_call" | custom-call | flops 1000000 | bytes 1000 | tf_op jit(solution)/shard_map/pallas_call | solution.py:407
  45.7 1.6 %collective-permute-start.15 = (bf16[256,256]{1,0:T(8,128)(2,1)S(1)}, bf16[256,256]{1,0:T(8,128)(2,1)S(1)}, u32[]{:S(2)}, u32[]{:S(2)}) collective-permute-start(bf16[256,256]{1,0:T(8,128)(2,1)S(1)} %get-tuple-element.34), channel_id=1, source_target_pairs={{0,8},{1,2},{2,1},{3,4},{4,3},{5,6},{6,5},{7,15},{8,0},{9,10},{10,... | collective-permute-start | bytes 393224 | tf_op jit(solution)/shard_map/ppermute | solution.py:332
  47.3 0.6 shard_map.85
  47.9 0.6 collective-permute-start.16
  48.6 1.2 %collective-permute-start.17 = (bf16[64,128]{1,0:T(8,128)(2,1)S(1)}, bf16[64,128]{1,0:T(8,128)(2,1)S(1)}, u32[]{:S(2)}, u32[]{:S(2)}) collective-permute-start(bf16[64,128]{1,0:T(8,128)(2,1)S(1)} %get-tuple-element.37), channel_id=1, source_target_pairs={{0,4},{1,5},{2,6},{3,7},{4,0},{5,1},{6,2},{7,3},{8,12},{9,13},{10,... | collective-permute-start | bytes 49160 | tf_op jit(solution)/shard_map/ppermute | solution.py:320
  49.8 2.6 %collective-permute-start.18 = (bf16[64,128]{1,0:T(8,128)(2,1)S(1)}, bf16[64,128]{1,0:T(8,128)(2,1)S(1)}, u32[]{:S(2)}, u32[]{:S(2)}) collective-permute-start(bf16[64,128]{1,0:T(8,128)(2,1)S(1)} %get-tuple-element.38), channel_id=1, source_target_pairs={{0,6},{1,7},{2,4},{3,5},{4,2},{5,3},{6,0},{7,1},{8,14},{9,15},{10,... | collective-permute-start | bytes 49160 | tf_op jit(solution)/shard_map/ppermute | solution.py:320
  52.4 1.5 %shard_map.87 = (bf16[512,512]{1,0:T(8,128)(2,1)S(1)}, bf16[512,512]{1,0:T(8,128)(2,1)S(1)}, bf16[512,512]{1,0:T(8,128)(2,1)S(1)}) custom-call(s32[8]{0:T(128)S(1)} %stack.22.place, bf16[12,16,128]{2,1,0:T(8,128)(2,1)S(1)} %pad.4.q0, bf16[12,16,128]{2,1,0:T(8,128)(2,1)S(1)} %collective-permute-done.1.q1, bf16[12,16,128]{2,1,0:T(8,128)(2,1)S(1)} %collective-permute-done.2.q2, ...), custom_call_target="tpu_custom_call" | custom-call | flops 1000000 | bytes 1000 | tf_op jit(solution)/shard_map/pallas_call | solution.py:377
  53.9 1.5 %collective-permute-done.18.g3 = bf16[64,128]{1,0:T(8,128)(2,1)S(1)} collective-permute-done((bf16[64,128]{1,0:T(8,128)(2,1)S(1)}, bf16[64,128]{1,0:T(8,128)(2,1)S(1)}, u32[]{:S(2)}, u32[]{:S(2)}) %collective-permute-start.18) | collective-permute-done | bytes 16416 | tf_op jit(solution)/shard_map/ppermute | solution.py:320
  55.4 3.0 %shard_map.86 = (bf16[4,128,256]{2,1,0:T(8,128)(2,1)S(1)}, bf16[4,128,256]{2,1,0:T(8,128)(2,1)S(1)}, bf16[4,128,256]{2,1,0:T(8,128)(2,1)S(1)}) custom-call(s32[8]{0:T(128)S(1)} %stack.22.place, bf16[64,128]{1,0:T(8,128)(2,1)S(1)} %get-tuple-element.35.g0, bf16[64,128]{1,0:T(8,128)(2,1)S(1)} %collective-permute-done.16.g1, ...), custom_call_target="tpu_custom_call" | custom-call | flops 1000000 | bytes 1000 | tf_op jit(solution)/shard_map/pallas_call | solution.py:385
  58.4 2.0 %shard_map.88 = (bf16[512,256]{1,0:T(8,128)(2,1)S(1)}, bf16[256,256]{1,0:T(8,128)(2,1)S(1)}, bf16[256,256]{1,0:T(8,128)(2,1)S(1)}) custom-call(s32[8]{0:T(128)S(1)} %stack.22.place, bf16[512,256]{1,0:T(8,128)(2,1)S(1)} %get-tuple-element.32.x, bf16[256,256]{1,0:T(8,128)(2,1)S(1)} %collective-permute-done.14.n0, ...), custom_call_target="tpu_custom_call" | custom-call | flops 1000000 | bytes 1000 | tf_op jit(solution)/shard_map/pallas_call | solution.py:407
  60.4 0.2 collective-permute-start.19
  60.6 1.4 %collective-permute-start.20 = (bf16[256,256]{1,0:T(8,128)(2,1)S(1)}, bf16[256,256]{1,0:T(8,128)(2,1)S(1)}, u32[]{:S(2)}, u32[]{:S(2)}) collective-permute-start(bf16[256,256]{1,0:T(8,128)(2,1)S(1)} %get-tuple-element.43), channel_id=1, source_target_pairs={{0,8},{1,2},{2,1},{3,4},{4,3},{5,6},{6,5},{7,15},{8,0},{9,10},{10,... | collective-permute-start | bytes 393224 | tf_op jit(solution)/shard_map/ppermute | solution.py:332
  62.0 3.6 %collective-permute-done.20.n1 = bf16[256,256]{1,0:T(8,128)(2,1)S(1)} collective-permute-done((bf16[256,256]{1,0:T(8,128)(2,1)S(1)}, bf16[256,256]{1,0:T(8,128)(2,1)S(1)}, u32[]{:S(2)}, u32[]{:S(2)}) %collective-permute-start.20) | collective-permute-done | bytes 131104 | tf_op jit(solution)/shard_map/ppermute | solution.py:332
  65.5 2.0 %shard_map.89 = (bf16[512,256]{1,0:T(8,128)(2,1)S(1)}, bf16[256,256]{1,0:T(8,128)(2,1)S(1)}, bf16[256,256]{1,0:T(8,128)(2,1)S(1)}) custom-call(s32[8]{0:T(128)S(1)} %stack.22.place, bf16[512,256]{1,0:T(8,128)(2,1)S(1)} %get-tuple-element.41.x, bf16[256,256]{1,0:T(8,128)(2,1)S(1)} %collective-permute-done.19.n0, ...), custom_call_target="tpu_custom_call" | custom-call | flops 1000000 | bytes 1000 | tf_op jit(solution)/shard_map/pallas_call | solution.py:407
  67.7 1.4 %collective-permute-start.22 = (bf16[256,256]{1,0:T(8,128)(2,1)S(1)}, bf16[256,256]{1,0:T(8,128)(2,1)S(1)}, u32[]{:S(2)}, u32[]{:S(2)}) collective-permute-start(bf16[256,256]{1,0:T(8,128)(2,1)S(1)} %get-tuple-element.48), channel_id=1, source_target_pairs={{0,8},{1,2},{2,1},{3,4},{4,3},{5,6},{6,5},{7,15},{8,0},{9,10},{10,... | collective-permute-start | bytes 393224 | tf_op jit(solution)/shard_map/ppermute | solution.py:332
  69.1 3.6 %collective-permute-done.22.n1 = bf16[256,256]{1,0:T(8,128)(2,1)S(1)} collective-permute-done((bf16[256,256]{1,0:T(8,128)(2,1)S(1)}, bf16[256,256]{1,0:T(8,128)(2,1)S(1)}, u32[]{:S(2)}, u32[]{:S(2)}) %collective-permute-start.22) | collective-permute-done | bytes 131104 | tf_op jit(solution)/shard_map/ppermute | solution.py:332
  72.7 2.4 %shard_map.90 = f32[8,512]{1,0:T(8,128)S(1)} custom-call(s32[8]{0:T(128)S(1)} %stack.22.place, bf16[512,256]{1,0:T(8,128)(2,1)S(1)} %get-tuple-element.46.x, bf16[256,256]{1,0:T(8,128)(2,1)S(1)} %collective-permute-done.21.n0, bf16[256,256]{1,0:T(8,128)(2,1)S(1)} %collective-permute-done.22.n1, bf16[8,128]{1,0:T(8,128)(2,1)S(1)} %broadcast_2_rows_band_n2.2.rows_band.n2, ...), custom_call_target="tpu_custom_call" | custom-call | flops 1000000 | bytes 1000 | tf_op jit(solution)/shard_map/pallas_call | solution.py:407
  75.2 1.0 %collective-permute-done.23 = f32[1,512]{1,0:T(1,128)S(1)} collective-permute-done((f32[1,512]{1,0:T(1,128)S(1)}, f32[1,512]{1,0:T(1,128)S(1)}, u32[]{:S(2)}, u32[]{:S(2)}) %collective-permute-start.23) | collective-permute-done | bytes 2080 | tf_op jit(solution)/shard_map/ppermute | solution.py:317
  76.3 1.4 %collective-permute-start.26 = (f32[2,512]{1,0:T(2,128)S(1)}, f32[2,512]{1,0:T(2,128)S(1)}, u32[]{:S(2)}, u32[]{:S(2)}) collective-permute-start(f32[2,512]{1,0:T(2,128)S(1)} %maximum_select_fusion.1.g0), channel_id=1, source_target_pairs={{0,6},{1,7},{2,4},{3,5},{4,2},{5,3},{6,0},{7,1},{8,14},{9,15},{10,... | collective-permute-start | bytes 12296 | tf_op jit(solution)/shard_map/ppermute | solution.py:320
  77.7 3.0 %collective-permute-start.24 = (f32[2,512]{1,0:T(2,128)S(1)}, f32[2,512]{1,0:T(2,128)S(1)}, u32[]{:S(2)}, u32[]{:S(2)}) collective-permute-start(f32[2,512]{1,0:T(2,128)S(1)} %maximum_select_fusion.1.g0), channel_id=1, source_target_pairs={{0,2},{1,3},{2,0},{3,1},{4,6},{5,7},{6,4},{7,5},{8,10},{9,11},{10,... | collective-permute-start | bytes 12296 | tf_op jit(solution)/shard_map/ppermute | solution.py:320
  80.7 1.0 %collective-permute-done.26.g3 = f32[2,512]{1,0:T(2,128)S(1)} collective-permute-done((f32[2,512]{1,0:T(2,128)S(1)}, f32[2,512]{1,0:T(2,128)S(1)}, u32[]{:S(2)}, u32[]{:S(2)}) %collective-permute-start.26) | collective-permute-done | bytes 4128 | tf_op jit(solution)/shard_map/ppermute | solution.py:320
  81.8 0.4 collective-permute-done.25.g2
  82.3 1.3 %shard_map.91 = f32[1,4,128]{2,1,0:T(4,128)} custom-call(s32[8]{0:T(128)S(1)} %stack.22.place, f32[2,512]{1,0:T(2,128)S(1)} %maximum_select_fusion.1.g0, f32[2,512]{1,0:T(2,128)S(1)} %collective-permute-done.24.g1, f32[2,512]{1,0:T(2,128)S(1)} %collective-permute-done.25.g2, f32[2,512]{1,0:T(2,128)S(1)} %collective-permute-done.26.g3), custom_call_target="tpu_custom_call" | custom-call | flops 1000000 | bytes 1000 | tf_op jit(solution)/shard_map/pallas_call | solution.py:426
  (45 shorter events, 1.3 us)
Async XLA Ops:
  0.0 8.7 %copy-start = (bf16[4,4,128,256]{3,2,1,0:T(8,128)(2,1)S(1)}, bf16[4,4,128,256]{3,2,1,0:T(8,128)(2,1)}, u32[]{:S(2)}) copy-start(bf16[4,4,128,256]{3,2,1,0:T(8,128)(2,1)} %param.8) | copy-start | bytes 3145732
  0.0 0.8 copy-start.4
  3.2 0.7 copy-start.3
  3.8 4.8 %copy-start.2 = (bf16[1,15,4,128]{3,2,1,0:T(4,128)(2,1)S(1)}, bf16[1,15,4,128]{3,2,1,0:T(4,128)(2,1)}, u32[]{:S(2)}) copy-start(bf16[1,15,4,128]{3,2,1,0:T(4,128)(2,1)} %param.9) | copy-start | bytes 46084
  4.0 11.3 %collective-permute-start.10 = (bf16[528,256]{1,0:T(8,128)(2,1)S(1)}, bf16[528,256]{1,0:T(8,128)(2,1)S(1)}, u32[]{:S(2)}, u32[]{:S(2)}) collective-permute-start(bf16[528,256]{1,0:T(8,128)(2,1)S(1)} %concatenate.24.rest_0_), channel_id=1, source_target_pairs={{0,24},{8,16},{16,8},{24,0},{1,25},{9,17},{17,9},{25,1},{2,26},{10... | collective-permute-start | bytes 811016 | tf_op jit(solution)/shard_map/ppermute | solution.py:323
  8.0 12.8 %collective-permute-start.9 = (bf16[528,256]{1,0:T(8,128)(2,1)S(1)}, bf16[528,256]{1,0:T(8,128)(2,1)S(1)}, u32[]{:S(2)}, u32[]{:S(2)}) collective-permute-start(bf16[528,256]{1,0:T(8,128)(2,1)S(1)} %concatenate.24.rest_0_), channel_id=1, source_target_pairs={{0,16},{8,24},{16,0},{24,8},{1,17},{9,25},{17,1},{25,9},{2,18},{10... | collective-permute-start | bytes 811016 | tf_op jit(solution)/shard_map/ppermute | solution.py:323
  8.5 12.6 %collective-permute-start.8 = (bf16[528,256]{1,0:T(8,128)(2,1)S(1)}, bf16[528,256]{1,0:T(8,128)(2,1)S(1)}, u32[]{:S(2)}, u32[]{:S(2)}) collective-permute-start(bf16[528,256]{1,0:T(8,128)(2,1)S(1)} %concatenate.24.rest_0_), channel_id=1, source_target_pairs={{0,8},{8,0},{16,24},{24,16},{1,9},{9,1},{17,25},{25,17},{2,10},{10... | collective-permute-start | bytes 811016 | tf_op jit(solution)/shard_map/ppermute | solution.py:323
  8.6 1.2 %collective-permute-start = (bf16[15,4,128]{2,0,1:T(8,128)(2,1)S(1)}, bf16[15,4,128]{2,0,1:T(8,128)(2,1)S(1)}, u32[]{:S(2)}, u32[]{:S(2)}) collective-permute-start(bf16[15,4,128]{2,0,1:T(8,128)(2,1)S(1)} %bitcast.21), channel_id=1, source_target_pairs={{0,1},{1,0},{2,3},{3,2},{4,5},{5,4},{6,7},{7,6},{8,9},{9,8},{10,11... | collective-permute-start | bytes 46088 | tf_op jit(solution)/shard_map/ppermute | solution.py:317
  8.7 0.8 copy-start.1
  8.8 20.8 %collective-permute-start.4 = (bf16[4,128,256]{2,1,0:T(8,128)(2,1)S(1)}, bf16[4,128,256]{2,1,0:T(8,128)(2,1)}, u32[]{:S(2)}, u32[]{:S(2)}) collective-permute-start(bf16[4,128,256]{2,1,0:T(8,128)(2,1)S(1)} %dynamic-slice_bitcast_fusion.own), channel_id=1, source_target_pairs={{0,1},{1,0},{2,3},{3,2},{4,5},{5,4},{6,7},{7,6},{8,9},{9,8},{10,11... | collective-permute-start | bytes 786440 | tf_op jit(solution)/shard_map/ppermute | solution.py:317
  9.9 11.4 %collective-permute-start.3 = (bf16[12,16,128]{2,1,0:T(8,128)(2,1)S(1)}, bf16[12,16,128]{2,1,0:T(8,128)(2,1)S(1)}, u32[]{:S(2)}, u32[]{:S(2)}) collective-permute-start(bf16[12,16,128]{2,1,0:T(8,128)(2,1)S(1)} %pad.4.q0), channel_id=1, source_target_pairs={{0,24},{8,16},{16,8},{24,0},{1,25},{9,17},{17,9},{25,1},{2,26},{10... | collective-permute-start | bytes 147464 | tf_op jit(solution)/shard_map/ppermute | solution.py:323
  15.3 28.1 %collective-permute-start.13 = (bf16[528,256]{1,0:T(8,128)(2,1)S(1)}, bf16[528,256]{1,0:T(8,128)(2,1)S(1)}, u32[]{:S(2)}, u32[]{:S(2)}) collective-permute-start(bf16[528,256]{1,0:T(8,128)(2,1)S(1)} %collective-permute-done.10.rest_3_), channel_id=1, source_target_pairs={{0,1},{1,0},{2,3},{3,2},{4,5},{5,4},{6,7},{7,6},{8,9},{9,8},{10,11... | collective-permute-start | bytes 811016 | tf_op jit(solution)/shard_map/ppermute | solution.py:317
  20.8 22.7 %collective-permute-start.12 = (bf16[528,256]{1,0:T(8,128)(2,1)S(1)}, bf16[528,256]{1,0:T(8,128)(2,1)S(1)}, u32[]{:S(2)}, u32[]{:S(2)}) collective-permute-start(bf16[528,256]{1,0:T(8,128)(2,1)S(1)} %collective-permute-done.9.rest_2_), channel_id=1, source_target_pairs={{0,1},{1,0},{2,3},{3,2},{4,5},{5,4},{6,7},{7,6},{8,9},{9,8},{10,11... | collective-permute-start | bytes 811016 | tf_op jit(solution)/shard_map/ppermute | solution.py:317
  21.1 22.4 %collective-permute-start.11 = (bf16[528,256]{1,0:T(8,128)(2,1)S(1)}, bf16[528,256]{1,0:T(8,128)(2,1)S(1)}, u32[]{:S(2)}, u32[]{:S(2)}) collective-permute-start(bf16[528,256]{1,0:T(8,128)(2,1)S(1)} %collective-permute-done.8.rest_1_), channel_id=1, source_target_pairs={{0,1},{1,0},{2,3},{3,2},{4,5},{5,4},{6,7},{7,6},{8,9},{9,8},{10,11... | collective-permute-start | bytes 811016 | tf_op jit(solution)/shard_map/ppermute | solution.py:317
  21.3 4.1 %collective-permute-start.2 = (bf16[12,16,128]{2,1,0:T(8,128)(2,1)S(1)}, bf16[12,16,128]{2,1,0:T(8,128)(2,1)S(1)}, u32[]{:S(2)}, u32[]{:S(2)}) collective-permute-start(bf16[12,16,128]{2,1,0:T(8,128)(2,1)S(1)} %pad.4.q0), channel_id=1, source_target_pairs={{0,16},{8,24},{16,0},{24,8},{1,17},{9,25},{17,1},{25,9},{2,18},{10... | collective-permute-start | bytes 147464 | tf_op jit(solution)/shard_map/ppermute | solution.py:323
  25.4 4.1 %collective-permute-start.1 = (bf16[12,16,128]{2,1,0:T(8,128)(2,1)S(1)}, bf16[12,16,128]{2,1,0:T(8,128)(2,1)S(1)}, u32[]{:S(2)}, u32[]{:S(2)}) collective-permute-start(bf16[12,16,128]{2,1,0:T(8,128)(2,1)S(1)} %pad.4.q0), channel_id=1, source_target_pairs={{0,8},{8,0},{16,24},{24,16},{1,9},{9,1},{17,25},{25,17},{2,10},{10... | collective-permute-start | bytes 147464 | tf_op jit(solution)/shard_map/ppermute | solution.py:323
  31.7 4.5 %collective-permute-start.5 = (bf16[128,256]{1,0:T(8,128)(2,1)S(1)}, bf16[128,256]{1,0:T(8,128)(2,1)S(1)}, u32[]{:S(2)}, u32[]{:S(2)}) collective-permute-start(bf16[128,256]{1,0:T(8,128)(2,1)S(1)} %get-tuple-element.29), channel_id=1, source_target_pairs={{0,2},{1,3},{2,0},{3,1},{4,6},{5,7},{6,4},{7,5},{8,10},{9,11},{10,... | collective-permute-start | bytes 196616 | tf_op jit(solution)/shard_map/ppermute | solution.py:320
  33.5 6.3 %copy-start.5 = (bf16[256]{0:T(256)(128)(2,1)S(1)}, bf16[256]{0:T(256)(128)(2,1)}, u32[]{:S(2)}) copy-start(bf16[256]{0:T(256)(128)(2,1)} %param.15) | copy-start | bytes 1540
  33.5 9.9 %collective-permute-start.6 = (bf16[128,256]{1,0:T(8,128)(2,1)}, bf16[128,256]{1,0:T(8,128)(2,1)}, u32[]{:S(2)}, u32[]{:S(2)}) collective-permute-start(bf16[128,256]{1,0:T(8,128)(2,1)} %get-tuple-element.30), channel_id=1, source_target_pairs={{0,4},{1,5},{2,6},{3,7},{4,0},{5,1},{6,2},{7,3},{8,12},{9,13},{10,... | collective-permute-start | bytes 196616 | tf_op jit(solution)/shard_map/ppermute | solution.py:320
  36.3 7.2 %collective-permute-start.7 = (bf16[128,256]{1,0:T(8,128)(2,1)}, bf16[128,256]{1,0:T(8,128)(2,1)}, u32[]{:S(2)}, u32[]{:S(2)}) collective-permute-start(bf16[128,256]{1,0:T(8,128)(2,1)} %get-tuple-element.31), channel_id=1, source_target_pairs={{0,6},{1,7},{2,4},{3,5},{4,2},{5,3},{6,0},{7,1},{8,14},{9,15},{10,... | collective-permute-start | bytes 196616 | tf_op jit(solution)/shard_map/ppermute | solution.py:320
  45.7 12.7 %collective-permute-start.14 = (bf16[256,256]{1,0:T(8,128)(2,1)S(1)}, bf16[256,256]{1,0:T(8,128)(2,1)S(1)}, u32[]{:S(2)}, u32[]{:S(2)}) collective-permute-start(bf16[256,256]{1,0:T(8,128)(2,1)S(1)} %get-tuple-element.33), channel_id=1, source_target_pairs={{0,1},{1,0},{2,3},{3,2},{4,5},{5,4},{6,7},{7,6},{8,9},{9,8},{10,11... | collective-permute-start | bytes 393224 | tf_op jit(solution)/shard_map/ppermute | solution.py:317
  45.7 12.7 %collective-permute-start.15 = (bf16[256,256]{1,0:T(8,128)(2,1)S(1)}, bf16[256,256]{1,0:T(8,128)(2,1)S(1)}, u32[]{:S(2)}, u32[]{:S(2)}) collective-permute-start(bf16[256,256]{1,0:T(8,128)(2,1)S(1)} %get-tuple-element.34), channel_id=1, source_target_pairs={{0,8},{1,2},{2,1},{3,4},{4,3},{5,6},{6,5},{7,15},{8,0},{9,10},{10,... | collective-permute-start | bytes 393224 | tf_op jit(solution)/shard_map/ppermute | solution.py:332
  47.9 6.0 %collective-permute-start.16 = (bf16[64,128]{1,0:T(8,128)(2,1)S(1)}, bf16[64,128]{1,0:T(8,128)(2,1)S(1)}, u32[]{:S(2)}, u32[]{:S(2)}) collective-permute-start(bf16[64,128]{1,0:T(8,128)(2,1)S(1)} %get-tuple-element.36), channel_id=1, source_target_pairs={{0,2},{1,3},{2,0},{3,1},{4,6},{5,7},{6,4},{7,5},{8,10},{9,11},{10,... | collective-permute-start | bytes 49160 | tf_op jit(solution)/shard_map/ppermute | solution.py:320
  48.6 5.3 %collective-permute-start.17 = (bf16[64,128]{1,0:T(8,128)(2,1)S(1)}, bf16[64,128]{1,0:T(8,128)(2,1)S(1)}, u32[]{:S(2)}, u32[]{:S(2)}) collective-permute-start(bf16[64,128]{1,0:T(8,128)(2,1)S(1)} %get-tuple-element.37), channel_id=1, source_target_pairs={{0,4},{1,5},{2,6},{3,7},{4,0},{5,1},{6,2},{7,3},{8,12},{9,13},{10,... | collective-permute-start | bytes 49160 | tf_op jit(solution)/shard_map/ppermute | solution.py:320
  49.8 5.6 %collective-permute-start.18 = (bf16[64,128]{1,0:T(8,128)(2,1)S(1)}, bf16[64,128]{1,0:T(8,128)(2,1)S(1)}, u32[]{:S(2)}, u32[]{:S(2)}) collective-permute-start(bf16[64,128]{1,0:T(8,128)(2,1)S(1)} %get-tuple-element.38), channel_id=1, source_target_pairs={{0,6},{1,7},{2,4},{3,5},{4,2},{5,3},{6,0},{7,1},{8,14},{9,15},{10,... | collective-permute-start | bytes 49160 | tf_op jit(solution)/shard_map/ppermute | solution.py:320
  60.4 1.6 %collective-permute-start.19 = (bf16[256,256]{1,0:T(8,128)(2,1)S(1)}, bf16[256,256]{1,0:T(8,128)(2,1)S(1)}, u32[]{:S(2)}, u32[]{:S(2)}) collective-permute-start(bf16[256,256]{1,0:T(8,128)(2,1)S(1)} %get-tuple-element.42), channel_id=1, source_target_pairs={{0,1},{1,0},{2,3},{3,2},{4,5},{5,4},{6,7},{7,6},{8,9},{9,8},{10,11... | collective-permute-start | bytes 393224 | tf_op jit(solution)/shard_map/ppermute | solution.py:317
  60.6 5.0 %collective-permute-start.20 = (bf16[256,256]{1,0:T(8,128)(2,1)S(1)}, bf16[256,256]{1,0:T(8,128)(2,1)S(1)}, u32[]{:S(2)}, u32[]{:S(2)}) collective-permute-start(bf16[256,256]{1,0:T(8,128)(2,1)S(1)} %get-tuple-element.43), channel_id=1, source_target_pairs={{0,8},{1,2},{2,1},{3,4},{4,3},{5,6},{6,5},{7,15},{8,0},{9,10},{10,... | collective-permute-start | bytes 393224 | tf_op jit(solution)/shard_map/ppermute | solution.py:332
  67.5 1.6 %collective-permute-start.21 = (bf16[256,256]{1,0:T(8,128)(2,1)S(1)}, bf16[256,256]{1,0:T(8,128)(2,1)S(1)}, u32[]{:S(2)}, u32[]{:S(2)}) collective-permute-start(bf16[256,256]{1,0:T(8,128)(2,1)S(1)} %get-tuple-element.47), channel_id=1, source_target_pairs={{0,1},{1,0},{2,3},{3,2},{4,5},{5,4},{6,7},{7,6},{8,9},{9,8},{10,11... | collective-permute-start | bytes 393224 | tf_op jit(solution)/shard_map/ppermute | solution.py:317
  67.7 5.0 %collective-permute-start.22 = (bf16[256,256]{1,0:T(8,128)(2,1)S(1)}, bf16[256,256]{1,0:T(8,128)(2,1)S(1)}, u32[]{:S(2)}, u32[]{:S(2)}) collective-permute-start(bf16[256,256]{1,0:T(8,128)(2,1)S(1)} %get-tuple-element.48), channel_id=1, source_target_pairs={{0,8},{1,2},{2,1},{3,4},{4,3},{5,6},{6,5},{7,15},{8,0},{9,10},{10,... | collective-permute-start | bytes 393224 | tf_op jit(solution)/shard_map/ppermute | solution.py:332
  75.0 1.2 %collective-permute-start.23 = (f32[1,512]{1,0:T(1,128)S(1)}, f32[1,512]{1,0:T(1,128)S(1)}, u32[]{:S(2)}, u32[]{:S(2)}) collective-permute-start(f32[1,512]{1,0:T(1,128)S(1)} %slice.4), channel_id=1, source_target_pairs={{0,1},{1,0},{2,3},{3,2},{4,5},{5,4},{6,7},{7,6},{8,9},{9,8},{10,11... | collective-permute-start | bytes 6152 | tf_op jit(solution)/shard_map/ppermute | solution.py:317
  76.3 5.5 %collective-permute-start.26 = (f32[2,512]{1,0:T(2,128)S(1)}, f32[2,512]{1,0:T(2,128)S(1)}, u32[]{:S(2)}, u32[]{:S(2)}) collective-permute-start(f32[2,512]{1,0:T(2,128)S(1)} %maximum_select_fusion.1.g0), channel_id=1, source_target_pairs={{0,6},{1,7},{2,4},{3,5},{4,2},{5,3},{6,0},{7,1},{8,14},{9,15},{10,... | collective-permute-start | bytes 12296 | tf_op jit(solution)/shard_map/ppermute | solution.py:320
  77.7 4.5 %collective-permute-start.25 = (f32[2,512]{1,0:T(2,128)S(1)}, f32[2,512]{1,0:T(2,128)S(1)}, u32[]{:S(2)}, u32[]{:S(2)}) collective-permute-start(f32[2,512]{1,0:T(2,128)S(1)} %maximum_select_fusion.1.g0), channel_id=1, source_target_pairs={{0,4},{1,5},{2,6},{3,7},{4,0},{5,1},{6,2},{7,3},{8,12},{9,13},{10,... | collective-permute-start | bytes 12296 | tf_op jit(solution)/shard_map/ppermute | solution.py:320
  77.7 4.6 %collective-permute-start.24 = (f32[2,512]{1,0:T(2,128)S(1)}, f32[2,512]{1,0:T(2,128)S(1)}, u32[]{:S(2)}, u32[]{:S(2)}) collective-permute-start(f32[2,512]{1,0:T(2,128)S(1)} %maximum_select_fusion.1.g0), channel_id=1, source_target_pairs={{0,2},{1,3},{2,0},{3,1},{4,6},{5,7},{6,4},{7,5},{8,10},{9,11},{10,... | collective-permute-start | bytes 12296 | tf_op jit(solution)/shard_map/ppermute | solution.py:320

commit v2 on v0

v2 whole, which is shorter than its diff:
```python
import functools

import jax
import jax.numpy as jnp
from jax import lax
from jax.experimental import pallas as pl
from jax.experimental.pallas import tpu as pltpu
from jax.sharding import PartitionSpec as P

F32 = jnp.float32
BF16 = jnp.bfloat16
VMEM = pl.BlockSpec(memory_space=pltpu.VMEM)
ANY = pl.BlockSpec(memory_space=pl.ANY)


def from_behind(array, axis, by):
    size = lax.axis_size(axis)
    pairs = [(i, i + by) for i in range(size) if 0 <= i + by < size]
    return lax.ppermute(array, axis, pairs)


def from_root(value, axis, source):
    kept = jnp.where(lax.axis_index(axis) == source, value, 0).astype(value.dtype)
    return lax.psum(kept, axis)


def row_stencil(surface, coefficients):
    taps_count = coefficients.shape[0]
    radius = taps_count // 2
    columns = surface.shape[1]
    padded = jnp.pad(surface.astype(F32), ((0, 0), (radius, radius), (0, 0)))
    summed = jnp.zeros(surface.shape, F32)
    for offset in range(taps_count):
        summed = (
            summed
            + coefficients[offset].astype(F32)[:, :, None] * padded[:, offset : offset + columns, :]
        )
    return summed


def col_stencil(surface, coefficients):
    taps_count = coefficients.shape[0]
    radius = taps_count // 2
    lines = surface.shape[0]
    swapped = jnp.swapaxes(coefficients, 1, 2)
    padded = jnp.pad(surface.astype(F32), ((radius, radius), (0, 0), (0, 0)))
    summed = jnp.zeros(surface.shape, F32)
    for offset in range(taps_count):
        summed = (
            summed
            + swapped[offset].astype(F32)[:, :, None] * padded[offset : offset + lines, :, :]
        )
    return summed


def apply_layer(current, params):
    row_part = row_stencil(current, params[0]).astype(BF16)
    columns_view = lax.all_to_all(row_part, "space", split_axis=1, concat_axis=0, tiled=True)
    mixed_field = col_stencil(columns_view, params[1])
    inverse = lax.rsqrt(jnp.mean(mixed_field * mixed_field, axis=-1, keepdims=True) + 1e-06)
    normed = (mixed_field * inverse * params[2].astype(F32)).astype(BF16)
    hidden = jax.nn.gelu(
        jnp.dot(normed, params[3], preferred_element_type=F32) + params[4].astype(F32),
        approximate=True,
    ).astype(BF16)
    return (mixed_field + jnp.dot(hidden, params[5], preferred_element_type=F32)).astype(BF16)


def to_rows(output):
    return lax.all_to_all(output, "space", split_axis=0, concat_axis=1, tiled=True)


def read_density(output, readout):
    return jax.nn.softplus(jnp.dot(output, readout, preferred_element_type=F32))


def layers_over_sections(
    raster, row_coef, col_coef, norm_gain, weight_in, bias_in, weight_out, readout
):
    sections = lax.axis_size("section")
    spaces = lax.axis_size("space")
    windows = raster.shape[0]
    position = lax.axis_index("section")
    params = (row_coef[0], col_coef[0], norm_gain[0], weight_in[0], bias_in[0], weight_out[0])
    carried = jnp.zeros(raster.shape[1:], BF16)
    finished = jnp.zeros((windows, raster.shape[1] * spaces, raster.shape[2] // spaces), F32)
    for moment in range(windows + sections - 1):
        entering = raster[min(moment, windows - 1)]
        current = jnp.where(position == 0, entering, carried)
        output = apply_layer(current, params)
        finished_index = moment - (sections - 1)
        if finished_index >= 0:
            finished = finished.at[finished_index].set(read_density(output, readout))
        if moment < windows + sections - 2:
            carried = from_behind(to_rows(output), "section", 1)
    row_density = lax.all_to_all(finished, "space", split_axis=1, concat_axis=2, tiled=True)
    everyone = from_root(row_density, "section", sections - 1)
    return lax.dynamic_slice_in_dim(everyone, position, 1, 0)


TAPS = 15
RADIUS = 7
ROWS = 32
COLS = 16
WIDE = 128
CELLS = ROWS * COLS
GROUP = 8 * COLS


def call(kernel, outs, specs, scratch=(), room=48, place=VMEM):
    return pl.pallas_call(
        kernel,
        out_shape=outs,
        in_specs=specs,
        out_specs=jax.tree.map(lambda _: place, outs),
        scratch_shapes=list(scratch),
        compiler_params=pltpu.CompilerParams(vmem_limit_bytes=room * 1024 * 1024),
        cost_estimate=pl.CostEstimate(flops=1, bytes_accessed=1, transcendentals=0),
    )


def after(array, *others):
    return lax.optimization_barrier((array, *others))[0]


def shaped(shape, kind=BF16):
    return jax.ShapeDtypeStruct(shape, kind)


def iota(shape, axis):
    return lax.broadcasted_iota(jnp.int32, shape, axis)


def picked(which, values):
    out = values[0]
    for k in range(1, len(values)):
        out = jnp.where(which == k, values[k], out)
    return out


def position():
    s, p = lax.axis_index("section"), lax.axis_index("space")
    return s, p % 2, p // 2, p


def pack_kernel(weight_in, weight_out, bias, gain, out, half, biases, gains, arrive, leave):
    _, c, _, _ = position()
    start = pl.multiple_of(c * 256, 256)
    copies = [
        pltpu.make_async_copy(bias, biases, arrive.at[0]),
        pltpu.make_async_copy(gain, gains, arrive.at[1]),
        pltpu.make_async_copy(weight_in.at[0, :, pl.ds(start, 256)], half.at[0:256, :], arrive.at[2]),
        pltpu.make_async_copy(weight_out.at[0, pl.ds(start, 256), :], half.at[256:512, :], arrive.at[3]),
    ]
    for copy in copies:
        copy.start()
    for copy in copies[:2]:
        copy.wait()
    line = iota((16, 256), 0)
    part = jnp.where(c == 0, biases[:, 0:256].astype(F32), biases[:, 256:512].astype(F32))
    tail = jnp.where(line == 0, part, jnp.where(line == 1, gains[...].astype(F32), 0.0))
    half[512:528, :] = tail.astype(BF16)
    for copy in copies[2:]:
        copy.wait()
    copies = [pltpu.make_async_copy(half, out.at[n], leave.at[n]) for n in range(4)]
    for copy in copies:
        copy.start()
    for copy in copies:
        copy.wait()


def chunk_kernel(own_taps, sib_taps, own, sib, o0, o1, o2, o3, chunk):
    _, c, z, _ = position()
    channels = own.shape[-1]
    for i in range(8):
        cells = jnp.where(c == i // 4, own[i % 4], sib[i % 4]).reshape(4, 2, COLS, channels)
        chunk[:, COLS * i : COLS * (i + 1), :] = jnp.where(c == 0, cells[:, 0], cells[:, 1])
    first, second = own_taps[0:4].astype(F32), sib_taps[0:4].astype(F32)
    taps = jnp.concatenate([jnp.where(c == 0, first, second), jnp.where(c == 0, second, first)], 0)
    turned = jnp.transpose(taps.reshape(WIDE, WIDE)).reshape(16, 8, WIDE)
    for to in range(4):
        at = [jnp.where(c == 0, turned[(4 * to + d) % 16], turned[(4 * to + d + 2) % 16]) for d in (-1, 0, 1, 2)]
        sides = [jnp.concatenate([at[1], at[2]], 0), jnp.concatenate([at[0], at[3]], 0)]
        chunk[to, GROUP : GROUP + 16, :] = jnp.concatenate(sides, 1).astype(BF16)
        edge = [jnp.where(c == 0, sib_taps[m + 6], sib_taps[m + 4]) for m in range(2)]
        chunk[to, GROUP + 16 : GROUP + 32, :] = jnp.concatenate(edge, 1)
    for k, out in enumerate((o0, o1, o2, o3)):
        out[...] = chunk[z ^ k]


def assemble_kernel(g0, g1, g2, g3, own_taps, sib_taps, field, taps, edges):
    _, c, z, _ = position()
    for k, g in enumerate((g0, g1, g2, g3)):
        field[pl.ds(pl.multiple_of((z ^ k) * GROUP, GROUP), GROUP), :] = g[0:GROUP, :]
        taps[16 * k : 16 * (k + 1), :] = g[GROUP : GROUP + 16, :]
        edges[z ^ k] = g[GROUP + 16 : GROUP + 32, :]
    edge = edges[(z + 3 + 2 * c) % 4]
    for m in range(4):
        core, chip = sib_taps[4 + (m + 2) % 4], edge[:, WIDE * (m % 2) : WIDE * (m % 2 + 1)]
        margin = jnp.where(c == 0, chip, core) if m < 2 else jnp.where(c == 0, core, chip)
        taps[64 + 16 * m : 80 + 16 * m, 0:WIDE] = own_taps[4 + m]
        taps[64 + 16 * m : 80 + 16 * m, WIDE : 2 * WIDE] = margin


def prepare_kernel(layers, last, q0, q1, q2, q3, *rest):
    s, c, z, p = position()
    outs, (turned, ordered, parts) = list(rest[:-3]), rest[-3:]

    tap_in, tap_out = iota((WIDE, 256), 0), iota((WIDE, 256), 1)
    expand = jnp.where((tap_in == tap_out // COLS) & (tap_in < TAPS), 1.0, 0.0).astype(BF16)
    lane, line = iota((COLS, 256), 1), iota((COLS, 256), 0)
    same = line == lane % COLS

    def columns(table, out):
        for m in range(4):
            turned[128 * m : 128 * (m + 1), :] = jnp.concatenate(
                [jnp.transpose(table[16 * m : 16 * (m + 1)]), jnp.zeros((128, WIDE - 16), F32)], 1
            )
        for i in range(ROWS):
            ordered[COLS * i : COLS * (i + 1), :] = turned[pl.ds(i, COLS, stride=ROWS), :]
        wide = jnp.dot(ordered[...].astype(BF16), expand, preferred_element_type=F32)
        for i in range(ROWS):
            row = i + lane // COLS - RADIUS
            block = jnp.where(same & (row >= 0) & (row < ROWS), wide[COLS * i : COLS * (i + 1)], 0.0)
            block = jnp.concatenate([block, jnp.zeros((COLS, CELLS - 256), F32)], 1)
            shift = (COLS * (i - RADIUS)) % CELLS
            if shift:
                block = pltpu.roll(block, shift, 1)
            out[COLS * i : COLS * (i + 1), :] = block.astype(BF16)

    lane2, line2 = iota((GROUP, WIDE), 1), iota((GROUP, WIDE), 0)
    tap = (lane2 - line2 + RADIUS + WIDE) % WIDE
    source = line2 % COLS + tap - RADIUS
    inside = (tap < TAPS) & (source >= 0) & (source < COLS)
    on_left = (tap < TAPS) & (source < 0) & (p > 0)
    on_right = (tap < TAPS) & (source >= COLS) & (p < last)
    h = line2 % COLS
    tap_u = (lane2 - line2 - 1 + WIDE) % WIDE
    tap_v = (lane2 - line2 + 15 + WIDE) % WIDE
    u_left = (h < 8) & (tap_u < TAPS) & (h + tap_u < 15)
    u_own = (h >= 8) & (tap_u < TAPS) & (h + tap_u < 15)
    v_own = (h < 8) & (tap_v < TAPS) & (h + tap_v >= 15)
    v_right = (h >= 8) & (tap_v < TAPS) & (h + tap_v >= 15)

    def rolled(part, shift):
        return jnp.concatenate([pltpu.roll(part, shift, 1, stride=1, stride_axis=0)] * 8, 0)

    def sides(left, right):
        return jnp.where(c == 0, right, left).astype(BF16), jnp.where(c == 0, left, right).astype(BF16)

    for layer in layers:
        table = picked(s ^ layer, [q[...].astype(F32) for q in (q0, q1, q2, q3)])
        columns(table[64:128, 0:WIDE], outs.pop(0))
        if layer % 2 == 0:
            columns(table[64:128, WIDE : 2 * WIDE], outs.pop(0))
        out = outs.pop(0)
        for k in range(4):
            parts[z ^ k] = table[16 * k : 16 * (k + 1)]
        for g in range(4):
            part = parts[g]
            band = rolled(part[:, 0:WIDE], WIDE - RADIUS)
            left, right = jnp.where(on_left, band, 0.0), jnp.where(on_right, band, 0.0)
            out[g, 0:GROUP, 0:WIDE] = jnp.where(inside, band, 0.0).astype(BF16)
            if layer % 2 == 1:
                margin = pltpu.roll(left, 8, 1) + pltpu.roll(right, WIDE - 8, 1)
                out[g, 0:GROUP, WIDE : 2 * WIDE] = margin.astype(BF16)
                continue
            core, chip = sides(pltpu.roll(left, 16, 1), pltpu.roll(right, WIDE - 16, 1))
            out[g, 0:GROUP, WIDE : 2 * WIDE] = core
            out[g, 0:GROUP, 2 * WIDE : 3 * WIDE] = chip
            band = rolled(part[:, WIDE : 2 * WIDE], 1)
            back = pltpu.roll(band, WIDE - 16, 1)
            mid = jnp.where(u_own, band, jnp.where(v_own, back, 0.0))
            core, chip = sides(jnp.where(u_left, band, 0.0), jnp.where(v_right, back, 0.0))
            out[g, GROUP : 2 * GROUP, 0:WIDE] = mid.astype(BF16)
            out[g, GROUP : 2 * GROUP, WIDE : 2 * WIDE] = core
            out[g, GROUP : 2 * GROUP, 2 * WIDE : 3 * WIDE] = chip


def layer_kernel(layer, fields, final, *refs):
    cells, refs = refs[:fields], refs[fields:]
    wide = fields == 3
    bands, refs = refs[0], refs[1:]
    col_bands, refs = refs[: 1 + wide], refs[1 + wide :]
    if final:
        readout, refs = refs[0], refs[1:]
    mine, theirs, refs = refs[0], refs[1], refs[2:]
    outs, (weights, sems) = refs[: 1 + wide], refs[1 + wide : 3 + wide]
    rows = refs[3 + wide :]
    copies = [
        pltpu.make_async_copy(half, weights.at[n], sems.at[n])
        for n, half in enumerate((mine.at[layer], theirs.at[max(layer - 1, 0)]))
    ]
    for copy in copies:
        copy.start()
    channels = cells[0].shape[-1]
    for g in range(4):
        cut = slice(GROUP * g, GROUP * (g + 1))
        stacked = jnp.concatenate([x[cut] for x in cells], 0)
        done = jnp.dot(bands[g], stacked, preferred_element_type=F32).astype(BF16)
        for n, row in enumerate(rows):
            row[cut, :] = done[GROUP * n : GROUP * (n + 1)]
    size = 256
    mixed = [
        jnp.dot(band[size * b : size * (b + 1), :], row[...], preferred_element_type=F32)
        for band, row in zip(col_bands, rows)
        for b in range(CELLS // size)
    ]
    for copy in copies:
        copy.wait()
    gain = weights[0, 512:528, :].astype(F32)[1:2]
    for n, total in enumerate(mixed):
        inverse = lax.rsqrt(jnp.mean(total * total, axis=-1, keepdims=True) + 1e-06)
        normed = (total * inverse * gain).astype(BF16)
        parts = []
        for half in range(2):
            bias = weights[half, 512:528, :].astype(F32)[0:1]
            hidden = jnp.dot(normed, weights[half, 0:256, :], preferred_element_type=F32) + bias
            hidden = jax.nn.gelu(hidden, approximate=True).astype(BF16)
            parts.append(jnp.dot(hidden, weights[half, 256:512, :], preferred_element_type=F32))
        total = (total + (parts[0] + parts[1])).astype(BF16)
        out, b = outs[n // 2], n % 2
        if final:
            reader = jnp.broadcast_to(readout[...], (8, channels))
            logit = lax.dot_general(reader, total, (((1,), (1,)), ((), ())), preferred_element_type=F32)
            logit = jnp.maximum(logit, 0.0) + jnp.log1p(jnp.exp(-jnp.abs(logit)))
            for d in range(4):
                moved = pltpu.roll(logit, size - 64 * d, 1) if d else logit
                out[4 * b + d : 4 * b + d + 1, :] = moved[0:1, 0:WIDE]
        else:
            out[size * b : size * (b + 1), :] = total


def gather_kernel(got, out):
    lane, line = iota((8, WIDE), 1), iota((8, WIDE), 0)
    mask = lane // COLS == line
    cells = pltpu.roll(got[...], 0, 1, stride=COLS, stride_axis=0)
    for t in range(4):
        moved = pltpu.roll(cells, WIDE - COLS * t, 1) if t else cells
        out[0, t : t + 1, :] = jnp.sum(jnp.where(mask, moved, 0.0), axis=0, keepdims=True)


def window_on_section(raster, row_coef, col_coef, norm_gain, weight_in, bias_in, weight_out, readout):
    c = lax.axis_index("space") % 2
    channels = raster.shape[-1]
    spaces = lax.axis_size("space")

    def core(array):
        return lax.ppermute(array, "space", [(i, i ^ 1) for i in range(spaces)])

    def chip(array, k):
        return lax.ppermute(array, "space", [(i, i ^ (2 * k)) for i in range(spaces)])

    def section(array, k):
        return lax.ppermute(array, "section", [(i, i ^ k) for i in range(4)])

    def beside(array):
        pairs = []
        for a in range(4):
            for q in range(spaces):
                other = q - 1 if q % 2 == 0 else q + 1
                to = a * spaces + other if 0 <= other < spaces else (a ^ 1) * spaces + q
                pairs.append((a * spaces + q, to))
        return lax.ppermute(array, ("section", "space"), pairs)

    window = lax.dynamic_index_in_dim(raster, lax.axis_index("section"), 0, keepdims=False)
    window_sib = core(window)
    packed = call(
        pack_kernel,
        shaped((4, 528, 256)),
        [ANY] * 4,
        [
            pltpu.VMEM((528, 256), BF16),
            pltpu.VMEM((1, 512), BF16),
            pltpu.VMEM((1, 256), BF16),
            pltpu.SemaphoreType.DMA((4,)),
            pltpu.SemaphoreType.DMA((4,)),
        ],
        room=60,
        place=ANY,
    )(weight_in, weight_out, bias_in, norm_gain)
    own = jnp.concatenate([row_coef[0], col_coef[0].reshape(TAPS, 4, WIDE)], 1)
    own = jnp.pad(jnp.swapaxes(own, 0, 1), ((0, 0), (0, 1), (0, 0)))
    sib = core(own)

    chunks = call(
        chunk_kernel,
        (shaped((GROUP + 32, channels)),) * 4,
        [VMEM] * 4,
        [pltpu.VMEM((4, GROUP + 32, channels), BF16)],
    )(own, sib, window, window_sib)
    sent = chunks
    chunks = [sent[0]] + [chip(sent[k], k) for k in (1, 2, 3)]

    packed = after(packed, window_sib, sib)
    mine = lax.all_to_all(packed, "section", split_axis=0, concat_axis=0, tiled=True)

    field, taps = call(
        assemble_kernel,
        (shaped((CELLS, channels)), shaped((WIDE, 256))),
        [VMEM] * 6,
        [pltpu.VMEM((4, 16, 256), BF16)],
    )(*chunks, own, sib)
    field_core, field_chip = core(field), beside(field)
    tables = [taps] + [section(taps, k) for k in (1, 2, 3)]
    theirs = [core(after(mine[:1], field_chip, *tables)), core(after(mine[1:], field_chip, *tables))]

    def prepare(layers, tables):
        outs = []
        for layer in layers:
            even = layer % 2 == 0
            outs += [shaped((CELLS, CELLS))] * (1 + even)
            outs.append(shaped((4, 2 * GROUP, 3 * WIDE) if even else (4, GROUP, 2 * WIDE)))
        return call(
            functools.partial(prepare_kernel, layers, spaces - 1),
            tuple(outs),
            [VMEM] * 4,
            [pltpu.VMEM((CELLS, WIDE), F32), pltpu.VMEM((CELLS, WIDE), F32), pltpu.VMEM((4, 16, 256), F32)],
        )(*tables)

    def run(layer, cells, bands, readers=()):
        wide = len(cells) == 3
        final = bool(readers)
        outs = (shaped((8, WIDE), F32),) if final else (shaped((CELLS, channels)),) * (1 + wide)
        return call(
            functools.partial(layer_kernel, layer, len(cells), final),
            outs,
            [VMEM] * (len(cells) + 2 + wide + final) + [ANY] * 2,
            [pltpu.VMEM((2, 528, 256), BF16), pltpu.SemaphoreType.DMA((2,))]
            + [pltpu.VMEM((CELLS, channels), BF16)] * (1 + wide),
        )(*cells, bands[-1], *bands[:-1], *readers, mine, theirs[layer > 0])

    bands0 = prepare((0,), [after(tables[0], field_chip)] + tables[1:])
    cells = run(0, (field, field_core, field_chip), bands0)
    bands1 = prepare((1,), [after(tables[0], cells[0])] + tables[1:])
    (state,) = run(1, cells, bands1)
    bands23 = prepare((2, 3), [after(t, state) for t in tables])
    cells = run(2, (state, core(state), beside(state)), bands23[:3])
    (density,) = run(3, cells, bands23[3:], (readout.reshape(1, channels),))

    density = lax.all_to_all(density, "space", split_axis=0, concat_axis=0, tiled=True)
    return call(gather_kernel, shaped((1, 4, WIDE), F32), [VMEM])(density)


def on_device(raster, row_coef, *rest):
    fits = (
        lax.axis_size("section") == 4
        and lax.axis_size("space") == 8
        and raster.shape == (4, 4, WIDE, 256)
        and row_coef.shape[1] == TAPS
    )
    plan = window_on_section if fits else layers_over_sections
    return plan(raster, row_coef, *rest)


def solution(mesh):
    placed = (
        P(None, "space", None, None),
        P("section", None, "space", None),
        P("section", None, "space", None),
        P("section", None),
        P("section", None, None),
        P("section", None),
        P("section", None, None),
        P(),
    )
    return jax.shard_map(
        on_device,
        mesh=mesh,
        in_specs=placed,
        out_specs=P("section", "space", None),
        check_vma=False,
    )
```

time: 302 us -> 59.9 us (0.20)
  blocking collectives: 136 us -> 8.63 us
  waiting for transfers between devices: 60.8 us -> 16 us
  other arithmetic: 42.3 us -> 0.01 us
  starting transfers between devices: 44.7 us -> 17.9 us
  Pallas kernels: 0 us -> 13.8 us
  matrix products: 8.33 us -> 0 us
  local copies, waits for them, and re-layouts: 8.77 us -> 3 us
    all_to_all x10 -> x1, blocking collectives: 124 us -> 8.63 us  [window_on_section(): lax.all_to_all(density, 'space', split_axis=0, concat_axis=0, tiled=True)]
    all_to_all x4 -> x1, waiting for transfers between devices: 30.2 us -> 0.01 us  [window_on_section(): lax.all_to_all(packed, 'section', split_axis=0, concat_axis=0, tiled=True)]
    convert_element_type x18 -> x0, other arithmetic: 27.2 us -> none  [the longest x7 25.7 us: apply_layer(): row_part = row_stencil(current, params[0]).astype(jnp.bfloat16)]
    ppermute x6 -> x14, starting transfers between devices: 28 us -> 12.7 us  [the longest x3 4.45 us: chip(): return lax.ppermute(array, 'space', [(i, i ^ 2 * k) for i in range(spaces)])]
    ppermute x6 -> x14, waiting for transfers between devices: 30.5 us -> 16 us  [the longest x3 6.38 us: chip(): return lax.ppermute(array, 'space', [(i, i ^ 2 * k) for i in range(spaces)])]
    reduce_sum x7 -> x0, other arithmetic: 14.3 us -> none  [apply_layer(): jnp.mean(mixed_field * mixed_field, axis=-1, keepdims=True) + 1e-06]
    pallas_call x0 -> x11, Pallas kernels: none -> 13.8 us  [the longest x4 7.55 us: run(): call(functools.partial(layer_kernel, layer, len(cells), final), outs, [VM...]
    psum x1 -> x0, blocking collectives: 11.7 us -> none  [from_root(): return lax.psum(kept, axis)]
  transfers between devices with their start and end apart: 10 -> 15, of which waited for: 10 -> 6; matrix products, arithmetic and copies ran while one was open for 1% -> 3% of each run, Pallas kernels for 0% -> 13%
where the time goes in v2:
time: 59.9 us; the launch traced here: 59.5 us
  starting transfers between devices  17.9 us (30%)
  waiting for transfers between devices  16 us (27%)
  Pallas kernels  13.8 us (23%)
  blocking collectives  8.63 us (14%)
  local copies, waits for them, and re-layouts  3 us (5%)
    all_to_all x1, blocking collectives, window_on_section(): lax.all_to_all(density, 'space', split_axis=0, concat_axis=0, tiled=True)  8.63 us
    pallas_call x4, Pallas kernels, run(): call(functools.partial(layer_kernel, layer, len(cells), final), outs, [VM...  7.55 us
    ppermute x3, waiting for transfers between devices, chip(): return lax.ppermute(array, 'space', [(i, i ^ 2 * k) for i in range(spaces)])  6.38 us
    all_to_all x1, starting transfers between devices, window_on_section(): lax.all_to_all(packed, 'section', split_axis=0, concat_axis=0, tiled=True)  5.18 us
    ppermute x3, waiting for transfers between devices, section(): return lax.ppermute(array, 'section', [(i, i ^ k) for i in range(4)])  5.06 us
    ppermute x3, starting transfers between devices, chip(): return lax.ppermute(array, 'space', [(i, i ^ 2 * k) for i in range(spaces)])  4.45 us
    ppermute x3, starting transfers between devices, section(): return lax.ppermute(array, 'section', [(i, i ^ k) for i in range(4)])  3.49 us
    ppermute x2, starting transfers between devices, beside(): return lax.ppermute(array, ('section', 'space'), pairs)  3.3 us
  transfers between devices with their start and end apart: 15, of which 6 were waited for; matrix products, arithmetic and copies ran while one was open for 3% of the time, Pallas kernels for 13%

profile of v2, /device:TPU:0, one launch (start us, length us, event | category | flops | bytes accessed | tf_op | source)
XLA Modules:
  0.0 59.5 jit_solution(8066984982416599523)
XLA Ops:
  0.0 0.0 copy-start
  0.0 1.2 %copy-done = bf16[4,4,128,256]{3,2,1,0:T(8,128)(2,1)S(1)} copy-done((bf16[4,4,128,256]{3,2,1,0:T(8,128)(2,1)S(1)}, bf16[4,4,128,256]{3,2,1,0:T(8,128)(2,1)}, u32[]{:S(2)}) %copy-start) | copy-done | bytes 1048600
  1.2 0.5 collective-permute-start.1
  1.8 0.9 %reshape_squeeze.3 = bf16[15,4,128]{2,1,0:T(4,128)(2,1)S(1)} reshape(bf16[1,15,16,32]{3,2,1,0:T(8,128)(2,1)} %param.10) | data formatting | bytes 30720 | tf_op jit(solution)/shard_map/reshape;squeeze | solution.py:382
  2.7 0.7 %copy.16 = bf16[1,15,4,128]{3,1,2,0:T(8,128)(2,1)S(1)} copy(bf16[1,15,4,128]{3,2,1,0:T(4,128)(2,1)} %param.9) | data formatting | bytes 30720 | tf_op args[1]
  3.5 0.1 collective-permute-start
  3.6 2.1 %shard_map.85 = bf16[4,528,256]{2,1,0:T(8,128)(2,1)} custom-call(bf16[1,256,512]{2,1,0:T(8,128)(2,1)} %weight_in.1, bf16[1,512,256]{2,1,0:T(8,128)(2,1)} %weight_out.1, bf16[1,512]{1,0:T(2,128)(2,1)} %bias.1, bf16[1,256]{1,0:T(2,128)(2,1)} %gain.1), custom_call_target="tpu_custom_call" | custom-call | flops 1 | bytes 1 | tf_op jit(solution)/shard_map/pallas_call | solution.py:368
  5.7 0.0 collective-permute-done.sib_taps
  5.7 0.0 collective-permute-done.1.sib
  5.7 5.2 %all-to-all-start = ((bf16[4,528,256]{2,1,0:T(8,128)(2,1)}), bf16[4,528,256]{2,1,0:T(8,128)(2,1)S(1)}, u32[]{:S(2)}, u32[]{:S(2)}) async-start(bf16[4,528,256]{2,1,0:T(8,128)(2,1)} %shard_map.85), calls=%async_computation | async-start | bytes 2162688 | tf_op jit(solution)/shard_map/all_to_all | solution.py:396
  10.9 0.1 shard_map.82
  11.0 1.6 %collective-permute-start.2 = (bf16[160,256]{1,0:T(8,128)(2,1)S(1)}, bf16[160,256]{1,0:T(8,128)(2,1)S(1)}, u32[]{:S(2)}, u32[]{:S(2)}) collective-permute-start(bf16[160,256]{1,0:T(8,128)(2,1)S(1)} %get-tuple-element.35), channel_id=1, source_target_pairs={{0,2},{1,3},{2,0},{3,1},{4,6},{5,7},{6,4},{7,5},{8,10},{9,11},{10,... | collective-permute-start | bytes 245768 | tf_op jit(solution)/shard_map/ppermute | solution.py:352
  12.7 2.6 %collective-permute-start.3 = (bf16[160,256]{1,0:T(8,128)(2,1)S(1)}, bf16[160,256]{1,0:T(8,128)(2,1)S(1)}, u32[]{:S(2)}, u32[]{:S(2)}) collective-permute-start(bf16[160,256]{1,0:T(8,128)(2,1)S(1)} %get-tuple-element.36), channel_id=1, source_target_pairs={{0,4},{1,5},{2,6},{3,7},{4,0},{5,1},{6,2},{7,3},{8,12},{9,13},{10,... | collective-permute-start | bytes 245768 | tf_op jit(solution)/shard_map/ppermute | solution.py:352
  15.3 0.2 collective-permute-start.4
  15.5 0.1 collective-permute-done.2.g1
  15.5 6.3 %collective-permute-done.3.g2 = bf16[160,256]{1,0:T(8,128)(2,1)S(1)} collective-permute-done((bf16[160,256]{1,0:T(8,128)(2,1)S(1)}, bf16[160,256]{1,0:T(8,128)(2,1)S(1)}, u32[]{:S(2)}, u32[]{:S(2)}) %collective-permute-start.3) | collective-permute-done | bytes 81952 | tf_op jit(solution)/shard_map/ppermute | solution.py:352
  21.9 0.0 collective-permute-done.4.g3
  21.9 1.8 %collective-permute-start.6 = (bf16[512,256]{1,0:T(8,128)(2,1)S(1)}, bf16[512,256]{1,0:T(8,128)(2,1)S(1)}, u32[]{:S(2)}, u32[]{:S(2)}) collective-permute-start(bf16[512,256]{1,0:T(8,128)(2,1)S(1)} %get-tuple-element.38.refs_0_), channel_id=1, source_target_pairs={{0,8},{1,2},{2,1},{3,4},{4,3},{5,6},{6,5},{7,15},{8,0},{9,10},{10,... | collective-permute-start | bytes 786440 | tf_op jit(solution)/shard_map/ppermute | solution.py:364
  23.7 0.3 collective-permute-start.7
  24.0 1.8 %collective-permute-start.8 = (bf16[128,256]{1,0:T(8,128)(2,1)S(1)}, bf16[128,256]{1,0:T(8,128)(2,1)S(1)}, u32[]{:S(2)}, u32[]{:S(2)}) collective-permute-start(bf16[128,256]{1,0:T(8,128)(2,1)S(1)} %get-tuple-element.52.q0), channel_id=1, source_target_pairs={{0,16},{8,24},{16,0},{24,8},{1,17},{9,25},{17,1},{25,9},{2,18},{10... | collective-permute-start | bytes 196616 | tf_op jit(solution)/shard_map/ppermute | solution.py:355
  25.8 1.5 %collective-permute-start.9 = (bf16[128,256]{1,0:T(8,128)(2,1)S(1)}, bf16[128,256]{1,0:T(8,128)(2,1)S(1)}, u32[]{:S(2)}, u32[]{:S(2)}) collective-permute-start(bf16[128,256]{1,0:T(8,128)(2,1)S(1)} %get-tuple-element.52.q0), channel_id=1, source_target_pairs={{0,24},{8,16},{16,8},{24,0},{1,25},{9,17},{17,9},{25,1},{2,26},{10... | collective-permute-start | bytes 196616 | tf_op jit(solution)/shard_map/ppermute | solution.py:355
  27.2 0.0 all-to-all-done.refs_6_.refs_4_.refs_5_
  27.2 0.1 slice.9
  27.3 3.2 %collective-permute-done.7.q1 = bf16[128,256]{1,0:T(8,128)(2,1)S(1)} collective-permute-done((bf16[128,256]{1,0:T(8,128)(2,1)S(1)}, bf16[128,256]{1,0:T(8,128)(2,1)S(1)}, u32[]{:S(2)}, u32[]{:S(2)}) %collective-permute-start.7) | collective-permute-done | bytes 65568 | tf_op jit(solution)/shard_map/ppermute | solution.py:355
  30.5 0.0 collective-permute-done.8.q2
  30.5 1.9 %collective-permute-done.9.q3 = bf16[128,256]{1,0:T(8,128)(2,1)S(1)} collective-permute-done((bf16[128,256]{1,0:T(8,128)(2,1)S(1)}, bf16[128,256]{1,0:T(8,128)(2,1)S(1)}, u32[]{:S(2)}, u32[]{:S(2)}) %collective-permute-start.9) | collective-permute-done | bytes 65568 | tf_op jit(solution)/shard_map/ppermute | solution.py:355
  32.4 0.0 collective-permute-done.6.refs_2_
  32.4 0.0 collective-permute-start.11
  32.4 0.6 collective-permute-start.10
  33.0 0.1 collective-permute-start.5
  33.0 1.0 %shard_map.84 = (bf16[512,512]{1,0:T(8,128)(2,1)S(1)}, bf16[512,512]{1,0:T(8,128)(2,1)S(1)}, bf16[4,256,384]{2,1,0:T(8,128)(2,1)S(1)}) custom-call(bf16[128,256]{1,0:T(8,128)(2,1)S(1)} %get-tuple-element.52.q0, bf16[128,256]{1,0:T(8,128)(2,1)S(1)} %collective-permute-done.7.q1, bf16[128,256]{1,0:T(8,128)(2,1)S(1)} %collective-permute-done.8.q2, ...), custom_call_target="tpu_custom_call" | custom-call | flops 1 | bytes 1 | tf_op jit(solution)/shard_map/pallas_call | solution.py:414
  34.0 1.4 %collective-permute-done.5.refs_1_ = bf16[512,256]{1,0:T(8,128)(2,1)S(1)} collective-permute-done((bf16[512,256]{1,0:T(8,128)(2,1)S(1)}, bf16[512,256]{1,0:T(8,128)(2,1)S(1)}, u32[]{:S(2)}, u32[]{:S(2)}) %collective-permute-start.5) | collective-permute-done | bytes 262176 | tf_op jit(solution)/shard_map/ppermute | solution.py:349
  35.4 0.0 collective-permute-done.10.refs_7_
  35.4 2.1 %shard_map.86 = (bf16[512,256]{1,0:T(8,128)(2,1)S(1)}, bf16[512,256]{1,0:T(8,128)(2,1)S(1)}) custom-call(bf16[512,256]{1,0:T(8,128)(2,1)S(1)} %get-tuple-element.38.refs_0_, bf16[512,256]{1,0:T(8,128)(2,1)S(1)} %collective-permute-done.5.refs_1_, bf16[512,256]{1,0:T(8,128)(2,1)S(1)} %collective-permute-done.6.refs_2_, ...), custom_call_target="tpu_custom_call" | custom-call | flops 1 | bytes 1 | tf_op jit(solution)/shard_map/pallas_call | solution.py:425
  37.6 0.6 shard_map.87
  38.2 0.0 collective-permute-done.11.refs_5_.refs_7_.refs_6_
  38.2 0.0 copy-start.1
  38.2 1.4 %shard_map.88.refs_0_ = bf16[512,256]{1,0:T(8,128)(2,1)S(1)} custom-call(bf16[512,256]{1,0:T(8,128)(2,1)S(1)} %get-tuple-element.46.refs_0_, bf16[512,256]{1,0:T(8,128)(2,1)S(1)} %get-tuple-element.47.refs_1_, bf16[4,128,256]{2,1,0:T(8,128)(2,1)S(1)} %get-tuple-element.49.refs_2_, bf16[512,512]{1,0:T(8,128)(2,1)S(1)} %get-tuple-element.50.refs_3_, ...), custom_call_target="tpu_custom_call" | custom-call | flops 1 | bytes 1 | tf_op jit(solution)/shard_map/pallas_call | solution.py:425
  39.6 0.2 collective-permute-start.12
  39.8 1.5 %collective-permute-start.13 = (bf16[512,256]{1,0:T(8,128)(2,1)S(1)}, bf16[512,256]{1,0:T(8,128)(2,1)S(1)}, u32[]{:S(2)}, u32[]{:S(2)}) collective-permute-start(bf16[512,256]{1,0:T(8,128)(2,1)S(1)} %shard_map.88.refs_0_), channel_id=1, source_target_pairs={{0,8},{1,2},{2,1},{3,4},{4,3},{5,6},{6,5},{7,15},{8,0},{9,10},{10,... | collective-permute-start | bytes 786440 | tf_op jit(solution)/shard_map/ppermute | solution.py:364
  41.2 0.0 copy-done.1
  41.2 1.7 %shard_map.89 = (bf16[512,512]{1,0:T(8,128)(2,1)S(1)}, bf16[512,512]{1,0:T(8,128)(2,1)S(1)}, bf16[4,256,384]{2,1,0:T(8,128)(2,1)S(1)}, bf16[512,512]{1,0:T(8,128)(2,1)S(1)}, bf16[4,128,256]{2,1,0:T(8,128)(2,1)S(1)}) custom-call(bf16[128,256]{1,0:T(8,128)(2,1)S(1)} %get-tuple-element.52.q0, bf16[128,256]{1,0:T(8,128)(2,1)S(1)} %collective-permute-done.7.q1, ...), custom_call_target="tpu_custom_call" | custom-call | flops 1 | bytes 1 | tf_op jit(solution)/shard_map/pallas_call | solution.py:414
  43.0 0.0 collective-permute-done.12.refs_1_
  43.0 3.2 %collective-permute-done.13.refs_2_ = bf16[512,256]{1,0:T(8,128)(2,1)S(1)} collective-permute-done((bf16[512,256]{1,0:T(8,128)(2,1)S(1)}, bf16[512,256]{1,0:T(8,128)(2,1)S(1)}, u32[]{:S(2)}, u32[]{:S(2)}) %collective-permute-start.13) | collective-permute-done | bytes 262176 | tf_op jit(solution)/shard_map/ppermute | solution.py:364
  46.1 2.1 %shard_map.90 = (bf16[512,256]{1,0:T(8,128)(2,1)S(1)}, bf16[512,256]{1,0:T(8,128)(2,1)S(1)}) custom-call(bf16[512,256]{1,0:T(8,128)(2,1)S(1)} %shard_map.88.refs_0_, bf16[512,256]{1,0:T(8,128)(2,1)S(1)} %collective-permute-done.12.refs_1_, bf16[512,256]{1,0:T(8,128)(2,1)S(1)} %collective-permute-done.13.refs_2_, ...), custom_call_target="tpu_custom_call" | custom-call | flops 1 | bytes 1 | tf_op jit(solution)/shard_map/pallas_call | solution.py:425
  48.3 1.9 %shard_map.91 = f32[8,128]{1,0:T(8,128)S(1)} custom-call(bf16[512,256]{1,0:T(8,128)(2,1)S(1)} %get-tuple-element.59.refs_0_, bf16[512,256]{1,0:T(8,128)(2,1)S(1)} %get-tuple-element.60.refs_1_, bf16[4,128,256]{2,1,0:T(8,128)(2,1)S(1)} %get-tuple-element.61.refs_2_, bf16[512,512]{1,0:T(8,128)(2,1)S(1)} %get-tuple-element.62.refs_3_, ...), custom_call_target="tpu_custom_call" | custom-call | flops 1 | bytes 1 | tf_op jit(solution)/shard_map/pallas_call | solution.py:425
  50.2 8.6 %all_to_all.16 = f32[8,1,128]{2,1,0:T(1,128)S(1)} all-to-all(f32[8,1,128]{2,1,0:T(1,128)S(1)} %bitcast.13), channel_id=1, replica_groups=mesh['section'=4,'space'=8] {'space'}, dimensions={0} | all-to-all | bytes 8192 | tf_op jit(solution)/shard_map/all_to_all | solution.py:441
  58.8 0.7 %shard_map.92 = f32[1,4,128]{2,1,0:T(4,128)} custom-call(f32[8,128]{1,0:T(8,128)S(1)} %bitcast.14), custom_call_target="tpu_custom_call" | custom-call | flops 1 | bytes 1 | tf_op jit(solution)/shard_map/pallas_call | solution.py:442
  (7 shorter events, 0.1 us)
Async XLA Ops:
  0.0 1.2 %copy-start = (bf16[4,4,128,256]{3,2,1,0:T(8,128)(2,1)S(1)}, bf16[4,4,128,256]{3,2,1,0:T(8,128)(2,1)}, u32[]{:S(2)}) copy-start(bf16[4,4,128,256]{3,2,1,0:T(8,128)(2,1)} %param.8) | copy-start | bytes 3145732
  1.2 4.5 %collective-permute-start.1 = (bf16[4,128,256]{2,1,0:T(8,128)(2,1)S(1)}, bf16[4,128,256]{2,1,0:T(8,128)(2,1)S(1)}, u32[]{:S(2)}, u32[]{:S(2)}) collective-permute-start(bf16[4,128,256]{2,1,0:T(8,128)(2,1)S(1)} %dynamic-slice_bitcast_fusion.own), channel_id=1, source_target_pairs={{0,1},{1,0},{2,3},{3,2},{4,5},{5,4},{6,7},{7,6},{8,9},{9,8},{10,11... | collective-permute-start | bytes 786440 | tf_op jit(solution)/shard_map/ppermute | solution.py:349
  3.5 2.2 %collective-permute-start = (bf16[8,16,128]{2,1,0:T(8,128)(2,1)S(1)}, bf16[8,16,128]{2,1,0:T(8,128)(2,1)S(1)}, u32[]{:S(2)}, u32[]{:S(2)}) collective-permute-start(bf16[8,16,128]{2,1,0:T(8,128)(2,1)S(1)} %pad.4.own_taps), channel_id=1, source_target_pairs={{0,1},{1,0},{2,3},{3,2},{4,5},{5,4},{6,7},{7,6},{8,9},{9,8},{10,11... | collective-permute-start | bytes 98312 | tf_op jit(solution)/shard_map/ppermute | solution.py:349
  5.7 21.5 %all-to-all-start = ((bf16[4,528,256]{2,1,0:T(8,128)(2,1)}), bf16[4,528,256]{2,1,0:T(8,128)(2,1)S(1)}, u32[]{:S(2)}, u32[]{:S(2)}) async-start(bf16[4,528,256]{2,1,0:T(8,128)(2,1)} %shard_map.85), calls=%async_computation | async-start | bytes 2162688 | tf_op jit(solution)/shard_map/all_to_all | solution.py:396
  11.0 4.5 %collective-permute-start.2 = (bf16[160,256]{1,0:T(8,128)(2,1)S(1)}, bf16[160,256]{1,0:T(8,128)(2,1)S(1)}, u32[]{:S(2)}, u32[]{:S(2)}) collective-permute-start(bf16[160,256]{1,0:T(8,128)(2,1)S(1)} %get-tuple-element.35), channel_id=1, source_target_pairs={{0,2},{1,3},{2,0},{3,1},{4,6},{5,7},{6,4},{7,5},{8,10},{9,11},{10,... | collective-permute-start | bytes 245768 | tf_op jit(solution)/shard_map/ppermute | solution.py:352
  12.7 9.2 %collective-permute-start.3 = (bf16[160,256]{1,0:T(8,128)(2,1)S(1)}, bf16[160,256]{1,0:T(8,128)(2,1)S(1)}, u32[]{:S(2)}, u32[]{:S(2)}) collective-permute-start(bf16[160,256]{1,0:T(8,128)(2,1)S(1)} %get-tuple-element.36), channel_id=1, source_target_pairs={{0,4},{1,5},{2,6},{3,7},{4,0},{5,1},{6,2},{7,3},{8,12},{9,13},{10,... | collective-permute-start | bytes 245768 | tf_op jit(solution)/shard_map/ppermute | solution.py:352
  15.3 6.6 %collective-permute-start.4 = (bf16[160,256]{1,0:T(8,128)(2,1)S(1)}, bf16[160,256]{1,0:T(8,128)(2,1)S(1)}, u32[]{:S(2)}, u32[]{:S(2)}) collective-permute-start(bf16[160,256]{1,0:T(8,128)(2,1)S(1)} %get-tuple-element.37), channel_id=1, source_target_pairs={{0,6},{1,7},{2,4},{3,5},{4,2},{5,3},{6,0},{7,1},{8,14},{9,15},{10,... | collective-permute-start | bytes 245768 | tf_op jit(solution)/shard_map/ppermute | solution.py:352
  21.9 10.4 %collective-permute-start.6 = (bf16[512,256]{1,0:T(8,128)(2,1)S(1)}, bf16[512,256]{1,0:T(8,128)(2,1)S(1)}, u32[]{:S(2)}, u32[]{:S(2)}) collective-permute-start(bf16[512,256]{1,0:T(8,128)(2,1)S(1)} %get-tuple-element.38.refs_0_), channel_id=1, source_target_pairs={{0,8},{1,2},{2,1},{3,4},{4,3},{5,6},{6,5},{7,15},{8,0},{9,10},{10,... | collective-permute-start | bytes 786440 | tf_op jit(solution)/shard_map/ppermute | solution.py:364
  23.7 6.7 %collective-permute-start.7 = (bf16[128,256]{1,0:T(8,128)(2,1)S(1)}, bf16[128,256]{1,0:T(8,128)(2,1)S(1)}, u32[]{:S(2)}, u32[]{:S(2)}) collective-permute-start(bf16[128,256]{1,0:T(8,128)(2,1)S(1)} %get-tuple-element.52.q0), channel_id=1, source_target_pairs={{0,8},{8,0},{16,24},{24,16},{1,9},{9,1},{17,25},{25,17},{2,10},{10... | collective-permute-start | bytes 196616 | tf_op jit(solution)/shard_map/ppermute | solution.py:355
  24.0 6.5 %collective-permute-start.8 = (bf16[128,256]{1,0:T(8,128)(2,1)S(1)}, bf16[128,256]{1,0:T(8,128)(2,1)S(1)}, u32[]{:S(2)}, u32[]{:S(2)}) collective-permute-start(bf16[128,256]{1,0:T(8,128)(2,1)S(1)} %get-tuple-element.52.q0), channel_id=1, source_target_pairs={{0,16},{8,24},{16,0},{24,8},{1,17},{9,25},{17,1},{25,9},{2,18},{10... | collective-permute-start | bytes 196616 | tf_op jit(solution)/shard_map/ppermute | solution.py:355
  25.8 6.6 %collective-permute-start.9 = (bf16[128,256]{1,0:T(8,128)(2,1)S(1)}, bf16[128,256]{1,0:T(8,128)(2,1)S(1)}, u32[]{:S(2)}, u32[]{:S(2)}) collective-permute-start(bf16[128,256]{1,0:T(8,128)(2,1)S(1)} %get-tuple-element.52.q0), channel_id=1, source_target_pairs={{0,24},{8,16},{16,8},{24,0},{1,25},{9,17},{17,9},{25,1},{2,26},{10... | collective-permute-start | bytes 196616 | tf_op jit(solution)/shard_map/ppermute | solution.py:355
  32.4 5.8 %collective-permute-start.11 = (bf16[3,528,256]{2,1,0:T(8,128)(2,1)S(1)}, bf16[3,528,256]{2,1,0:T(8,128)(2,1)S(1)}, u32[]{:S(2)}, u32[]{:S(2)}) collective-permute-start(bf16[3,528,256]{2,1,0:T(8,128)(2,1)S(1)} %slice.9), channel_id=1, source_target_pairs={{0,1},{1,0},{2,3},{3,2},{4,5},{5,4},{6,7},{7,6},{8,9},{9,8},{10,11... | collective-permute-start | bytes 2433032 | tf_op jit(solution)/shard_map/ppermute | solution.py:349
  32.4 3.1 %collective-permute-start.10 = (bf16[1,528,256]{2,1,0:T(8,128)(2,1)S(1)}, bf16[1,528,256]{2,1,0:T(8,128)(2,1)S(1)}, u32[]{:S(2)}, u32[]{:S(2)}) collective-permute-start(bf16[1,528,256]{2,1,0:T(8,128)(2,1)S(1)} %slice.8), channel_id=1, source_target_pairs={{0,1},{1,0},{2,3},{3,2},{4,5},{5,4},{6,7},{7,6},{8,9},{9,8},{10,11... | collective-permute-start | bytes 811016 | tf_op jit(solution)/shard_map/ppermute | solution.py:349
  33.0 2.5 %collective-permute-start.5 = (bf16[512,256]{1,0:T(8,128)(2,1)S(1)}, bf16[512,256]{1,0:T(8,128)(2,1)S(1)}, u32[]{:S(2)}, u32[]{:S(2)}) collective-permute-start(bf16[512,256]{1,0:T(8,128)(2,1)S(1)} %get-tuple-element.38.refs_0_), channel_id=1, source_target_pairs={{0,1},{1,0},{2,3},{3,2},{4,5},{5,4},{6,7},{7,6},{8,9},{9,8},{10,11... | collective-permute-start | bytes 786440 | tf_op jit(solution)/shard_map/ppermute | solution.py:349
  38.2 3.1 %copy-start.1 = (bf16[256]{0:T(256)(128)(2,1)S(1)}, bf16[256]{0:T(256)(128)(2,1)}, u32[]{:S(2)}) copy-start(bf16[256]{0:T(256)(128)(2,1)} %param.15) | copy-start | bytes 1540
  39.6 3.4 %collective-permute-start.12 = (bf16[512,256]{1,0:T(8,128)(2,1)S(1)}, bf16[512,256]{1,0:T(8,128)(2,1)S(1)}, u32[]{:S(2)}, u32[]{:S(2)}) collective-permute-start(bf16[512,256]{1,0:T(8,128)(2,1)S(1)} %shard_map.88.refs_0_), channel_id=1, source_target_pairs={{0,1},{1,0},{2,3},{3,2},{4,5},{5,4},{6,7},{7,6},{8,9},{9,8},{10,11... | collective-permute-start | bytes 786440 | tf_op jit(solution)/shard_map/ppermute | solution.py:349
  39.8 6.4 %collective-permute-start.13 = (bf16[512,256]{1,0:T(8,128)(2,1)S(1)}, bf16[512,256]{1,0:T(8,128)(2,1)S(1)}, u32[]{:S(2)}, u32[]{:S(2)}) collective-permute-start(bf16[512,256]{1,0:T(8,128)(2,1)S(1)} %shard_map.88.refs_0_), channel_id=1, source_target_pairs={{0,8},{1,2},{2,1},{3,4},{4,3},{5,6},{6,5},{7,15},{8,0},{9,10},{10,... | collective-permute-start | bytes 786440 | tf_op jit(solution)/shard_map/ppermute | solution.py:364

commit v3 on v2

--- a/solution.py
+++ b/solution.py
@@ -143,29 +143,42 @@
     return s, p % 2, p // 2, p
 
 
-def pack_kernel(weight_in, weight_out, bias, gain, out, half, biases, gains, arrive, leave):
+def stage_kernel(row_coef, col_coef, weight_in, weight_out, bias, gain, out, own, *scratch):
+    rows, cols, biases, gains, half, taps, arrive, leave = scratch
     _, c, _, _ = position()
     start = pl.multiple_of(c * 256, 256)
     copies = [
-        pltpu.make_async_copy(bias, biases, arrive.at[0]),
-        pltpu.make_async_copy(gain, gains, arrive.at[1]),
-        pltpu.make_async_copy(weight_in.at[0, :, pl.ds(start, 256)], half.at[0:256, :], arrive.at[2]),
-        pltpu.make_async_copy(weight_out.at[0, pl.ds(start, 256), :], half.at[256:512, :], arrive.at[3]),
+        pltpu.make_async_copy(row_coef.at[0], rows, arrive.at[0]),
+        pltpu.make_async_copy(col_coef.at[0], cols, arrive.at[1]),
+        pltpu.make_async_copy(bias, biases, arrive.at[2]),
+        pltpu.make_async_copy(gain, gains, arrive.at[3]),
+        pltpu.make_async_copy(weight_in.at[0, :, pl.ds(start, 256)], half.at[0:256, :], arrive.at[4]),
+        pltpu.make_async_copy(weight_out.at[0, pl.ds(start, 256), :], half.at[256:512, :], arrive.at[5]),
     ]
     for copy in copies:
         copy.start()
-    for copy in copies[:2]:
+    for copy in copies[2:4]:
         copy.wait()
     line = iota((16, 256), 0)
     part = jnp.where(c == 0, biases[:, 0:256].astype(F32), biases[:, 256:512].astype(F32))
     tail = jnp.where(line == 0, part, jnp.where(line == 1, gains[...].astype(F32), 0.0))
     half[512:528, :] = tail.astype(BF16)
-    for copy in copies[2:]:
+    for copy in copies[4:]:
         copy.wait()
-    copies = [pltpu.make_async_copy(half, out.at[n], leave.at[n]) for n in range(4)]
-    for copy in copies:
+    sends = [pltpu.make_async_copy(half, out.at[n], leave.at[n]) for n in range(4)]
+    for copy in sends:
         copy.start()
-    for copy in copies:
+    for copy in copies[:2]:
+        copy.wait()
+    zero = jnp.zeros((1, WIDE), F32)
+    row, col = rows[...].astype(F32), cols[...].astype(F32)
+    for m in range(4):
+        taps[m] = jnp.concatenate([row[:, m, :], zero], 0).astype(BF16)
+        group = jnp.concatenate([col[:, 4 * m + j, :] for j in range(4)], 1)
+        taps[4 + m] = jnp.concatenate([group, zero], 0).astype(BF16)
+    sends.append(pltpu.make_async_copy(taps, own, leave.at[4]))
+    sends[-1].start()
+    for copy in sends:
         copy.wait()
 
 
@@ -188,10 +201,9 @@
         out[...] = chunk[z ^ k]
 
 
-def assemble_kernel(g0, g1, g2, g3, own_taps, sib_taps, field, taps, edges):
+def tables_kernel(g0, g3, g2, g1, own_taps, sib_taps, taps, edges):
     _, c, z, _ = position()
     for k, g in enumerate((g0, g1, g2, g3)):
-        field[pl.ds(pl.multiple_of((z ^ k) * GROUP, GROUP), GROUP), :] = g[0:GROUP, :]
         taps[16 * k : 16 * (k + 1), :] = g[GROUP : GROUP + 16, :]
         edges[z ^ k] = g[GROUP + 16 : GROUP + 32, :]
     edge = edges[(z + 3 + 2 * c) % 4]
@@ -202,7 +214,13 @@
         taps[64 + 16 * m : 80 + 16 * m, WIDE : 2 * WIDE] = margin
 
 
-def prepare_kernel(layers, last, q0, q1, q2, q3, *rest):
+def field_kernel(g0, g3, g2, g1, field):
+    _, _, z, _ = position()
+    for k, g in enumerate((g0, g1, g2, g3)):
+        field[pl.ds(pl.multiple_of((z ^ k) * GROUP, GROUP), GROUP), :] = g[0:GROUP, :]
+
+
+def prepare_kernel(layers, last, q0, q3, q2, q1, *rest):
     s, c, z, p = position()
     outs, (turned, ordered, parts) = list(rest[:-3]), rest[-3:]
 
@@ -285,14 +303,8 @@
     if final:
         readout, refs = refs[0], refs[1:]
     mine, theirs, refs = refs[0], refs[1], refs[2:]
-    outs, (weights, sems) = refs[: 1 + wide], refs[1 + wide : 3 + wide]
-    rows = refs[3 + wide :]
-    copies = [
-        pltpu.make_async_copy(half, weights.at[n], sems.at[n])
-        for n, half in enumerate((mine.at[layer], theirs.at[max(layer - 1, 0)]))
-    ]
-    for copy in copies:
-        copy.start()
+    outs, rows = refs[: 1 + wide], refs[1 + wide :]
+    halves = (mine.at[layer], theirs.at[max(layer - 1, 0)])
     channels = cells[0].shape[-1]
     for g in range(4):
         cut = slice(GROUP * g, GROUP * (g + 1))
@@ -306,18 +318,16 @@
         for band, row in zip(col_bands, rows)
         for b in range(CELLS // size)
     ]
-    for copy in copies:
-        copy.wait()
-    gain = weights[0, 512:528, :].astype(F32)[1:2]
+    gain = halves[0][512:528, :].astype(F32)[1:2]
     for n, total in enumerate(mixed):
         inverse = lax.rsqrt(jnp.mean(total * total, axis=-1, keepdims=True) + 1e-06)
         normed = (total * inverse * gain).astype(BF16)
         parts = []
-        for half in range(2):
-            bias = weights[half, 512:528, :].astype(F32)[0:1]
-            hidden = jnp.dot(normed, weights[half, 0:256, :], preferred_element_type=F32) + bias
+        for half in halves:
+            bias = half[512:528, :].astype(F32)[0:1]
+            hidden = jnp.dot(normed, half[0:256, :], preferred_element_type=F32) + bias
             hidden = jax.nn.gelu(hidden, approximate=True).astype(BF16)
-            parts.append(jnp.dot(hidden, weights[half, 256:512, :], preferred_element_type=F32))
+            parts.append(jnp.dot(hidden, half[256:512, :], preferred_element_type=F32))
         total = (total + (parts[0] + parts[1])).astype(BF16)
         out, b = outs[n // 2], n % 2
         if final:
@@ -354,33 +364,35 @@
     def section(array, k):
         return lax.ppermute(array, "section", [(i, i ^ k) for i in range(4)])
 
-    def beside(array):
+    def beside(array, ends=True):
         pairs = []
         for a in range(4):
             for q in range(spaces):
                 other = q - 1 if q % 2 == 0 else q + 1
                 to = a * spaces + other if 0 <= other < spaces else (a ^ 1) * spaces + q
-                pairs.append((a * spaces + q, to))
+                if ends or 0 <= other < spaces:
+                    pairs.append((a * spaces + q, to))
         return lax.ppermute(array, ("section", "space"), pairs)
 
     window = lax.dynamic_index_in_dim(raster, lax.axis_index("section"), 0, keepdims=False)
     window_sib = core(window)
-    packed = call(
-        pack_kernel,
-        shaped((4, 528, 256)),
-        [ANY] * 4,
+    packed, own = call(
+        stage_kernel,
+        (shaped((4, 528, 256)), shaped((8, 16, WIDE))),
+        [ANY] * 6,
         [
-            pltpu.VMEM((528, 256), BF16),
+            pltpu.VMEM(row_coef.shape[1:], BF16),
+            pltpu.VMEM(col_coef.shape[1:], BF16),
             pltpu.VMEM((1, 512), BF16),
             pltpu.VMEM((1, 256), BF16),
-            pltpu.SemaphoreType.DMA((4,)),
-            pltpu.SemaphoreType.DMA((4,)),
+            pltpu.VMEM((528, 256), BF16),
+            pltpu.VMEM((8, 16, WIDE), BF16),
+            pltpu.SemaphoreType.DMA((6,)),
+            pltpu.SemaphoreType.DMA((5,)),
         ],
         room=60,
         place=ANY,
-    )(weight_in, weight_out, bias_in, norm_gain)
-    own = jnp.concatenate([row_coef[0], col_coef[0].reshape(TAPS, 4, WIDE)], 1)
-    own = jnp.pad(jnp.swapaxes(own, 0, 1), ((0, 0), (0, 1), (0, 0)))
+    )(row_coef, col_coef, weight_in, weight_out, bias_in, norm_gain)
     sib = core(own)
 
     chunks = call(
@@ -390,20 +402,18 @@
         [pltpu.VMEM((4, GROUP + 32, channels), BF16)],
     )(own, sib, window, window_sib)
     sent = chunks
-    chunks = [sent[0]] + [chip(sent[k], k) for k in (1, 2, 3)]
-
-    packed = after(packed, window_sib, sib)
+    chunks = [sent[0]] + [chip(sent[k], k) for k in (3, 2, 1)][::-1]
+
     mine = lax.all_to_all(packed, "section", split_axis=0, concat_axis=0, tiled=True)
 
-    field, taps = call(
-        assemble_kernel,
-        (shaped((CELLS, channels)), shaped((WIDE, 256))),
-        [VMEM] * 6,
-        [pltpu.VMEM((4, 16, 256), BF16)],
-    )(*chunks, own, sib)
+    taps = call(
+        tables_kernel, shaped((WIDE, 256)), [VMEM] * 6, [pltpu.VMEM((4, 16, 256), BF16)]
+    )(chunks[0], *chunks[:0:-1], own, sib)
+    field = call(field_kernel, shaped((CELLS, channels)), [VMEM] * 4)(after(chunks[0], taps), *chunks[:0:-1])
     field_core, field_chip = core(field), beside(field)
-    tables = [taps] + [section(taps, k) for k in (1, 2, 3)]
-    theirs = [core(after(mine[:1], field_chip, *tables)), core(after(mine[1:], field_chip, *tables))]
+    tables = [section(taps, k) for k in (3, 2, 1)]
+    tables = [taps] + tables[::-1]
+    theirs = [core(after(m, *tables[::-1], field_core, field_chip)) for m in (mine[:1], mine[1:])]
 
     def prepare(layers, tables):
         outs = []
@@ -416,7 +426,7 @@
             tuple(outs),
             [VMEM] * 4,
             [pltpu.VMEM((CELLS, WIDE), F32), pltpu.VMEM((CELLS, WIDE), F32), pltpu.VMEM((4, 16, 256), F32)],
-        )(*tables)
+        )(tables[0], *tables[:0:-1])
 
     def run(layer, cells, bands, readers=()):
         wide = len(cells) == 3
@@ -425,14 +435,13 @@
         return call(
             functools.partial(layer_kernel, layer, len(cells), final),
             outs,
-            [VMEM] * (len(cells) + 2 + wide + final) + [ANY] * 2,
-            [pltpu.VMEM((2, 528, 256), BF16), pltpu.SemaphoreType.DMA((2,))]
-            + [pltpu.VMEM((CELLS, channels), BF16)] * (1 + wide),
+            [VMEM] * (len(cells) + 4 + wide + final),
+            [pltpu.VMEM((CELLS, channels), BF16)] * (1 + wide),
         )(*cells, bands[-1], *bands[:-1], *readers, mine, theirs[layer > 0])
 
     bands0 = prepare((0,), [after(tables[0], field_chip)] + tables[1:])
     cells = run(0, (field, field_core, field_chip), bands0)
-    bands1 = prepare((1,), [after(tables[0], cells[0])] + tables[1:])
+    bands1 = prepare((1,), [after(tables[0], field_chip)] + tables[1:])
     (state,) = run(1, cells, bands1)
     bands23 = prepare((2, 3), [after(t, state) for t in tables])
     cells = run(2, (state, core(state), beside(state)), bands23[:3])

time: 59.9 us -> 54.9 us (0.917)
  local copies, waits for them, and re-layouts: 3 us -> 0.11 us
  waiting for transfers between devices: 16 us -> 15 us
  Pallas kernels: 13.8 us -> 13 us
  blocking collectives: 8.63 us -> 7.93 us
    unnamed x5 -> x6, local copies, waits for them, and re-layouts: 1.95 us -> 0.01 us
    ppermute x3, waiting for transfers between devices: 5.06 us -> 4.11 us  [section(): return lax.ppermute(array, 'section', [(i, i ^ k) for i in range(4)])]
    pallas_call x4, Pallas kernels: 7.55 us -> 6.6 us  [run(): call(functools.partial(layer_kernel, layer, len(cells), final), outs, [VM...]
    another operation x2 -> x0, local copies, waits for them, and re-layouts: 0.94 us -> none  [window_on_section(): own = jnp.concatenate([row_coef[0], col_coef[0].reshape(TAPS, 4, WIDE)], 1)]
    all_to_all x1, blocking collectives: 8.63 us -> 7.93 us  [window_on_section(): lax.all_to_all(density, 'space', split_axis=0, concat_axis=0, tiled=True)]
    pallas_call x2 -> x3, Pallas kernels: 2.14 us -> 2.31 us  [the longest x1 2.25 us: window_on_section(): call(stage_kernel, (shaped((4, 528, 256)), shaped((8, 16, WIDE))), [ANY]...]
  transfers between devices with their start and end apart: 15 -> 15, of which waited for: 6 -> 6; matrix products, arithmetic and copies ran while one was open for 3% -> 0% of each run, Pallas kernels for 13% -> 10%
where the time goes in v3:
time: 54.9 us; the launch traced here: 54.7 us
  starting transfers between devices  18.4 us (34%)
  waiting for transfers between devices  15 us (27%)
  Pallas kernels  13 us (24%)
  blocking collectives  7.93 us (14%)
    all_to_all x1, blocking collectives, window_on_section(): lax.all_to_all(density, 'space', split_axis=0, concat_axis=0, tiled=True)  7.93 us
    pallas_call x4, Pallas kernels, run(): call(functools.partial(layer_kernel, layer, len(cells), final), outs, [VM...  6.6 us
    ppermute x3, waiting for transfers between devices, chip(): return lax.ppermute(array, 'space', [(i, i ^ 2 * k) for i in range(spaces)])  6.38 us
    all_to_all x1, starting transfers between devices, window_on_section(): lax.all_to_all(packed, 'section', split_axis=0, concat_axis=0, tiled=True)  5.18 us
    ppermute x3, starting transfers between devices, chip(): return lax.ppermute(array, 'space', [(i, i ^ 2 * k) for i in range(spaces)])  4.45 us
    ppermute x3, waiting for transfers between devices, section(): return lax.ppermute(array, 'section', [(i, i ^ k) for i in range(4)])  4.11 us
    ppermute x2, starting transfers between devices, beside(): return lax.ppermute(array, ('section', 'space'), pairs)  3.81 us
    ppermute x3, starting transfers between devices, section(): return lax.ppermute(array, 'section', [(i, i ^ k) for i in range(4)])  3.49 us
  transfers between devices with their start and end apart: 15, of which 6 were waited for; matrix products, arithmetic and copies ran while one was open for 0% of the time, Pallas kernels for 10%

profile of v3, /device:TPU:0, one launch (start us, length us, event | category | flops | bytes accessed | tf_op | source)
XLA Modules:
  0.0 54.7 jit_solution(3058164947208281867)
XLA Ops:
  0.0 0.0 copy-start
  0.0 2.3 %shard_map.82 = (bf16[4,528,256]{2,1,0:T(8,128)(2,1)}, bf16[8,16,128]{2,1,0:T(8,128)(2,1)}) custom-call(bf16[1,15,4,128]{3,2,1,0:T(4,128)(2,1)} %row_coef.1, bf16[1,15,16,32]{3,2,1,0:T(8,128)(2,1)} %col_coef.1, bf16[1,256,512]{2,1,0:T(8,128)(2,1)} %weight_in.1, bf16[1,512,256]{2,1,0:T(8,128)(2,1)} %weight_out.1, bf16[1,512]{1,0:T(2,128)(2,1)} %bias.1, ...), custom_call_target="tpu_custom_call" | custom-call | flops 1 | bytes 1 | tf_op jit(solution)/shard_map/pallas_call | solution.py:379
  2.3 0.0 copy-start.1
  2.3 5.2 %all-to-all-start = ((bf16[4,528,256]{2,1,0:T(8,128)(2,1)}), bf16[4,528,256]{2,1,0:T(8,128)(2,1)S(1)}, u32[]{:S(2)}, u32[]{:S(2)}) async-start(bf16[4,528,256]{2,1,0:T(8,128)(2,1)} %get-tuple-element.43), calls=%async_computation | async-start | bytes 2162688 | tf_op jit(solution)/shard_map/all_to_all | solution.py:407
  7.4 0.0 copy-done
  7.5 0.1 collective-permute-start.1
  7.6 0.0 copy-done.1
  7.6 0.5 collective-permute-start
  8.1 1.1 %collective-permute-done.sib_taps = bf16[8,16,128]{2,1,0:T(8,128)(2,1)S(1)} collective-permute-done((bf16[8,16,128]{2,1,0:T(8,128)(2,1)S(1)}, bf16[8,16,128]{2,1,0:T(8,128)(2,1)S(1)}, u32[]{:S(2)}, u32[]{:S(2)}) %collective-permute-start) | collective-permute-done | bytes 32800 | tf_op jit(solution)/shard_map/ppermute | solution.py:359
  9.1 0.0 collective-permute-done.1.sib
  9.1 0.1 shard_map.83
  9.3 3.7 %collective-permute-start.2 = (bf16[160,256]{1,0:T(8,128)(2,1)S(1)}, bf16[160,256]{1,0:T(8,128)(2,1)S(1)}, u32[]{:S(2)}, u32[]{:S(2)}) collective-permute-start(bf16[160,256]{1,0:T(8,128)(2,1)S(1)} %get-tuple-element.35), channel_id=1, source_target_pairs={{0,6},{1,7},{2,4},{3,5},{4,2},{5,3},{6,0},{7,1},{8,14},{9,15},{10,... | collective-permute-start | bytes 245768 | tf_op jit(solution)/shard_map/ppermute | solution.py:362
  12.9 0.0 collective-permute-start.3
  12.9 0.8 %collective-permute-start.4 = (bf16[160,256]{1,0:T(8,128)(2,1)S(1)}, bf16[160,256]{1,0:T(8,128)(2,1)S(1)}, u32[]{:S(2)}, u32[]{:S(2)}) collective-permute-start(bf16[160,256]{1,0:T(8,128)(2,1)S(1)} %get-tuple-element.37), channel_id=1, source_target_pairs={{0,2},{1,3},{2,0},{3,1},{4,6},{5,7},{6,4},{7,5},{8,10},{9,11},{10,... | collective-permute-start | bytes 245768 | tf_op jit(solution)/shard_map/ppermute | solution.py:362
  13.7 2.6 %collective-permute-done.2.g3 = bf16[160,256]{1,0:T(8,128)(2,1)S(1)} collective-permute-done((bf16[160,256]{1,0:T(8,128)(2,1)S(1)}, bf16[160,256]{1,0:T(8,128)(2,1)S(1)}, u32[]{:S(2)}, u32[]{:S(2)}) %collective-permute-start.2) | collective-permute-done | bytes 81952 | tf_op jit(solution)/shard_map/ppermute | solution.py:362
  16.3 3.8 %collective-permute-done.3.g2 = bf16[160,256]{1,0:T(8,128)(2,1)S(1)} collective-permute-done((bf16[160,256]{1,0:T(8,128)(2,1)S(1)}, bf16[160,256]{1,0:T(8,128)(2,1)S(1)}, u32[]{:S(2)}, u32[]{:S(2)}) %collective-permute-start.3) | collective-permute-done | bytes 81952 | tf_op jit(solution)/shard_map/ppermute | solution.py:362
  20.1 0.0 collective-permute-done.4.g1
  20.2 0.1 collective-permute-start.5
  20.2 2.1 %collective-permute-start.6 = (bf16[512,256]{1,0:T(8,128)(2,1)S(1)}, bf16[512,256]{1,0:T(8,128)(2,1)S(1)}, u32[]{:S(2)}, u32[]{:S(2)}) collective-permute-start(bf16[512,256]{1,0:T(8,128)(2,1)S(1)} %shard_map.85.refs_0_), channel_id=1, source_target_pairs={{0,8},{1,2},{2,1},{3,4},{4,3},{5,6},{6,5},{7,15},{8,0},{9,10},{10,... | collective-permute-start | bytes 786440 | tf_op jit(solution)/shard_map/ppermute | solution.py:375
  22.3 1.5 %collective-permute-start.7 = (bf16[128,256]{1,0:T(8,128)(2,1)S(1)}, bf16[128,256]{1,0:T(8,128)(2,1)S(1)}, u32[]{:S(2)}, u32[]{:S(2)}) collective-permute-start(bf16[128,256]{1,0:T(8,128)(2,1)S(1)} %shard_map.84.q0), channel_id=1, source_target_pairs={{0,24},{8,16},{16,8},{24,0},{1,25},{9,17},{17,9},{25,1},{2,26},{10... | collective-permute-start | bytes 196616 | tf_op jit(solution)/shard_map/ppermute | solution.py:365
  23.8 0.1 collective-permute-start.8
  23.9 1.9 %collective-permute-start.9 = (bf16[128,256]{1,0:T(8,128)(2,1)S(1)}, bf16[128,256]{1,0:T(8,128)(2,1)S(1)}, u32[]{:S(2)}, u32[]{:S(2)}) collective-permute-start(bf16[128,256]{1,0:T(8,128)(2,1)S(1)} %shard_map.84.q0), channel_id=1, source_target_pairs={{0,8},{8,0},{16,24},{24,16},{1,9},{9,1},{17,25},{25,17},{2,10},{10... | collective-permute-start | bytes 196616 | tf_op jit(solution)/shard_map/ppermute | solution.py:365
  25.8 0.0 all-to-all-done.refs_6_.refs_4_.refs_5_
  25.8 0.1 slice.9
  25.9 4.1 %collective-permute-done.7.q3 = bf16[128,256]{1,0:T(8,128)(2,1)S(1)} collective-permute-done((bf16[128,256]{1,0:T(8,128)(2,1)S(1)}, bf16[128,256]{1,0:T(8,128)(2,1)S(1)}, u32[]{:S(2)}, u32[]{:S(2)}) %collective-permute-start.7) | collective-permute-done | bytes 65568 | tf_op jit(solution)/shard_map/ppermute | solution.py:365
  30.0 0.0 collective-permute-done.8.q2
  30.0 0.0 collective-permute-done.9.q1
  30.0 0.0 collective-permute-done.5.refs_1_
  30.0 0.0 collective-permute-done.6.refs_2_
  30.0 0.1 collective-permute-start.11
  30.1 0.6 %collective-permute-start.10 = (bf16[1,528,256]{2,1,0:T(8,128)(2,1)S(1)}, bf16[1,528,256]{2,1,0:T(8,128)(2,1)S(1)}, u32[]{:S(2)}, u32[]{:S(2)}) collective-permute-start(bf16[1,528,256]{2,1,0:T(8,128)(2,1)S(1)} %slice.8), channel_id=1, source_target_pairs={{0,1},{1,0},{2,3},{3,2},{4,5},{5,4},{6,7},{7,6},{8,9},{9,8},{10,11... | collective-permute-start | bytes 811016 | tf_op jit(solution)/shard_map/ppermute | solution.py:359
  30.7 1.0 %shard_map.86 = (bf16[512,512]{1,0:T(8,128)(2,1)S(1)}, bf16[512,512]{1,0:T(8,128)(2,1)S(1)}, bf16[4,256,384]{2,1,0:T(8,128)(2,1)S(1)}) custom-call(bf16[128,256]{1,0:T(8,128)(2,1)S(1)} %shard_map.84.q0, bf16[128,256]{1,0:T(8,128)(2,1)S(1)} %collective-permute-done.7.q3, bf16[128,256]{1,0:T(8,128)(2,1)S(1)} %collective-permute-done.8.q2, ...), custom_call_target="tpu_custom_call" | custom-call | flops 1 | bytes 1 | tf_op jit(solution)/shard_map/pallas_call | solution.py:424
  31.7 0.6 %shard_map.88 = (bf16[512,512]{1,0:T(8,128)(2,1)S(1)}, bf16[4,128,256]{2,1,0:T(8,128)(2,1)S(1)}) custom-call(bf16[128,256]{1,0:T(8,128)(2,1)S(1)} %shard_map.84.q0, bf16[128,256]{1,0:T(8,128)(2,1)S(1)} %collective-permute-done.7.q3, bf16[128,256]{1,0:T(8,128)(2,1)S(1)} %collective-permute-done.8.q2, bf16[128,256]{1,0:T(8,128)(2,1)S(1)} %collective-permute-done.9.q1), custom_call_target="tpu_custom_call" | custom-call | flops 1 | bytes 1 | tf_op jit(solution)/shard_map/pallas_call | solution.py:424
  32.2 0.5 collective-permute-done.10.refs_7_
  32.8 1.9 %shard_map.87 = (bf16[512,256]{1,0:T(8,128)(2,1)S(1)}, bf16[512,256]{1,0:T(8,128)(2,1)S(1)}) custom-call(bf16[512,256]{1,0:T(8,128)(2,1)S(1)} %shard_map.85.refs_0_, bf16[512,256]{1,0:T(8,128)(2,1)S(1)} %collective-permute-done.5.refs_1_, bf16[512,256]{1,0:T(8,128)(2,1)S(1)} %collective-permute-done.6.refs_2_, ...), custom_call_target="tpu_custom_call" | custom-call | flops 1 | bytes 1 | tf_op jit(solution)/shard_map/pallas_call | solution.py:435
  34.7 0.0 collective-permute-done.11.refs_5_.refs_7_.refs_6_
  34.7 0.0 copy-start.2
  34.7 1.2 %shard_map.89.refs_0_ = bf16[512,256]{1,0:T(8,128)(2,1)S(1)} custom-call(bf16[512,256]{1,0:T(8,128)(2,1)S(1)} %get-tuple-element.45.refs_0_, bf16[512,256]{1,0:T(8,128)(2,1)S(1)} %get-tuple-element.46.refs_1_, bf16[4,128,256]{2,1,0:T(8,128)(2,1)S(1)} %get-tuple-element.47.refs_2_, bf16[512,512]{1,0:T(8,128)(2,1)S(1)} %get-tuple-element.48.refs_3_, ...), custom_call_target="tpu_custom_call" | custom-call | flops 1 | bytes 1 | tf_op jit(solution)/shard_map/pallas_call | solution.py:435
  35.9 0.2 collective-permute-start.12
  36.1 1.7 %collective-permute-start.13 = (bf16[512,256]{1,0:T(8,128)(2,1)S(1)}, bf16[512,256]{1,0:T(8,128)(2,1)S(1)}, u32[]{:S(2)}, u32[]{:S(2)}) collective-permute-start(bf16[512,256]{1,0:T(8,128)(2,1)S(1)} %shard_map.89.refs_0_), channel_id=1, source_target_pairs={{0,8},{1,2},{2,1},{3,4},{4,3},{5,6},{6,5},{7,15},{8,0},{9,10},{10,... | collective-permute-start | bytes 786440 | tf_op jit(solution)/shard_map/ppermute | solution.py:375
  37.8 0.0 copy-done.2
  37.8 1.7 %shard_map.90 = (bf16[512,512]{1,0:T(8,128)(2,1)S(1)}, bf16[512,512]{1,0:T(8,128)(2,1)S(1)}, bf16[4,256,384]{2,1,0:T(8,128)(2,1)S(1)}, bf16[512,512]{1,0:T(8,128)(2,1)S(1)}, bf16[4,128,256]{2,1,0:T(8,128)(2,1)S(1)}) custom-call(bf16[128,256]{1,0:T(8,128)(2,1)S(1)} %shard_map.84.q0, bf16[128,256]{1,0:T(8,128)(2,1)S(1)} %collective-permute-done.7.q3, ...), custom_call_target="tpu_custom_call" | custom-call | flops 1 | bytes 1 | tf_op jit(solution)/shard_map/pallas_call | solution.py:424
  39.5 0.0 collective-permute-done.12.refs_1_
  39.5 2.9 %collective-permute-done.13.refs_2_ = bf16[512,256]{1,0:T(8,128)(2,1)S(1)} collective-permute-done((bf16[512,256]{1,0:T(8,128)(2,1)S(1)}, bf16[512,256]{1,0:T(8,128)(2,1)S(1)}, u32[]{:S(2)}, u32[]{:S(2)}) %collective-permute-start.13) | collective-permute-done | bytes 262176 | tf_op jit(solution)/shard_map/ppermute | solution.py:375
  42.4 1.8 %shard_map.91 = (bf16[512,256]{1,0:T(8,128)(2,1)S(1)}, bf16[512,256]{1,0:T(8,128)(2,1)S(1)}) custom-call(bf16[512,256]{1,0:T(8,128)(2,1)S(1)} %shard_map.89.refs_0_, bf16[512,256]{1,0:T(8,128)(2,1)S(1)} %collective-permute-done.12.refs_1_, bf16[512,256]{1,0:T(8,128)(2,1)S(1)} %collective-permute-done.13.refs_2_, ...), custom_call_target="tpu_custom_call" | custom-call | flops 1 | bytes 1 | tf_op jit(solution)/shard_map/pallas_call | solution.py:435
  44.3 1.7 %shard_map.92 = f32[8,128]{1,0:T(8,128)S(1)} custom-call(bf16[512,256]{1,0:T(8,128)(2,1)S(1)} %get-tuple-element.57.refs_0_, bf16[512,256]{1,0:T(8,128)(2,1)S(1)} %get-tuple-element.58.refs_1_, bf16[4,128,256]{2,1,0:T(8,128)(2,1)S(1)} %get-tuple-element.59.refs_2_, bf16[512,512]{1,0:T(8,128)(2,1)S(1)} %get-tuple-element.60.refs_3_, ...), custom_call_target="tpu_custom_call" | custom-call | flops 1 | bytes 1 | tf_op jit(solution)/shard_map/pallas_call | solution.py:435
  46.0 7.9 %all_to_all.16 = f32[8,1,128]{2,1,0:T(1,128)S(1)} all-to-all(f32[8,1,128]{2,1,0:T(1,128)S(1)} %bitcast.6), channel_id=1, replica_groups=mesh['section'=4,'space'=8] {'space'}, dimensions={0} | all-to-all | bytes 8192 | tf_op jit(solution)/shard_map/all_to_all | solution.py:450
  53.9 0.7 %shard_map.93 = f32[1,4,128]{2,1,0:T(4,128)} custom-call(f32[8,128]{1,0:T(8,128)S(1)} %bitcast.7), custom_call_target="tpu_custom_call" | custom-call | flops 1 | bytes 1 | tf_op jit(solution)/shard_map/pallas_call | solution.py:451
  (5 shorter events, 0.1 us)
Async XLA Ops:
  0.0 7.5 %copy-start = (bf16[4,4,128,256]{3,2,1,0:T(8,128)(2,1)S(1)}, bf16[4,4,128,256]{3,2,1,0:T(8,128)(2,1)}, u32[]{:S(2)}) copy-start(bf16[4,4,128,256]{3,2,1,0:T(8,128)(2,1)} %param.8) | copy-start | bytes 3145732
  2.3 5.3 %copy-start.1 = (bf16[8,16,128]{2,1,0:T(8,128)(2,1)S(1)}, bf16[8,16,128]{2,1,0:T(8,128)(2,1)}, u32[]{:S(2)}) copy-start(bf16[8,16,128]{2,1,0:T(8,128)(2,1)} %get-tuple-element.33.own_taps) | copy-start | bytes 98308
  2.3 23.6 %all-to-all-start = ((bf16[4,528,256]{2,1,0:T(8,128)(2,1)}), bf16[4,528,256]{2,1,0:T(8,128)(2,1)S(1)}, u32[]{:S(2)}, u32[]{:S(2)}) async-start(bf16[4,528,256]{2,1,0:T(8,128)(2,1)} %get-tuple-element.43), calls=%async_computation | async-start | bytes 2162688 | tf_op jit(solution)/shard_map/all_to_all | solution.py:407
  7.5 1.7 %collective-permute-start.1 = (bf16[4,128,256]{2,1,0:T(8,128)(2,1)S(1)}, bf16[4,128,256]{2,1,0:T(8,128)(2,1)S(1)}, u32[]{:S(2)}, u32[]{:S(2)}) collective-permute-start(bf16[4,128,256]{2,1,0:T(8,128)(2,1)S(1)} %dynamic-slice_bitcast_fusion.own), channel_id=1, source_target_pairs={{0,1},{1,0},{2,3},{3,2},{4,5},{5,4},{6,7},{7,6},{8,9},{9,8},{10,11... | collective-permute-start | bytes 786440 | tf_op jit(solution)/shard_map/ppermute | solution.py:359
  7.6 1.6 %collective-permute-start = (bf16[8,16,128]{2,1,0:T(8,128)(2,1)S(1)}, bf16[8,16,128]{2,1,0:T(8,128)(2,1)S(1)}, u32[]{:S(2)}, u32[]{:S(2)}) collective-permute-start(bf16[8,16,128]{2,1,0:T(8,128)(2,1)S(1)} %copy-done.1), channel_id=1, source_target_pairs={{0,1},{1,0},{2,3},{3,2},{4,5},{5,4},{6,7},{7,6},{8,9},{9,8},{10,11... | collective-permute-start | bytes 98312 | tf_op jit(solution)/shard_map/ppermute | solution.py:359
  9.3 7.0 %collective-permute-start.2 = (bf16[160,256]{1,0:T(8,128)(2,1)S(1)}, bf16[160,256]{1,0:T(8,128)(2,1)S(1)}, u32[]{:S(2)}, u32[]{:S(2)}) collective-permute-start(bf16[160,256]{1,0:T(8,128)(2,1)S(1)} %get-tuple-element.35), channel_id=1, source_target_pairs={{0,6},{1,7},{2,4},{3,5},{4,2},{5,3},{6,0},{7,1},{8,14},{9,15},{10,... | collective-permute-start | bytes 245768 | tf_op jit(solution)/shard_map/ppermute | solution.py:362
  12.9 7.2 %collective-permute-start.3 = (bf16[160,256]{1,0:T(8,128)(2,1)S(1)}, bf16[160,256]{1,0:T(8,128)(2,1)S(1)}, u32[]{:S(2)}, u32[]{:S(2)}) collective-permute-start(bf16[160,256]{1,0:T(8,128)(2,1)S(1)} %get-tuple-element.36), channel_id=1, source_target_pairs={{0,4},{1,5},{2,6},{3,7},{4,0},{5,1},{6,2},{7,3},{8,12},{9,13},{10,... | collective-permute-start | bytes 245768 | tf_op jit(solution)/shard_map/ppermute | solution.py:362
  12.9 7.2 %collective-permute-start.4 = (bf16[160,256]{1,0:T(8,128)(2,1)S(1)}, bf16[160,256]{1,0:T(8,128)(2,1)S(1)}, u32[]{:S(2)}, u32[]{:S(2)}) collective-permute-start(bf16[160,256]{1,0:T(8,128)(2,1)S(1)} %get-tuple-element.37), channel_id=1, source_target_pairs={{0,2},{1,3},{2,0},{3,1},{4,6},{5,7},{6,4},{7,5},{8,10},{9,11},{10,... | collective-permute-start | bytes 245768 | tf_op jit(solution)/shard_map/ppermute | solution.py:362
  20.2 9.8 %collective-permute-start.5 = (bf16[512,256]{1,0:T(8,128)(2,1)S(1)}, bf16[512,256]{1,0:T(8,128)(2,1)S(1)}, u32[]{:S(2)}, u32[]{:S(2)}) collective-permute-start(bf16[512,256]{1,0:T(8,128)(2,1)S(1)} %shard_map.85.refs_0_), channel_id=1, source_target_pairs={{0,1},{1,0},{2,3},{3,2},{4,5},{5,4},{6,7},{7,6},{8,9},{9,8},{10,11... | collective-permute-start | bytes 786440 | tf_op jit(solution)/shard_map/ppermute | solution.py:359
  20.2 9.8 %collective-permute-start.6 = (bf16[512,256]{1,0:T(8,128)(2,1)S(1)}, bf16[512,256]{1,0:T(8,128)(2,1)S(1)}, u32[]{:S(2)}, u32[]{:S(2)}) collective-permute-start(bf16[512,256]{1,0:T(8,128)(2,1)S(1)} %shard_map.85.refs_0_), channel_id=1, source_target_pairs={{0,8},{1,2},{2,1},{3,4},{4,3},{5,6},{6,5},{7,15},{8,0},{9,10},{10,... | collective-permute-start | bytes 786440 | tf_op jit(solution)/shard_map/ppermute | solution.py:375
  22.3 7.7 %collective-permute-start.7 = (bf16[128,256]{1,0:T(8,128)(2,1)S(1)}, bf16[128,256]{1,0:T(8,128)(2,1)S(1)}, u32[]{:S(2)}, u32[]{:S(2)}) collective-permute-start(bf16[128,256]{1,0:T(8,128)(2,1)S(1)} %shard_map.84.q0), channel_id=1, source_target_pairs={{0,24},{8,16},{16,8},{24,0},{1,25},{9,17},{17,9},{25,1},{2,26},{10... | collective-permute-start | bytes 196616 | tf_op jit(solution)/shard_map/ppermute | solution.py:365
  23.8 6.2 %collective-permute-start.8 = (bf16[128,256]{1,0:T(8,128)(2,1)S(1)}, bf16[128,256]{1,0:T(8,128)(2,1)S(1)}, u32[]{:S(2)}, u32[]{:S(2)}) collective-permute-start(bf16[128,256]{1,0:T(8,128)(2,1)S(1)} %shard_map.84.q0), channel_id=1, source_target_pairs={{0,16},{8,24},{16,0},{24,8},{1,17},{9,25},{17,1},{25,9},{2,18},{10... | collective-permute-start | bytes 196616 | tf_op jit(solution)/shard_map/ppermute | solution.py:365
  23.9 6.1 %collective-permute-start.9 = (bf16[128,256]{1,0:T(8,128)(2,1)S(1)}, bf16[128,256]{1,0:T(8,128)(2,1)S(1)}, u32[]{:S(2)}, u32[]{:S(2)}) collective-permute-start(bf16[128,256]{1,0:T(8,128)(2,1)S(1)} %shard_map.84.q0), channel_id=1, source_target_pairs={{0,8},{8,0},{16,24},{24,16},{1,9},{9,1},{17,25},{25,17},{2,10},{10... | collective-permute-start | bytes 196616 | tf_op jit(solution)/shard_map/ppermute | solution.py:365
  30.0 4.6 %collective-permute-start.11 = (bf16[3,528,256]{2,1,0:T(8,128)(2,1)S(1)}, bf16[3,528,256]{2,1,0:T(8,128)(2,1)S(1)}, u32[]{:S(2)}, u32[]{:S(2)}) collective-permute-start(bf16[3,528,256]{2,1,0:T(8,128)(2,1)S(1)} %slice.9), channel_id=1, source_target_pairs={{0,1},{1,0},{2,3},{3,2},{4,5},{5,4},{6,7},{7,6},{8,9},{9,8},{10,11... | collective-permute-start | bytes 2433032 | tf_op jit(solution)/shard_map/ppermute | solution.py:359
  30.1 2.7 %collective-permute-start.10 = (bf16[1,528,256]{2,1,0:T(8,128)(2,1)S(1)}, bf16[1,528,256]{2,1,0:T(8,128)(2,1)S(1)}, u32[]{:S(2)}, u32[]{:S(2)}) collective-permute-start(bf16[1,528,256]{2,1,0:T(8,128)(2,1)S(1)} %slice.8), channel_id=1, source_target_pairs={{0,1},{1,0},{2,3},{3,2},{4,5},{5,4},{6,7},{7,6},{8,9},{9,8},{10,11... | collective-permute-start | bytes 811016 | tf_op jit(solution)/shard_map/ppermute | solution.py:359
  34.7 3.1 %copy-start.2 = (bf16[256]{0:T(256)(128)(2,1)S(1)}, bf16[256]{0:T(256)(128)(2,1)}, u32[]{:S(2)}) copy-start(bf16[256]{0:T(256)(128)(2,1)} %param.15) | copy-start | bytes 1540
  35.9 3.6 %collective-permute-start.12 = (bf16[512,256]{1,0:T(8,128)(2,1)S(1)}, bf16[512,256]{1,0:T(8,128)(2,1)S(1)}, u32[]{:S(2)}, u32[]{:S(2)}) collective-permute-start(bf16[512,256]{1,0:T(8,128)(2,1)S(1)} %shard_map.89.refs_0_), channel_id=1, source_target_pairs={{0,1},{1,0},{2,3},{3,2},{4,5},{5,4},{6,7},{7,6},{8,9},{9,8},{10,11... | collective-permute-start | bytes 786440 | tf_op jit(solution)/shard_map/ppermute | solution.py:359
  36.1 6.4 %collective-permute-start.13 = (bf16[512,256]{1,0:T(8,128)(2,1)S(1)}, bf16[512,256]{1,0:T(8,128)(2,1)S(1)}, u32[]{:S(2)}, u32[]{:S(2)}) collective-permute-start(bf16[512,256]{1,0:T(8,128)(2,1)S(1)} %shard_map.89.refs_0_), channel_id=1, source_target_pairs={{0,8},{1,2},{2,1},{3,4},{4,3},{5,6},{6,5},{7,15},{8,0},{9,10},{10,... | collective-permute-start | bytes 786440 | tf_op jit(solution)/shard_map/ppermute | solution.py:375

commit v4 on v3

--- a/solution.py
+++ b/solution.py
@@ -198,14 +198,15 @@
         edge = [jnp.where(c == 0, sib_taps[m + 6], sib_taps[m + 4]) for m in range(2)]
         chunk[to, GROUP + 16 : GROUP + 32, :] = jnp.concatenate(edge, 1)
     for k, out in enumerate((o0, o1, o2, o3)):
-        out[...] = chunk[z ^ k]
+        out[...] = chunk[z ^ k, 0 : out.shape[0], :]
 
 
 def tables_kernel(g0, g3, g2, g1, own_taps, sib_taps, taps, edges):
     _, c, z, _ = position()
     for k, g in enumerate((g0, g1, g2, g3)):
         taps[16 * k : 16 * (k + 1), :] = g[GROUP : GROUP + 16, :]
-        edges[z ^ k] = g[GROUP + 16 : GROUP + 32, :]
+        if k != 2:
+            edges[z ^ k] = g[GROUP + 16 : GROUP + 32, :]
     edge = edges[(z + 3 + 2 * c) % 4]
     for m in range(4):
         core, chip = sib_taps[4 + (m + 2) % 4], edge[:, WIDE * (m % 2) : WIDE * (m % 2 + 1)]
@@ -304,7 +305,7 @@
         readout, refs = refs[0], refs[1:]
     mine, theirs, refs = refs[0], refs[1], refs[2:]
     outs, rows = refs[: 1 + wide], refs[1 + wide :]
-    halves = (mine.at[layer], theirs.at[max(layer - 1, 0)])
+    halves = (mine.at[layer], theirs.at[layer % 2])
     channels = cells[0].shape[-1]
     for g in range(4):
         cut = slice(GROUP * g, GROUP * (g + 1))
@@ -312,7 +313,7 @@
         done = jnp.dot(bands[g], stacked, preferred_element_type=F32).astype(BF16)
         for n, row in enumerate(rows):
             row[cut, :] = done[GROUP * n : GROUP * (n + 1)]
-    size = 256
+    size = 512
     mixed = [
         jnp.dot(band[size * b : size * (b + 1), :], row[...], preferred_element_type=F32)
         for band, row in zip(col_bands, rows)
@@ -326,25 +327,31 @@
         for half in halves:
             bias = half[512:528, :].astype(F32)[0:1]
             hidden = jnp.dot(normed, half[0:256, :], preferred_element_type=F32) + bias
-            hidden = jax.nn.gelu(hidden, approximate=True).astype(BF16)
+            inner = hidden * (0.7978845608028654 + 0.035677408136300125 * (hidden * hidden))
+            hidden = 0.5 * hidden
+            hidden = (hidden + hidden * jnp.tanh(inner)).astype(BF16)
             parts.append(jnp.dot(hidden, half[256:512, :], preferred_element_type=F32))
         total = (total + (parts[0] + parts[1])).astype(BF16)
-        out, b = outs[n // 2], n % 2
+        out, b = outs[n // (CELLS // size)], n % (CELLS // size)
         if final:
             reader = jnp.broadcast_to(readout[...], (8, channels))
             logit = lax.dot_general(reader, total, (((1,), (1,)), ((), ())), preferred_element_type=F32)
             logit = jnp.maximum(logit, 0.0) + jnp.log1p(jnp.exp(-jnp.abs(logit)))
-            for d in range(4):
+            for d in range(size // 64):
                 moved = pltpu.roll(logit, size - 64 * d, 1) if d else logit
-                out[4 * b + d : 4 * b + d + 1, :] = moved[0:1, 0:WIDE]
+                out[size // 64 * b + d : size // 64 * b + d + 1, :] = moved[0:1, 0:WIDE]
         else:
             out[size * b : size * (b + 1), :] = total
 
 
-def gather_kernel(got, out):
+def gather_kernel(g0, g3, g2, g1, out, parts):
+    _, _, z, p = position()
+    for k, g in enumerate((g0, g1, g2, g3)):
+        parts[z ^ k] = g[...]
     lane, line = iota((8, WIDE), 1), iota((8, WIDE), 0)
     mask = lane // COLS == line
-    cells = pltpu.roll(got[...], 0, 1, stride=COLS, stride_axis=0)
+    cells = jnp.concatenate([parts[g, core, pl.ds(p, 1), :] for g in range(4) for core in range(2)], 0)
+    cells = pltpu.roll(cells, 0, 1, stride=COLS, stride_axis=0)
     for t in range(4):
         moved = pltpu.roll(cells, WIDE - COLS * t, 1) if t else cells
         out[0, t : t + 1, :] = jnp.sum(jnp.where(mask, moved, 0.0), axis=0, keepdims=True)
@@ -390,14 +397,14 @@
             pltpu.SemaphoreType.DMA((6,)),
             pltpu.SemaphoreType.DMA((5,)),
         ],
-        room=60,
+        room=56,
         place=ANY,
     )(row_coef, col_coef, weight_in, weight_out, bias_in, norm_gain)
     sib = core(own)
 
     chunks = call(
         chunk_kernel,
-        (shaped((GROUP + 32, channels)),) * 4,
+        tuple(shaped((GROUP + lines, channels)) for lines in (32, 32, 16, 32)),
         [VMEM] * 4,
         [pltpu.VMEM((4, GROUP + 32, channels), BF16)],
     )(own, sib, window, window_sib)
@@ -413,7 +420,7 @@
     field_core, field_chip = core(field), beside(field)
     tables = [section(taps, k) for k in (3, 2, 1)]
     tables = [taps] + tables[::-1]
-    theirs = [core(after(m, *tables[::-1], field_core, field_chip)) for m in (mine[:1], mine[1:])]
+    theirs = [core(after(m, *tables[::-1], field_core, field_chip)) for m in (mine[:2], mine[2:])]
 
     def prepare(layers, tables):
         outs = []
@@ -437,7 +444,7 @@
             outs,
             [VMEM] * (len(cells) + 4 + wide + final),
             [pltpu.VMEM((CELLS, channels), BF16)] * (1 + wide),
-        )(*cells, bands[-1], *bands[:-1], *readers, mine, theirs[layer > 0])
+        )(*cells, bands[-1], *bands[:-1], *readers, mine, theirs[layer // 2])
 
     bands0 = prepare((0,), [after(tables[0], field_chip)] + tables[1:])
     cells = run(0, (field, field_core, field_chip), bands0)
@@ -447,8 +454,12 @@
     cells = run(2, (state, core(state), beside(state)), bands23[:3])
     (density,) = run(3, cells, bands23[3:], (readout.reshape(1, channels),))
 
-    density = lax.all_to_all(density, "space", split_axis=0, concat_axis=0, tiled=True)
-    return call(gather_kernel, shaped((1, 4, WIDE), F32), [VMEM])(density)
+    beside_density = core(density)
+    pair = jnp.where(c == 0, jnp.stack([density, beside_density]), jnp.stack([beside_density, density]))
+    pairs = [chip(pair, k) for k in (3, 2, 1)]
+    return call(
+        gather_kernel, shaped((1, 4, WIDE), F32), [VMEM] * 4, [pltpu.VMEM((4, 2, 8, WIDE), F32)]
+    )(pair, *pairs)
 
 
 def on_device(raster, row_coef, *rest):

time: 54.9 us -> 52.4 us (0.954)
  blocking collectives: 7.93 us -> 0 us
  starting transfers between devices: 18.4 us -> 22.8 us
  waiting for transfers between devices: 15 us -> 16.4 us
    all_to_all x1 -> x0, blocking collectives: 7.93 us -> none  [window_on_section(): lax.all_to_all(density, 'space', split_axis=0, concat_axis=0, tiled=True)]
    ppermute x3 -> x6, starting transfers between devices: 4.45 us -> 8.84 us  [chip(): return lax.ppermute(array, 'space', [(i, i ^ 2 * k) for i in range(spaces)])]
    ppermute x3 -> x6, waiting for transfers between devices: 6.38 us -> 7.68 us  [chip(): return lax.ppermute(array, 'space', [(i, i ^ 2 * k) for i in range(spaces)])]
    ppermute x6 -> x7, waiting for transfers between devices: 1.62 us -> 2.13 us  [core(): return lax.ppermute(array, 'space', [(i, i ^ 1) for i in range(spaces)])]
    ppermute x6 -> x7, starting transfers between devices: 1.46 us -> 1.47 us  [core(): return lax.ppermute(array, 'space', [(i, i ^ 1) for i in range(spaces)])]
  transfers between devices with their start and end apart: 15 -> 19, of which waited for: 6 -> 8; matrix products, arithmetic and copies ran while one was open for 0% -> 0% of each run, Pallas kernels for 10% -> 12%
where the time goes in v4:
time: 52.4 us; the launch traced here: 52.1 us
  starting transfers between devices  22.8 us (44%)
  waiting for transfers between devices  16.4 us (31%)
  Pallas kernels  12.6 us (24%)
    ppermute x6, starting transfers between devices, chip(): return lax.ppermute(array, 'space', [(i, i ^ 2 * k) for i in range(spaces)])  8.84 us
    ppermute x6, waiting for transfers between devices, chip(): return lax.ppermute(array, 'space', [(i, i ^ 2 * k) for i in range(spaces)])  7.68 us
    pallas_call x4, Pallas kernels, run(): call(functools.partial(layer_kernel, layer, len(cells), final), outs, [VM...  6.13 us
    all_to_all x1, starting transfers between devices, window_on_section(): lax.all_to_all(packed, 'section', split_axis=0, concat_axis=0, tiled=True)  5.18 us
    ppermute x2, starting transfers between devices, beside(): return lax.ppermute(array, ('section', 'space'), pairs)  3.87 us
    ppermute x3, waiting for transfers between devices, section(): return lax.ppermute(array, 'section', [(i, i ^ k) for i in range(4)])  3.77 us
    ppermute x3, starting transfers between devices, section(): return lax.ppermute(array, 'section', [(i, i ^ k) for i in range(4)])  3.49 us
    pallas_call x3, Pallas kernels, prepare(): call(functools.partial(prepare_kernel, layers, spaces - 1), tuple(outs),...  3.26 us
  transfers between devices with their start and end apart: 19, of which 8 were waited for; matrix products, arithmetic and copies ran while one was open for 0% of the time, Pallas kernels for 12%

profile of v4, /device:TPU:0, one launch (start us, length us, event | category | flops | bytes accessed | tf_op | source)
XLA Modules:
  0.0 52.1 jit_solution(12787310149261860919)
XLA Ops:
  0.0 2.3 %shard_map.82 = (bf16[4,528,256]{2,1,0:T(8,128)(2,1)}, bf16[8,16,128]{2,1,0:T(8,128)(2,1)}) custom-call(bf16[1,15,4,128]{3,2,1,0:T(4,128)(2,1)} %row_coef.1, bf16[1,15,16,32]{3,2,1,0:T(8,128)(2,1)} %col_coef.1, bf16[1,256,512]{2,1,0:T(8,128)(2,1)} %weight_in.1, bf16[1,512,256]{2,1,0:T(8,128)(2,1)} %weight_out.1, bf16[1,512]{1,0:T(2,128)(2,1)} %bias.1, ...), custom_call_target="tpu_custom_call" | custom-call | flops 1 | bytes 1 | tf_op jit(solution)/shard_map/pallas_call | solution.py:386
  2.3 5.2 %all-to-all-start = ((bf16[4,528,256]{2,1,0:T(8,128)(2,1)}), bf16[4,528,256]{2,1,0:T(8,128)(2,1)S(1)}, u32[]{:S(2)}, u32[]{:S(2)}) async-start(bf16[4,528,256]{2,1,0:T(8,128)(2,1)} %get-tuple-element.43), calls=%async_computation | async-start | bytes 2162688 | tf_op jit(solution)/shard_map/all_to_all | solution.py:414
  7.5 0.1 collective-permute-start.1
  7.6 0.5 collective-permute-start
  8.1 1.1 %collective-permute-done.sib_taps = bf16[8,16,128]{2,1,0:T(8,128)(2,1)S(1)} collective-permute-done((bf16[8,16,128]{2,1,0:T(8,128)(2,1)S(1)}, bf16[8,16,128]{2,1,0:T(8,128)(2,1)S(1)}, u32[]{:S(2)}, u32[]{:S(2)}) %collective-permute-start) | collective-permute-done | bytes 32800 | tf_op jit(solution)/shard_map/ppermute | solution.py:366
  9.1 0.0 collective-permute-done.1.sib
  9.1 0.1 shard_map.83
  9.3 3.7 %collective-permute-start.2 = (bf16[160,256]{1,0:T(8,128)(2,1)S(1)}, bf16[160,256]{1,0:T(8,128)(2,1)S(1)}, u32[]{:S(2)}, u32[]{:S(2)}) collective-permute-start(bf16[160,256]{1,0:T(8,128)(2,1)S(1)} %get-tuple-element.35), channel_id=1, source_target_pairs={{0,6},{1,7},{2,4},{3,5},{4,2},{5,3},{6,0},{7,1},{8,14},{9,15},{10,... | collective-permute-start | bytes 245768 | tf_op jit(solution)/shard_map/ppermute | solution.py:369
  12.9 0.0 collective-permute-start.4
  12.9 0.8 %collective-permute-start.3 = (bf16[144,256]{1,0:T(8,128)(2,1)S(1)}, bf16[144,256]{1,0:T(8,128)(2,1)S(1)}, u32[]{:S(2)}, u32[]{:S(2)}) collective-permute-start(bf16[144,256]{1,0:T(8,128)(2,1)S(1)} %get-tuple-element.36), channel_id=1, source_target_pairs={{0,4},{1,5},{2,6},{3,7},{4,0},{5,1},{6,2},{7,3},{8,12},{9,13},{10,... | collective-permute-start | bytes 221192 | tf_op jit(solution)/shard_map/ppermute | solution.py:369
  13.7 6.0 %collective-permute-done.3.g2 = bf16[144,256]{1,0:T(8,128)(2,1)S(1)} collective-permute-done((bf16[144,256]{1,0:T(8,128)(2,1)S(1)}, bf16[144,256]{1,0:T(8,128)(2,1)S(1)}, u32[]{:S(2)}, u32[]{:S(2)}) %collective-permute-start.3) | collective-permute-done | bytes 73760 | tf_op jit(solution)/shard_map/ppermute | solution.py:369
  19.8 0.0 collective-permute-done.2.g3
  19.8 0.0 collective-permute-done.4.g1
  19.8 0.1 collective-permute-start.5
  19.9 2.1 %collective-permute-start.6 = (bf16[512,256]{1,0:T(8,128)(2,1)S(1)}, bf16[512,256]{1,0:T(8,128)(2,1)S(1)}, u32[]{:S(2)}, u32[]{:S(2)}) collective-permute-start(bf16[512,256]{1,0:T(8,128)(2,1)S(1)} %shard_map.85.refs_0_), channel_id=1, source_target_pairs={{0,8},{1,2},{2,1},{3,4},{4,3},{5,6},{6,5},{7,15},{8,0},{9,10},{10,... | collective-permute-start | bytes 786440 | tf_op jit(solution)/shard_map/ppermute | solution.py:382
  22.0 1.5 %collective-permute-start.7 = (bf16[128,256]{1,0:T(8,128)(2,1)S(1)}, bf16[128,256]{1,0:T(8,128)(2,1)S(1)}, u32[]{:S(2)}, u32[]{:S(2)}) collective-permute-start(bf16[128,256]{1,0:T(8,128)(2,1)S(1)} %shard_map.84.q0), channel_id=1, source_target_pairs={{0,24},{8,16},{16,8},{24,0},{1,25},{9,17},{17,9},{25,1},{2,26},{10... | collective-permute-start | bytes 196616 | tf_op jit(solution)/shard_map/ppermute | solution.py:372
  23.5 0.1 collective-permute-start.8
  23.6 1.9 %collective-permute-start.9 = (bf16[128,256]{1,0:T(8,128)(2,1)S(1)}, bf16[128,256]{1,0:T(8,128)(2,1)S(1)}, u32[]{:S(2)}, u32[]{:S(2)}) collective-permute-start(bf16[128,256]{1,0:T(8,128)(2,1)S(1)} %shard_map.84.q0), channel_id=1, source_target_pairs={{0,8},{8,0},{16,24},{24,16},{1,9},{9,1},{17,25},{25,17},{2,10},{10... | collective-permute-start | bytes 196616 | tf_op jit(solution)/shard_map/ppermute | solution.py:372
  25.5 0.0 all-to-all-done.refs_6_.refs_4_.refs_5_
  25.5 0.1 fusion
  25.6 3.8 %collective-permute-done.7.q3 = bf16[128,256]{1,0:T(8,128)(2,1)S(1)} collective-permute-done((bf16[128,256]{1,0:T(8,128)(2,1)S(1)}, bf16[128,256]{1,0:T(8,128)(2,1)S(1)}, u32[]{:S(2)}, u32[]{:S(2)}) %collective-permute-start.7) | collective-permute-done | bytes 65568 | tf_op jit(solution)/shard_map/ppermute | solution.py:372
  29.3 0.0 collective-permute-done.8.q2
  29.3 0.0 collective-permute-done.9.q1
  29.3 0.0 collective-permute-done.5.refs_1_
  29.4 0.1 collective-permute-start.10
  29.4 0.5 collective-permute-start.13
  29.9 1.0 %shard_map.86 = (bf16[512,512]{1,0:T(8,128)(2,1)S(1)}, bf16[512,512]{1,0:T(8,128)(2,1)S(1)}, bf16[4,256,384]{2,1,0:T(8,128)(2,1)S(1)}) custom-call(bf16[128,256]{1,0:T(8,128)(2,1)S(1)} %shard_map.84.q0, bf16[128,256]{1,0:T(8,128)(2,1)S(1)} %collective-permute-done.7.q3, bf16[128,256]{1,0:T(8,128)(2,1)S(1)} %collective-permute-done.8.q2, ...), custom_call_target="tpu_custom_call" | custom-call | flops 1 | bytes 1 | tf_op jit(solution)/shard_map/pallas_call | solution.py:431
  30.9 0.6 %shard_map.88 = (bf16[512,512]{1,0:T(8,128)(2,1)S(1)}, bf16[4,128,256]{2,1,0:T(8,128)(2,1)S(1)}) custom-call(bf16[128,256]{1,0:T(8,128)(2,1)S(1)} %shard_map.84.q0, bf16[128,256]{1,0:T(8,128)(2,1)S(1)} %collective-permute-done.7.q3, bf16[128,256]{1,0:T(8,128)(2,1)S(1)} %collective-permute-done.8.q2, bf16[128,256]{1,0:T(8,128)(2,1)S(1)} %collective-permute-done.9.q1), custom_call_target="tpu_custom_call" | custom-call | flops 1 | bytes 1 | tf_op jit(solution)/shard_map/pallas_call | solution.py:431
  31.5 0.0 collective-permute-done.10.refs_7_.refs_5_
  31.5 1.8 %shard_map.87 = (bf16[512,256]{1,0:T(8,128)(2,1)S(1)}, bf16[512,256]{1,0:T(8,128)(2,1)S(1)}) custom-call(bf16[512,256]{1,0:T(8,128)(2,1)S(1)} %shard_map.85.refs_0_, bf16[512,256]{1,0:T(8,128)(2,1)S(1)} %collective-permute-done.5.refs_1_, bf16[512,256]{1,0:T(8,128)(2,1)S(1)} %collective-permute-done.6.refs_2_, ...), custom_call_target="tpu_custom_call" | custom-call | flops 1 | bytes 1 | tf_op jit(solution)/shard_map/pallas_call | solution.py:442
  33.3 0.0 copy-start.2
  33.3 1.2 %shard_map.89.refs_0_ = bf16[512,256]{1,0:T(8,128)(2,1)S(1)} custom-call(bf16[512,256]{1,0:T(8,128)(2,1)S(1)} %get-tuple-element.45.refs_0_, bf16[512,256]{1,0:T(8,128)(2,1)S(1)} %get-tuple-element.46.refs_1_, bf16[4,128,256]{2,1,0:T(8,128)(2,1)S(1)} %get-tuple-element.47.refs_2_, bf16[512,512]{1,0:T(8,128)(2,1)S(1)} %get-tuple-element.48.refs_3_, ...), custom_call_target="tpu_custom_call" | custom-call | flops 1 | bytes 1 | tf_op jit(solution)/shard_map/pallas_call | solution.py:442
  34.5 0.1 collective-permute-start.11
  34.6 1.8 %collective-permute-start.12 = (bf16[512,256]{1,0:T(8,128)(2,1)S(1)}, bf16[512,256]{1,0:T(8,128)(2,1)S(1)}, u32[]{:S(2)}, u32[]{:S(2)}) collective-permute-start(bf16[512,256]{1,0:T(8,128)(2,1)S(1)} %shard_map.89.refs_0_), channel_id=1, source_target_pairs={{0,8},{1,2},{2,1},{3,4},{4,3},{5,6},{6,5},{7,15},{8,0},{9,10},{10,... | collective-permute-start | bytes 786440 | tf_op jit(solution)/shard_map/ppermute | solution.py:382
  36.4 1.7 %shard_map.90 = (bf16[512,512]{1,0:T(8,128)(2,1)S(1)}, bf16[512,512]{1,0:T(8,128)(2,1)S(1)}, bf16[4,256,384]{2,1,0:T(8,128)(2,1)S(1)}, bf16[512,512]{1,0:T(8,128)(2,1)S(1)}, bf16[4,128,256]{2,1,0:T(8,128)(2,1)S(1)}) custom-call(bf16[128,256]{1,0:T(8,128)(2,1)S(1)} %shard_map.84.q0, bf16[128,256]{1,0:T(8,128)(2,1)S(1)} %collective-permute-done.7.q3, ...), custom_call_target="tpu_custom_call" | custom-call | flops 1 | bytes 1 | tf_op jit(solution)/shard_map/pallas_call | solution.py:431
  38.2 0.0 collective-permute-done.13.refs_7_.refs_6_
  38.2 2.8 %collective-permute-done.12.refs_2_ = bf16[512,256]{1,0:T(8,128)(2,1)S(1)} collective-permute-done((bf16[512,256]{1,0:T(8,128)(2,1)S(1)}, bf16[512,256]{1,0:T(8,128)(2,1)S(1)}, u32[]{:S(2)}, u32[]{:S(2)}) %collective-permute-start.12) | collective-permute-done | bytes 262176 | tf_op jit(solution)/shard_map/ppermute | solution.py:382
  41.0 1.8 %shard_map.91 = (bf16[512,256]{1,0:T(8,128)(2,1)S(1)}, bf16[512,256]{1,0:T(8,128)(2,1)S(1)}) custom-call(bf16[512,256]{1,0:T(8,128)(2,1)S(1)} %shard_map.89.refs_0_, bf16[512,256]{1,0:T(8,128)(2,1)S(1)} %collective-permute-done.11.refs_1_, bf16[512,256]{1,0:T(8,128)(2,1)S(1)} %collective-permute-done.12.refs_2_, ...), custom_call_target="tpu_custom_call" | custom-call | flops 1 | bytes 1 | tf_op jit(solution)/shard_map/pallas_call | solution.py:442
  42.8 1.4 %shard_map.92 = f32[8,128]{1,0:T(8,128)S(1)} custom-call(bf16[512,256]{1,0:T(8,128)(2,1)S(1)} %get-tuple-element.57.refs_0_, bf16[512,256]{1,0:T(8,128)(2,1)S(1)} %get-tuple-element.58.refs_1_, bf16[4,128,256]{2,1,0:T(8,128)(2,1)S(1)} %get-tuple-element.59.refs_2_, bf16[512,512]{1,0:T(8,128)(2,1)S(1)} %get-tuple-element.60.refs_3_, ...), custom_call_target="tpu_custom_call" | custom-call | flops 1 | bytes 1 | tf_op jit(solution)/shard_map/pallas_call | solution.py:442
  44.2 0.1 collective-permute-start.14
  44.3 1.1 %collective-permute-done.14 = f32[8,128]{1,0:T(8,128)S(1)} collective-permute-done((f32[8,128]{1,0:T(8,128)S(1)}, f32[8,128]{1,0:T(8,128)S(1)}, u32[]{:S(2)}, u32[]{:S(2)}) %collective-permute-start.14) | collective-permute-done | bytes 4128 | tf_op jit(solution)/shard_map/ppermute | solution.py:366
  45.4 1.2 %collective-permute-start.15 = (f32[2,8,128]{2,1,0:T(8,128)S(1)}, f32[2,8,128]{2,1,0:T(8,128)S(1)}, u32[]{:S(2)}, u32[]{:S(2)}) collective-permute-start(f32[2,8,128]{2,1,0:T(8,128)S(1)} %maximum_select_fusion.g0), channel_id=1, source_target_pairs={{0,6},{1,7},{2,4},{3,5},{4,2},{5,3},{6,0},{7,1},{8,14},{9,15},{10,... | collective-permute-start | bytes 24584 | tf_op jit(solution)/shard_map/ppermute | solution.py:369
  46.6 0.1 collective-permute-start.16
  46.7 3.0 %collective-permute-start.17 = (f32[2,8,128]{2,1,0:T(8,128)S(1)}, f32[2,8,128]{2,1,0:T(8,128)S(1)}, u32[]{:S(2)}, u32[]{:S(2)}) collective-permute-start(f32[2,8,128]{2,1,0:T(8,128)S(1)} %maximum_select_fusion.g0), channel_id=1, source_target_pairs={{0,2},{1,3},{2,0},{3,1},{4,6},{5,7},{6,4},{7,5},{8,10},{9,11},{10,... | collective-permute-start | bytes 24584 | tf_op jit(solution)/shard_map/ppermute | solution.py:369
  49.8 1.1 %collective-permute-done.15.g3 = f32[2,8,128]{2,1,0:T(8,128)S(1)} collective-permute-done((f32[2,8,128]{2,1,0:T(8,128)S(1)}, f32[2,8,128]{2,1,0:T(8,128)S(1)}, u32[]{:S(2)}, u32[]{:S(2)}) %collective-permute-start.15) | collective-permute-done | bytes 8224 | tf_op jit(solution)/shard_map/ppermute | solution.py:369
  50.8 0.3 collective-permute-done.16.g2
  51.1 0.3 collective-permute-done.17.g1
  51.4 0.7 %shard_map.93 = f32[1,4,128]{2,1,0:T(4,128)} custom-call(f32[2,8,128]{2,1,0:T(8,128)S(1)} %maximum_select_fusion.g0, f32[2,8,128]{2,1,0:T(8,128)S(1)} %collective-permute-done.15.g3, f32[2,8,128]{2,1,0:T(8,128)S(1)} %collective-permute-done.16.g2, f32[2,8,128]{2,1,0:T(8,128)S(1)} %collective-permute-done.17.g1), custom_call_target="tpu_custom_call" | custom-call | flops 1 | bytes 1 | tf_op jit(solution)/shard_map/pallas_call | solution.py:460
  (12 shorter events, 0.1 us)
Async XLA Ops:
  0.0 7.5 %copy-start = (bf16[4,4,128,256]{3,2,1,0:T(8,128)(2,1)S(1)}, bf16[4,4,128,256]{3,2,1,0:T(8,128)(2,1)}, u32[]{:S(2)}) copy-start(bf16[4,4,128,256]{3,2,1,0:T(8,128)(2,1)} %param.8) | copy-start | bytes 3145732
  2.3 5.3 %copy-start.1 = (bf16[8,16,128]{2,1,0:T(8,128)(2,1)S(1)}, bf16[8,16,128]{2,1,0:T(8,128)(2,1)}, u32[]{:S(2)}) copy-start(bf16[8,16,128]{2,1,0:T(8,128)(2,1)} %get-tuple-element.33.own_taps) | copy-start | bytes 98308
  2.3 23.2 %all-to-all-start = ((bf16[4,528,256]{2,1,0:T(8,128)(2,1)}), bf16[4,528,256]{2,1,0:T(8,128)(2,1)S(1)}, u32[]{:S(2)}, u32[]{:S(2)}) async-start(bf16[4,528,256]{2,1,0:T(8,128)(2,1)} %get-tuple-element.43), calls=%async_computation | async-start | bytes 2162688 | tf_op jit(solution)/shard_map/all_to_all | solution.py:414
  7.5 1.7 %collective-permute-start.1 = (bf16[4,128,256]{2,1,0:T(8,128)(2,1)S(1)}, bf16[4,128,256]{2,1,0:T(8,128)(2,1)S(1)}, u32[]{:S(2)}, u32[]{:S(2)}) collective-permute-start(bf16[4,128,256]{2,1,0:T(8,128)(2,1)S(1)} %dynamic-slice_bitcast_fusion.own), channel_id=1, source_target_pairs={{0,1},{1,0},{2,3},{3,2},{4,5},{5,4},{6,7},{7,6},{8,9},{9,8},{10,11... | collective-permute-start | bytes 786440 | tf_op jit(solution)/shard_map/ppermute | solution.py:366
  7.6 1.6 %collective-permute-start = (bf16[8,16,128]{2,1,0:T(8,128)(2,1)S(1)}, bf16[8,16,128]{2,1,0:T(8,128)(2,1)S(1)}, u32[]{:S(2)}, u32[]{:S(2)}) collective-permute-start(bf16[8,16,128]{2,1,0:T(8,128)(2,1)S(1)} %copy-done.1), channel_id=1, source_target_pairs={{0,1},{1,0},{2,3},{3,2},{4,5},{5,4},{6,7},{7,6},{8,9},{9,8},{10,11... | collective-permute-start | bytes 98312 | tf_op jit(solution)/shard_map/ppermute | solution.py:366
  9.3 10.5 %collective-permute-start.2 = (bf16[160,256]{1,0:T(8,128)(2,1)S(1)}, bf16[160,256]{1,0:T(8,128)(2,1)S(1)}, u32[]{:S(2)}, u32[]{:S(2)}) collective-permute-start(bf16[160,256]{1,0:T(8,128)(2,1)S(1)} %get-tuple-element.35), channel_id=1, source_target_pairs={{0,6},{1,7},{2,4},{3,5},{4,2},{5,3},{6,0},{7,1},{8,14},{9,15},{10,... | collective-permute-start | bytes 245768 | tf_op jit(solution)/shard_map/ppermute | solution.py:369
  12.9 6.8 %collective-permute-start.4 = (bf16[160,256]{1,0:T(8,128)(2,1)S(1)}, bf16[160,256]{1,0:T(8,128)(2,1)S(1)}, u32[]{:S(2)}, u32[]{:S(2)}) collective-permute-start(bf16[160,256]{1,0:T(8,128)(2,1)S(1)} %get-tuple-element.37), channel_id=1, source_target_pairs={{0,2},{1,3},{2,0},{3,1},{4,6},{5,7},{6,4},{7,5},{8,10},{9,11},{10,... | collective-permute-start | bytes 245768 | tf_op jit(solution)/shard_map/ppermute | solution.py:369
  12.9 6.8 %collective-permute-start.3 = (bf16[144,256]{1,0:T(8,128)(2,1)S(1)}, bf16[144,256]{1,0:T(8,128)(2,1)S(1)}, u32[]{:S(2)}, u32[]{:S(2)}) collective-permute-start(bf16[144,256]{1,0:T(8,128)(2,1)S(1)} %get-tuple-element.36), channel_id=1, source_target_pairs={{0,4},{1,5},{2,6},{3,7},{4,0},{5,1},{6,2},{7,3},{8,12},{9,13},{10,... | collective-permute-start | bytes 221192 | tf_op jit(solution)/shard_map/ppermute | solution.py:369
  19.8 9.5 %collective-permute-start.5 = (bf16[512,256]{1,0:T(8,128)(2,1)S(1)}, bf16[512,256]{1,0:T(8,128)(2,1)S(1)}, u32[]{:S(2)}, u32[]{:S(2)}) collective-permute-start(bf16[512,256]{1,0:T(8,128)(2,1)S(1)} %shard_map.85.refs_0_), channel_id=1, source_target_pairs={{0,1},{1,0},{2,3},{3,2},{4,5},{5,4},{6,7},{7,6},{8,9},{9,8},{10,11... | collective-permute-start | bytes 786440 | tf_op jit(solution)/shard_map/ppermute | solution.py:366
  19.9 9.4 %collective-permute-start.6 = (bf16[512,256]{1,0:T(8,128)(2,1)S(1)}, bf16[512,256]{1,0:T(8,128)(2,1)S(1)}, u32[]{:S(2)}, u32[]{:S(2)}) collective-permute-start(bf16[512,256]{1,0:T(8,128)(2,1)S(1)} %shard_map.85.refs_0_), channel_id=1, source_target_pairs={{0,8},{1,2},{2,1},{3,4},{4,3},{5,6},{6,5},{7,15},{8,0},{9,10},{10,... | collective-permute-start | bytes 786440 | tf_op jit(solution)/shard_map/ppermute | solution.py:382
  22.0 7.3 %collective-permute-start.7 = (bf16[128,256]{1,0:T(8,128)(2,1)S(1)}, bf16[128,256]{1,0:T(8,128)(2,1)S(1)}, u32[]{:S(2)}, u32[]{:S(2)}) collective-permute-start(bf16[128,256]{1,0:T(8,128)(2,1)S(1)} %shard_map.84.q0), channel_id=1, source_target_pairs={{0,24},{8,16},{16,8},{24,0},{1,25},{9,17},{17,9},{25,1},{2,26},{10... | collective-permute-start | bytes 196616 | tf_op jit(solution)/shard_map/ppermute | solution.py:372
  23.5 5.9 %collective-permute-start.8 = (bf16[128,256]{1,0:T(8,128)(2,1)S(1)}, bf16[128,256]{1,0:T(8,128)(2,1)S(1)}, u32[]{:S(2)}, u32[]{:S(2)}) collective-permute-start(bf16[128,256]{1,0:T(8,128)(2,1)S(1)} %shard_map.84.q0), channel_id=1, source_target_pairs={{0,16},{8,24},{16,0},{24,8},{1,17},{9,25},{17,1},{25,9},{2,18},{10... | collective-permute-start | bytes 196616 | tf_op jit(solution)/shard_map/ppermute | solution.py:372
  23.6 5.8 %collective-permute-start.9 = (bf16[128,256]{1,0:T(8,128)(2,1)S(1)}, bf16[128,256]{1,0:T(8,128)(2,1)S(1)}, u32[]{:S(2)}, u32[]{:S(2)}) collective-permute-start(bf16[128,256]{1,0:T(8,128)(2,1)S(1)} %shard_map.84.q0), channel_id=1, source_target_pairs={{0,8},{8,0},{16,24},{24,16},{1,9},{9,1},{17,25},{25,17},{2,10},{10... | collective-permute-start | bytes 196616 | tf_op jit(solution)/shard_map/ppermute | solution.py:372
  29.4 2.1 %collective-permute-start.10 = (bf16[2,528,256]{2,1,0:T(8,128)(2,1)S(1)}, bf16[2,528,256]{2,1,0:T(8,128)(2,1)S(1)}, u32[]{:S(2)}, u32[]{:S(2)}) collective-permute-start(bf16[2,528,256]{2,1,0:T(8,128)(2,1)S(1)} %get-tuple-element.44), channel_id=1, source_target_pairs={{0,1},{1,0},{2,3},{3,2},{4,5},{5,4},{6,7},{7,6},{8,9},{9,8},{10,11... | collective-permute-start | bytes 1622024 | tf_op jit(solution)/shard_map/ppermute | solution.py:366
  29.4 8.7 %collective-permute-start.13 = (bf16[2,528,256]{2,1,0:T(8,128)(2,1)S(1)}, bf16[2,528,256]{2,1,0:T(8,128)(2,1)S(1)}, u32[]{:S(2)}, u32[]{:S(2)}) collective-permute-start(bf16[2,528,256]{2,1,0:T(8,128)(2,1)S(1)} %get-tuple-element.56), channel_id=1, source_target_pairs={{0,1},{1,0},{2,3},{3,2},{4,5},{5,4},{6,7},{7,6},{8,9},{9,8},{10,11... | collective-permute-start | bytes 1622024 | tf_op jit(solution)/shard_map/ppermute | solution.py:366
  33.3 3.1 %copy-start.2 = (bf16[256]{0:T(256)(128)(2,1)S(1)}, bf16[256]{0:T(256)(128)(2,1)}, u32[]{:S(2)}) copy-start(bf16[256]{0:T(256)(128)(2,1)} %param.15) | copy-start | bytes 1540
  34.5 3.7 %collective-permute-start.11 = (bf16[512,256]{1,0:T(8,128)(2,1)S(1)}, bf16[512,256]{1,0:T(8,128)(2,1)S(1)}, u32[]{:S(2)}, u32[]{:S(2)}) collective-permute-start(bf16[512,256]{1,0:T(8,128)(2,1)S(1)} %shard_map.89.refs_0_), channel_id=1, source_target_pairs={{0,1},{1,0},{2,3},{3,2},{4,5},{5,4},{6,7},{7,6},{8,9},{9,8},{10,11... | collective-permute-start | bytes 786440 | tf_op jit(solution)/shard_map/ppermute | solution.py:366
  34.6 6.4 %collective-permute-start.12 = (bf16[512,256]{1,0:T(8,128)(2,1)S(1)}, bf16[512,256]{1,0:T(8,128)(2,1)S(1)}, u32[]{:S(2)}, u32[]{:S(2)}) collective-permute-start(bf16[512,256]{1,0:T(8,128)(2,1)S(1)} %shard_map.89.refs_0_), channel_id=1, source_target_pairs={{0,8},{1,2},{2,1},{3,4},{4,3},{5,6},{6,5},{7,15},{8,0},{9,10},{10,... | collective-permute-start | bytes 786440 | tf_op jit(solution)/shard_map/ppermute | solution.py:382
  44.2 1.2 %collective-permute-start.14 = (f32[8,128]{1,0:T(8,128)S(1)}, f32[8,128]{1,0:T(8,128)S(1)}, u32[]{:S(2)}, u32[]{:S(2)}) collective-permute-start(f32[8,128]{1,0:T(8,128)S(1)} %shard_map.92), channel_id=1, source_target_pairs={{0,1},{1,0},{2,3},{3,2},{4,5},{5,4},{6,7},{7,6},{8,9},{9,8},{10,11... | collective-permute-start | bytes 12296 | tf_op jit(solution)/shard_map/ppermute | solution.py:366
  45.4 5.4 %collective-permute-start.15 = (f32[2,8,128]{2,1,0:T(8,128)S(1)}, f32[2,8,128]{2,1,0:T(8,128)S(1)}, u32[]{:S(2)}, u32[]{:S(2)}) collective-permute-start(f32[2,8,128]{2,1,0:T(8,128)S(1)} %maximum_select_fusion.g0), channel_id=1, source_target_pairs={{0,6},{1,7},{2,4},{3,5},{4,2},{5,3},{6,0},{7,1},{8,14},{9,15},{10,... | collective-permute-start | bytes 24584 | tf_op jit(solution)/shard_map/ppermute | solution.py:369
  46.6 4.5 %collective-permute-start.16 = (f32[2,8,128]{2,1,0:T(8,128)S(1)}, f32[2,8,128]{2,1,0:T(8,128)S(1)}, u32[]{:S(2)}, u32[]{:S(2)}) collective-permute-start(f32[2,8,128]{2,1,0:T(8,128)S(1)} %maximum_select_fusion.g0), channel_id=1, source_target_pairs={{0,4},{1,5},{2,6},{3,7},{4,0},{5,1},{6,2},{7,3},{8,12},{9,13},{10,... | collective-permute-start | bytes 24584 | tf_op jit(solution)/shard_map/ppermute | solution.py:369
  46.7 4.7 %collective-permute-start.17 = (f32[2,8,128]{2,1,0:T(8,128)S(1)}, f32[2,8,128]{2,1,0:T(8,128)S(1)}, u32[]{:S(2)}, u32[]{:S(2)}) collective-permute-start(f32[2,8,128]{2,1,0:T(8,128)S(1)} %maximum_select_fusion.g0), channel_id=1, source_target_pairs={{0,2},{1,3},{2,0},{3,1},{4,6},{5,7},{6,4},{7,5},{8,10},{9,11},{10,... | collective-permute-start | bytes 24584 | tf_op jit(solution)/shard_map/ppermute | solution.py:369

commit v5 on v4

--- a/solution.py
+++ b/solution.py
@@ -320,18 +320,16 @@
         for b in range(CELLS // size)
     ]
     gain = halves[0][512:528, :].astype(F32)[1:2]
+    bias = jnp.concatenate([half[512:528, :].astype(F32)[0:1] for half in halves], 1)
+    weight_in = jnp.concatenate([half[0:256, :] for half in halves], 1)
+    weight_out = jnp.concatenate([half[256:512, :] for half in halves], 0)
     for n, total in enumerate(mixed):
         inverse = lax.rsqrt(jnp.mean(total * total, axis=-1, keepdims=True) + 1e-06)
         normed = (total * inverse * gain).astype(BF16)
-        parts = []
-        for half in halves:
-            bias = half[512:528, :].astype(F32)[0:1]
-            hidden = jnp.dot(normed, half[0:256, :], preferred_element_type=F32) + bias
-            inner = hidden * (0.7978845608028654 + 0.035677408136300125 * (hidden * hidden))
-            hidden = 0.5 * hidden
-            hidden = (hidden + hidden * jnp.tanh(inner)).astype(BF16)
-            parts.append(jnp.dot(hidden, half[256:512, :], preferred_element_type=F32))
-        total = (total + (parts[0] + parts[1])).astype(BF16)
+        hidden = jnp.dot(normed, weight_in, preferred_element_type=F32) + bias
+        inner = hidden * (0.7978845608028654 + 0.035677408136300125 * (hidden * hidden))
+        hidden = (hidden + hidden * jnp.tanh(inner)).astype(BF16)
+        total = (total + 0.5 * jnp.dot(hidden, weight_out, preferred_element_type=F32)).astype(BF16)
         out, b = outs[n // (CELLS // size)], n % (CELLS // size)
         if final:
             reader = jnp.broadcast_to(readout[...], (8, channels))

time: 52.4 us -> 51.8 us (0.989)
  Pallas kernels: 12.6 us -> 12 us
    pallas_call x4, Pallas kernels: 6.13 us -> 5.56 us  [run(): call(functools.partial(layer_kernel, layer, len(cells), final), outs, [VM...]
where the time goes in v5:
time: 51.8 us; the launch traced here: 51.6 us
  starting transfers between devices  22.9 us (44%)
  waiting for transfers between devices  16.4 us (32%)
  Pallas kernels  12 us (23%)
    ppermute x6, starting transfers between devices, chip(): return lax.ppermute(array, 'space', [(i, i ^ 2 * k) for i in range(spaces)])  8.84 us
    ppermute x6, waiting for transfers between devices, chip(): return lax.ppermute(array, 'space', [(i, i ^ 2 * k) for i in range(spaces)])  7.68 us
    pallas_call x4, Pallas kernels, run(): call(functools.partial(layer_kernel, layer, len(cells), final), outs, [VM...  5.56 us
    all_to_all x1, starting transfers between devices, window_on_section(): lax.all_to_all(packed, 'section', split_axis=0, concat_axis=0, tiled=True)  5.18 us
    ppermute x2, starting transfers between devices, beside(): return lax.ppermute(array, ('section', 'space'), pairs)  3.88 us
    ppermute x3, waiting for transfers between devices, section(): return lax.ppermute(array, 'section', [(i, i ^ k) for i in range(4)])  3.77 us
    ppermute x3, starting transfers between devices, section(): return lax.ppermute(array, 'section', [(i, i ^ k) for i in range(4)])  3.49 us
    pallas_call x3, Pallas kernels, prepare(): call(functools.partial(prepare_kernel, layers, spaces - 1), tuple(outs),...  3.26 us
  transfers between devices with their start and end apart: 19, of which 8 were waited for; matrix products, arithmetic and copies ran while one was open for 0% of the time, Pallas kernels for 12%

profile of v5, /device:TPU:0, one launch (start us, length us, event | category | flops | bytes accessed | tf_op | source)
XLA Modules:
  0.0 51.6 jit_solution(9767793582787327593)
XLA Ops:
  0.0 2.3 %shard_map.82 = (bf16[4,528,256]{2,1,0:T(8,128)(2,1)}, bf16[8,16,128]{2,1,0:T(8,128)(2,1)}) custom-call(bf16[1,15,4,128]{3,2,1,0:T(4,128)(2,1)} %row_coef.1, bf16[1,15,16,32]{3,2,1,0:T(8,128)(2,1)} %col_coef.1, bf16[1,256,512]{2,1,0:T(8,128)(2,1)} %weight_in.1, bf16[1,512,256]{2,1,0:T(8,128)(2,1)} %weight_out.1, bf16[1,512]{1,0:T(2,128)(2,1)} %bias.1, ...), custom_call_target="tpu_custom_call" | custom-call | flops 1 | bytes 1 | tf_op jit(solution)/shard_map/pallas_call | solution.py:384
  2.3 5.2 %all-to-all-start = ((bf16[4,528,256]{2,1,0:T(8,128)(2,1)}), bf16[4,528,256]{2,1,0:T(8,128)(2,1)S(1)}, u32[]{:S(2)}, u32[]{:S(2)}) async-start(bf16[4,528,256]{2,1,0:T(8,128)(2,1)} %get-tuple-element.43), calls=%async_computation | async-start | bytes 2162688 | tf_op jit(solution)/shard_map/all_to_all | solution.py:412
  7.5 0.1 collective-permute-start.1
  7.6 0.5 collective-permute-start
  8.1 1.1 %collective-permute-done.sib_taps = bf16[8,16,128]{2,1,0:T(8,128)(2,1)S(1)} collective-permute-done((bf16[8,16,128]{2,1,0:T(8,128)(2,1)S(1)}, bf16[8,16,128]{2,1,0:T(8,128)(2,1)S(1)}, u32[]{:S(2)}, u32[]{:S(2)}) %collective-permute-start) | collective-permute-done | bytes 32800 | tf_op jit(solution)/shard_map/ppermute | solution.py:364
  9.1 0.0 collective-permute-done.1.sib
  9.1 0.1 shard_map.83
  9.3 3.7 %collective-permute-start.2 = (bf16[160,256]{1,0:T(8,128)(2,1)S(1)}, bf16[160,256]{1,0:T(8,128)(2,1)S(1)}, u32[]{:S(2)}, u32[]{:S(2)}) collective-permute-start(bf16[160,256]{1,0:T(8,128)(2,1)S(1)} %get-tuple-element.35), channel_id=1, source_target_pairs={{0,6},{1,7},{2,4},{3,5},{4,2},{5,3},{6,0},{7,1},{8,14},{9,15},{10,... | collective-permute-start | bytes 245768 | tf_op jit(solution)/shard_map/ppermute | solution.py:367
  12.9 0.0 collective-permute-start.4
  12.9 0.8 %collective-permute-start.3 = (bf16[144,256]{1,0:T(8,128)(2,1)S(1)}, bf16[144,256]{1,0:T(8,128)(2,1)S(1)}, u32[]{:S(2)}, u32[]{:S(2)}) collective-permute-start(bf16[144,256]{1,0:T(8,128)(2,1)S(1)} %get-tuple-element.36), channel_id=1, source_target_pairs={{0,4},{1,5},{2,6},{3,7},{4,0},{5,1},{6,2},{7,3},{8,12},{9,13},{10,... | collective-permute-start | bytes 221192 | tf_op jit(solution)/shard_map/ppermute | solution.py:367
  13.7 6.0 %collective-permute-done.3.g2 = bf16[144,256]{1,0:T(8,128)(2,1)S(1)} collective-permute-done((bf16[144,256]{1,0:T(8,128)(2,1)S(1)}, bf16[144,256]{1,0:T(8,128)(2,1)S(1)}, u32[]{:S(2)}, u32[]{:S(2)}) %collective-permute-start.3) | collective-permute-done | bytes 73760 | tf_op jit(solution)/shard_map/ppermute | solution.py:367
  19.8 0.0 collective-permute-done.2.g3
  19.8 0.0 collective-permute-done.4.g1
  19.8 0.1 collective-permute-start.5
  19.9 2.1 %collective-permute-start.6 = (bf16[512,256]{1,0:T(8,128)(2,1)S(1)}, bf16[512,256]{1,0:T(8,128)(2,1)S(1)}, u32[]{:S(2)}, u32[]{:S(2)}) collective-permute-start(bf16[512,256]{1,0:T(8,128)(2,1)S(1)} %shard_map.85.refs_0_), channel_id=1, source_target_pairs={{0,8},{1,2},{2,1},{3,4},{4,3},{5,6},{6,5},{7,15},{8,0},{9,10},{10,... | collective-permute-start | bytes 786440 | tf_op jit(solution)/shard_map/ppermute | solution.py:380
  22.0 1.5 %collective-permute-start.7 = (bf16[128,256]{1,0:T(8,128)(2,1)S(1)}, bf16[128,256]{1,0:T(8,128)(2,1)S(1)}, u32[]{:S(2)}, u32[]{:S(2)}) collective-permute-start(bf16[128,256]{1,0:T(8,128)(2,1)S(1)} %shard_map.84.q0), channel_id=1, source_target_pairs={{0,24},{8,16},{16,8},{24,0},{1,25},{9,17},{17,9},{25,1},{2,26},{10... | collective-permute-start | bytes 196616 | tf_op jit(solution)/shard_map/ppermute | solution.py:370
  23.5 0.1 collective-permute-start.8
  23.6 1.9 %collective-permute-start.9 = (bf16[128,256]{1,0:T(8,128)(2,1)S(1)}, bf16[128,256]{1,0:T(8,128)(2,1)S(1)}, u32[]{:S(2)}, u32[]{:S(2)}) collective-permute-start(bf16[128,256]{1,0:T(8,128)(2,1)S(1)} %shard_map.84.q0), channel_id=1, source_target_pairs={{0,8},{8,0},{16,24},{24,16},{1,9},{9,1},{17,25},{25,17},{2,10},{10... | collective-permute-start | bytes 196616 | tf_op jit(solution)/shard_map/ppermute | solution.py:370
  25.5 0.0 all-to-all-done.refs_6_.refs_4_.refs_5_
  25.5 0.1 fusion
  25.6 3.8 %collective-permute-done.7.q3 = bf16[128,256]{1,0:T(8,128)(2,1)S(1)} collective-permute-done((bf16[128,256]{1,0:T(8,128)(2,1)S(1)}, bf16[128,256]{1,0:T(8,128)(2,1)S(1)}, u32[]{:S(2)}, u32[]{:S(2)}) %collective-permute-start.7) | collective-permute-done | bytes 65568 | tf_op jit(solution)/shard_map/ppermute | solution.py:370
  29.3 0.0 collective-permute-done.8.q2
  29.3 0.0 collective-permute-done.9.q1
  29.3 0.0 collective-permute-done.5.refs_1_
  29.4 0.0 collective-permute-done.6.refs_2_
  29.4 0.1 collective-permute-start.10
  29.4 0.5 collective-permute-start.13
  29.9 1.0 %shard_map.86 = (bf16[512,512]{1,0:T(8,128)(2,1)S(1)}, bf16[512,512]{1,0:T(8,128)(2,1)S(1)}, bf16[4,256,384]{2,1,0:T(8,128)(2,1)S(1)}) custom-call(bf16[128,256]{1,0:T(8,128)(2,1)S(1)} %shard_map.84.q0, bf16[128,256]{1,0:T(8,128)(2,1)S(1)} %collective-permute-done.7.q3, bf16[128,256]{1,0:T(8,128)(2,1)S(1)} %collective-permute-done.8.q2, ...), custom_call_target="tpu_custom_call" | custom-call | flops 1 | bytes 1 | tf_op jit(solution)/shard_map/pallas_call | solution.py:429
  30.9 0.6 %shard_map.88 = (bf16[512,512]{1,0:T(8,128)(2,1)S(1)}, bf16[4,128,256]{2,1,0:T(8,128)(2,1)S(1)}) custom-call(bf16[128,256]{1,0:T(8,128)(2,1)S(1)} %shard_map.84.q0, bf16[128,256]{1,0:T(8,128)(2,1)S(1)} %collective-permute-done.7.q3, bf16[128,256]{1,0:T(8,128)(2,1)S(1)} %collective-permute-done.8.q2, bf16[128,256]{1,0:T(8,128)(2,1)S(1)} %collective-permute-done.9.q1), custom_call_target="tpu_custom_call" | custom-call | flops 1 | bytes 1 | tf_op jit(solution)/shard_map/pallas_call | solution.py:429
  31.5 0.0 collective-permute-done.10.refs_7_.refs_5_
  31.5 1.7 %shard_map.87 = (bf16[512,256]{1,0:T(8,128)(2,1)S(1)}, bf16[512,256]{1,0:T(8,128)(2,1)S(1)}) custom-call(bf16[512,256]{1,0:T(8,128)(2,1)S(1)} %shard_map.85.refs_0_, bf16[512,256]{1,0:T(8,128)(2,1)S(1)} %collective-permute-done.5.refs_1_, bf16[512,256]{1,0:T(8,128)(2,1)S(1)} %collective-permute-done.6.refs_2_, ...), custom_call_target="tpu_custom_call" | custom-call | flops 1 | bytes 1 | tf_op jit(solution)/shard_map/pallas_call | solution.py:440
  33.2 0.0 copy-start.2
  33.2 1.0 %shard_map.89.refs_0_ = bf16[512,256]{1,0:T(8,128)(2,1)S(1)} custom-call(bf16[512,256]{1,0:T(8,128)(2,1)S(1)} %get-tuple-element.45.refs_0_, bf16[512,256]{1,0:T(8,128)(2,1)S(1)} %get-tuple-element.46.refs_1_, bf16[4,128,256]{2,1,0:T(8,128)(2,1)S(1)} %get-tuple-element.47.refs_2_, bf16[512,512]{1,0:T(8,128)(2,1)S(1)} %get-tuple-element.48.refs_3_, ...), custom_call_target="tpu_custom_call" | custom-call | flops 1 | bytes 1 | tf_op jit(solution)/shard_map/pallas_call | solution.py:440
  34.2 0.1 collective-permute-start.11
  34.4 1.8 %collective-permute-start.12 = (bf16[512,256]{1,0:T(8,128)(2,1)S(1)}, bf16[512,256]{1,0:T(8,128)(2,1)S(1)}, u32[]{:S(2)}, u32[]{:S(2)}) collective-permute-start(bf16[512,256]{1,0:T(8,128)(2,1)S(1)} %shard_map.89.refs_0_), channel_id=1, source_target_pairs={{0,8},{1,2},{2,1},{3,4},{4,3},{5,6},{6,5},{7,15},{8,0},{9,10},{10,... | collective-permute-start | bytes 786440 | tf_op jit(solution)/shard_map/ppermute | solution.py:380
  36.2 1.7 %shard_map.90 = (bf16[512,512]{1,0:T(8,128)(2,1)S(1)}, bf16[512,512]{1,0:T(8,128)(2,1)S(1)}, bf16[4,256,384]{2,1,0:T(8,128)(2,1)S(1)}, bf16[512,512]{1,0:T(8,128)(2,1)S(1)}, bf16[4,128,256]{2,1,0:T(8,128)(2,1)S(1)}) custom-call(bf16[128,256]{1,0:T(8,128)(2,1)S(1)} %shard_map.84.q0, bf16[128,256]{1,0:T(8,128)(2,1)S(1)} %collective-permute-done.7.q3, ...), custom_call_target="tpu_custom_call" | custom-call | flops 1 | bytes 1 | tf_op jit(solution)/shard_map/pallas_call | solution.py:429
  37.9 2.8 %collective-permute-done.12.refs_2_ = bf16[512,256]{1,0:T(8,128)(2,1)S(1)} collective-permute-done((bf16[512,256]{1,0:T(8,128)(2,1)S(1)}, bf16[512,256]{1,0:T(8,128)(2,1)S(1)}, u32[]{:S(2)}, u32[]{:S(2)}) %collective-permute-start.12) | collective-permute-done | bytes 262176 | tf_op jit(solution)/shard_map/ppermute | solution.py:380
  40.7 1.6 %shard_map.91 = (bf16[512,256]{1,0:T(8,128)(2,1)S(1)}, bf16[512,256]{1,0:T(8,128)(2,1)S(1)}) custom-call(bf16[512,256]{1,0:T(8,128)(2,1)S(1)} %shard_map.89.refs_0_, bf16[512,256]{1,0:T(8,128)(2,1)S(1)} %collective-permute-done.11.refs_1_, bf16[512,256]{1,0:T(8,128)(2,1)S(1)} %collective-permute-done.12.refs_2_, ...), custom_call_target="tpu_custom_call" | custom-call | flops 1 | bytes 1 | tf_op jit(solution)/shard_map/pallas_call | solution.py:440
  42.4 1.2 %shard_map.92 = f32[8,128]{1,0:T(8,128)S(1)} custom-call(bf16[512,256]{1,0:T(8,128)(2,1)S(1)} %get-tuple-element.57.refs_0_, bf16[512,256]{1,0:T(8,128)(2,1)S(1)} %get-tuple-element.58.refs_1_, bf16[4,128,256]{2,1,0:T(8,128)(2,1)S(1)} %get-tuple-element.59.refs_2_, bf16[512,512]{1,0:T(8,128)(2,1)S(1)} %get-tuple-element.60.refs_3_, ...), custom_call_target="tpu_custom_call" | custom-call | flops 1 | bytes 1 | tf_op jit(solution)/shard_map/pallas_call | solution.py:440
  43.6 0.1 collective-permute-start.14
  43.8 1.0 %collective-permute-done.14 = f32[8,128]{1,0:T(8,128)S(1)} collective-permute-done((f32[8,128]{1,0:T(8,128)S(1)}, f32[8,128]{1,0:T(8,128)S(1)}, u32[]{:S(2)}, u32[]{:S(2)}) %collective-permute-start.14) | collective-permute-done | bytes 4128 | tf_op jit(solution)/shard_map/ppermute | solution.py:364
  44.8 1.2 %collective-permute-start.15 = (f32[2,8,128]{2,1,0:T(8,128)S(1)}, f32[2,8,128]{2,1,0:T(8,128)S(1)}, u32[]{:S(2)}, u32[]{:S(2)}) collective-permute-start(f32[2,8,128]{2,1,0:T(8,128)S(1)} %maximum_select_fusion.g0), channel_id=1, source_target_pairs={{0,6},{1,7},{2,4},{3,5},{4,2},{5,3},{6,0},{7,1},{8,14},{9,15},{10,... | collective-permute-start | bytes 24584 | tf_op jit(solution)/shard_map/ppermute | solution.py:367
  46.0 0.1 collective-permute-start.16
  46.2 3.0 %collective-permute-start.17 = (f32[2,8,128]{2,1,0:T(8,128)S(1)}, f32[2,8,128]{2,1,0:T(8,128)S(1)}, u32[]{:S(2)}, u32[]{:S(2)}) collective-permute-start(f32[2,8,128]{2,1,0:T(8,128)S(1)} %maximum_select_fusion.g0), channel_id=1, source_target_pairs={{0,2},{1,3},{2,0},{3,1},{4,6},{5,7},{6,4},{7,5},{8,10},{9,11},{10,... | collective-permute-start | bytes 24584 | tf_op jit(solution)/shard_map/ppermute | solution.py:367
  49.2 1.1 %collective-permute-done.15.g3 = f32[2,8,128]{2,1,0:T(8,128)S(1)} collective-permute-done((f32[2,8,128]{2,1,0:T(8,128)S(1)}, f32[2,8,128]{2,1,0:T(8,128)S(1)}, u32[]{:S(2)}, u32[]{:S(2)}) %collective-permute-start.15) | collective-permute-done | bytes 8224 | tf_op jit(solution)/shard_map/ppermute | solution.py:367
  50.3 0.3 collective-permute-done.16.g2
  50.6 0.3 collective-permute-done.17.g1
  50.8 0.7 %shard_map.93 = f32[1,4,128]{2,1,0:T(4,128)} custom-call(f32[2,8,128]{2,1,0:T(8,128)S(1)} %maximum_select_fusion.g0, f32[2,8,128]{2,1,0:T(8,128)S(1)} %collective-permute-done.15.g3, f32[2,8,128]{2,1,0:T(8,128)S(1)} %collective-permute-done.16.g2, f32[2,8,128]{2,1,0:T(8,128)S(1)} %collective-permute-done.17.g1), custom_call_target="tpu_custom_call" | custom-call | flops 1 | bytes 1 | tf_op jit(solution)/shard_map/pallas_call | solution.py:458
  (12 shorter events, 0.1 us)
Async XLA Ops:
  0.0 7.5 %copy-start = (bf16[4,4,128,256]{3,2,1,0:T(8,128)(2,1)S(1)}, bf16[4,4,128,256]{3,2,1,0:T(8,128)(2,1)}, u32[]{:S(2)}) copy-start(bf16[4,4,128,256]{3,2,1,0:T(8,128)(2,1)} %param.8) | copy-start | bytes 3145732
  2.3 5.3 %copy-start.1 = (bf16[8,16,128]{2,1,0:T(8,128)(2,1)S(1)}, bf16[8,16,128]{2,1,0:T(8,128)(2,1)}, u32[]{:S(2)}) copy-start(bf16[8,16,128]{2,1,0:T(8,128)(2,1)} %get-tuple-element.33.own_taps) | copy-start | bytes 98308
  2.3 23.2 %all-to-all-start = ((bf16[4,528,256]{2,1,0:T(8,128)(2,1)}), bf16[4,528,256]{2,1,0:T(8,128)(2,1)S(1)}, u32[]{:S(2)}, u32[]{:S(2)}) async-start(bf16[4,528,256]{2,1,0:T(8,128)(2,1)} %get-tuple-element.43), calls=%async_computation | async-start | bytes 2162688 | tf_op jit(solution)/shard_map/all_to_all | solution.py:412
  7.5 1.7 %collective-permute-start.1 = (bf16[4,128,256]{2,1,0:T(8,128)(2,1)S(1)}, bf16[4,128,256]{2,1,0:T(8,128)(2,1)S(1)}, u32[]{:S(2)}, u32[]{:S(2)}) collective-permute-start(bf16[4,128,256]{2,1,0:T(8,128)(2,1)S(1)} %dynamic-slice_bitcast_fusion.own), channel_id=1, source_target_pairs={{0,1},{1,0},{2,3},{3,2},{4,5},{5,4},{6,7},{7,6},{8,9},{9,8},{10,11... | collective-permute-start | bytes 786440 | tf_op jit(solution)/shard_map/ppermute | solution.py:364
  7.6 1.6 %collective-permute-start = (bf16[8,16,128]{2,1,0:T(8,128)(2,1)S(1)}, bf16[8,16,128]{2,1,0:T(8,128)(2,1)S(1)}, u32[]{:S(2)}, u32[]{:S(2)}) collective-permute-start(bf16[8,16,128]{2,1,0:T(8,128)(2,1)S(1)} %copy-done.1), channel_id=1, source_target_pairs={{0,1},{1,0},{2,3},{3,2},{4,5},{5,4},{6,7},{7,6},{8,9},{9,8},{10,11... | collective-permute-start | bytes 98312 | tf_op jit(solution)/shard_map/ppermute | solution.py:364
  9.3 10.5 %collective-permute-start.2 = (bf16[160,256]{1,0:T(8,128)(2,1)S(1)}, bf16[160,256]{1,0:T(8,128)(2,1)S(1)}, u32[]{:S(2)}, u32[]{:S(2)}) collective-permute-start(bf16[160,256]{1,0:T(8,128)(2,1)S(1)} %get-tuple-element.35), channel_id=1, source_target_pairs={{0,6},{1,7},{2,4},{3,5},{4,2},{5,3},{6,0},{7,1},{8,14},{9,15},{10,... | collective-permute-start | bytes 245768 | tf_op jit(solution)/shard_map/ppermute | solution.py:367
  12.9 6.8 %collective-permute-start.4 = (bf16[160,256]{1,0:T(8,128)(2,1)S(1)}, bf16[160,256]{1,0:T(8,128)(2,1)S(1)}, u32[]{:S(2)}, u32[]{:S(2)}) collective-permute-start(bf16[160,256]{1,0:T(8,128)(2,1)S(1)} %get-tuple-element.37), channel_id=1, source_target_pairs={{0,2},{1,3},{2,0},{3,1},{4,6},{5,7},{6,4},{7,5},{8,10},{9,11},{10,... | collective-permute-start | bytes 245768 | tf_op jit(solution)/shard_map/ppermute | solution.py:367
  12.9 6.8 %collective-permute-start.3 = (bf16[144,256]{1,0:T(8,128)(2,1)S(1)}, bf16[144,256]{1,0:T(8,128)(2,1)S(1)}, u32[]{:S(2)}, u32[]{:S(2)}) collective-permute-start(bf16[144,256]{1,0:T(8,128)(2,1)S(1)} %get-tuple-element.36), channel_id=1, source_target_pairs={{0,4},{1,5},{2,6},{3,7},{4,0},{5,1},{6,2},{7,3},{8,12},{9,13},{10,... | collective-permute-start | bytes 221192 | tf_op jit(solution)/shard_map/ppermute | solution.py:367
  19.8 9.5 %collective-permute-start.5 = (bf16[512,256]{1,0:T(8,128)(2,1)S(1)}, bf16[512,256]{1,0:T(8,128)(2,1)S(1)}, u32[]{:S(2)}, u32[]{:S(2)}) collective-permute-start(bf16[512,256]{1,0:T(8,128)(2,1)S(1)} %shard_map.85.refs_0_), channel_id=1, source_target_pairs={{0,1},{1,0},{2,3},{3,2},{4,5},{5,4},{6,7},{7,6},{8,9},{9,8},{10,11... | collective-permute-start | bytes 786440 | tf_op jit(solution)/shard_map/ppermute | solution.py:364
  19.9 9.4 %collective-permute-start.6 = (bf16[512,256]{1,0:T(8,128)(2,1)S(1)}, bf16[512,256]{1,0:T(8,128)(2,1)S(1)}, u32[]{:S(2)}, u32[]{:S(2)}) collective-permute-start(bf16[512,256]{1,0:T(8,128)(2,1)S(1)} %shard_map.85.refs_0_), channel_id=1, source_target_pairs={{0,8},{1,2},{2,1},{3,4},{4,3},{5,6},{6,5},{7,15},{8,0},{9,10},{10,... | collective-permute-start | bytes 786440 | tf_op jit(solution)/shard_map/ppermute | solution.py:380
  22.0 7.3 %collective-permute-start.7 = (bf16[128,256]{1,0:T(8,128)(2,1)S(1)}, bf16[128,256]{1,0:T(8,128)(2,1)S(1)}, u32[]{:S(2)}, u32[]{:S(2)}) collective-permute-start(bf16[128,256]{1,0:T(8,128)(2,1)S(1)} %shard_map.84.q0), channel_id=1, source_target_pairs={{0,24},{8,16},{16,8},{24,0},{1,25},{9,17},{17,9},{25,1},{2,26},{10... | collective-permute-start | bytes 196616 | tf_op jit(solution)/shard_map/ppermute | solution.py:370
  23.5 5.9 %collective-permute-start.8 = (bf16[128,256]{1,0:T(8,128)(2,1)S(1)}, bf16[128,256]{1,0:T(8,128)(2,1)S(1)}, u32[]{:S(2)}, u32[]{:S(2)}) collective-permute-start(bf16[128,256]{1,0:T(8,128)(2,1)S(1)} %shard_map.84.q0), channel_id=1, source_target_pairs={{0,16},{8,24},{16,0},{24,8},{1,17},{9,25},{17,1},{25,9},{2,18},{10... | collective-permute-start | bytes 196616 | tf_op jit(solution)/shard_map/ppermute | solution.py:370
  23.6 5.8 %collective-permute-start.9 = (bf16[128,256]{1,0:T(8,128)(2,1)S(1)}, bf16[128,256]{1,0:T(8,128)(2,1)S(1)}, u32[]{:S(2)}, u32[]{:S(2)}) collective-permute-start(bf16[128,256]{1,0:T(8,128)(2,1)S(1)} %shard_map.84.q0), channel_id=1, source_target_pairs={{0,8},{8,0},{16,24},{24,16},{1,9},{9,1},{17,25},{25,17},{2,10},{10... | collective-permute-start | bytes 196616 | tf_op jit(solution)/shard_map/ppermute | solution.py:370
  29.4 2.1 %collective-permute-start.10 = (bf16[2,528,256]{2,1,0:T(8,128)(2,1)S(1)}, bf16[2,528,256]{2,1,0:T(8,128)(2,1)S(1)}, u32[]{:S(2)}, u32[]{:S(2)}) collective-permute-start(bf16[2,528,256]{2,1,0:T(8,128)(2,1)S(1)} %get-tuple-element.44), channel_id=1, source_target_pairs={{0,1},{1,0},{2,3},{3,2},{4,5},{5,4},{6,7},{7,6},{8,9},{9,8},{10,11... | collective-permute-start | bytes 1622024 | tf_op jit(solution)/shard_map/ppermute | solution.py:364
  29.4 8.4 %collective-permute-start.13 = (bf16[2,528,256]{2,1,0:T(8,128)(2,1)S(1)}, bf16[2,528,256]{2,1,0:T(8,128)(2,1)S(1)}, u32[]{:S(2)}, u32[]{:S(2)}) collective-permute-start(bf16[2,528,256]{2,1,0:T(8,128)(2,1)S(1)} %get-tuple-element.56), channel_id=1, source_target_pairs={{0,1},{1,0},{2,3},{3,2},{4,5},{5,4},{6,7},{7,6},{8,9},{9,8},{10,11... | collective-permute-start | bytes 1622024 | tf_op jit(solution)/shard_map/ppermute | solution.py:364
  33.2 3.0 %copy-start.2 = (bf16[256]{0:T(256)(128)(2,1)S(1)}, bf16[256]{0:T(256)(128)(2,1)}, u32[]{:S(2)}) copy-start(bf16[256]{0:T(256)(128)(2,1)} %param.15) | copy-start | bytes 1540
  34.2 3.7 %collective-permute-start.11 = (bf16[512,256]{1,0:T(8,128)(2,1)S(1)}, bf16[512,256]{1,0:T(8,128)(2,1)S(1)}, u32[]{:S(2)}, u32[]{:S(2)}) collective-permute-start(bf16[512,256]{1,0:T(8,128)(2,1)S(1)} %shard_map.89.refs_0_), channel_id=1, source_target_pairs={{0,1},{1,0},{2,3},{3,2},{4,5},{5,4},{6,7},{7,6},{8,9},{9,8},{10,11... | collective-permute-start | bytes 786440 | tf_op jit(solution)/shard_map/ppermute | solution.py:364
  34.4 6.4 %collective-permute-start.12 = (bf16[512,256]{1,0:T(8,128)(2,1)S(1)}, bf16[512,256]{1,0:T(8,128)(2,1)S(1)}, u32[]{:S(2)}, u32[]{:S(2)}) collective-permute-start(bf16[512,256]{1,0:T(8,128)(2,1)S(1)} %shard_map.89.refs_0_), channel_id=1, source_target_pairs={{0,8},{1,2},{2,1},{3,4},{4,3},{5,6},{6,5},{7,15},{8,0},{9,10},{10,... | collective-permute-start | bytes 786440 | tf_op jit(solution)/shard_map/ppermute | solution.py:380
  43.6 1.2 %collective-permute-start.14 = (f32[8,128]{1,0:T(8,128)S(1)}, f32[8,128]{1,0:T(8,128)S(1)}, u32[]{:S(2)}, u32[]{:S(2)}) collective-permute-start(f32[8,128]{1,0:T(8,128)S(1)} %shard_map.92), channel_id=1, source_target_pairs={{0,1},{1,0},{2,3},{3,2},{4,5},{5,4},{6,7},{7,6},{8,9},{9,8},{10,11... | collective-permute-start | bytes 12296 | tf_op jit(solution)/shard_map/ppermute | solution.py:364
  44.8 5.4 %collective-permute-start.15 = (f32[2,8,128]{2,1,0:T(8,128)S(1)}, f32[2,8,128]{2,1,0:T(8,128)S(1)}, u32[]{:S(2)}, u32[]{:S(2)}) collective-permute-start(f32[2,8,128]{2,1,0:T(8,128)S(1)} %maximum_select_fusion.g0), channel_id=1, source_target_pairs={{0,6},{1,7},{2,4},{3,5},{4,2},{5,3},{6,0},{7,1},{8,14},{9,15},{10,... | collective-permute-start | bytes 24584 | tf_op jit(solution)/shard_map/ppermute | solution.py:367
  46.0 4.5 %collective-permute-start.16 = (f32[2,8,128]{2,1,0:T(8,128)S(1)}, f32[2,8,128]{2,1,0:T(8,128)S(1)}, u32[]{:S(2)}, u32[]{:S(2)}) collective-permute-start(f32[2,8,128]{2,1,0:T(8,128)S(1)} %maximum_select_fusion.g0), channel_id=1, source_target_pairs={{0,4},{1,5},{2,6},{3,7},{4,0},{5,1},{6,2},{7,3},{8,12},{9,13},{10,... | collective-permute-start | bytes 24584 | tf_op jit(solution)/shard_map/ppermute | solution.py:367
  46.2 4.7 %collective-permute-start.17 = (f32[2,8,128]{2,1,0:T(8,128)S(1)}, f32[2,8,128]{2,1,0:T(8,128)S(1)}, u32[]{:S(2)}, u32[]{:S(2)}) collective-permute-start(f32[2,8,128]{2,1,0:T(8,128)S(1)} %maximum_select_fusion.g0), channel_id=1, source_target_pairs={{0,2},{1,3},{2,0},{3,1},{4,6},{5,7},{6,4},{7,5},{8,10},{9,11},{10,... | collective-permute-start | bytes 24584 | tf_op jit(solution)/shard_map/ppermute | solution.py:367

commit v6 on v5

--- a/solution.py
+++ b/solution.py
@@ -157,27 +157,26 @@
     ]
     for copy in copies:
         copy.start()
-    for copy in copies[2:4]:
+    for copy in copies[:4]:
         copy.wait()
     line = iota((16, 256), 0)
     part = jnp.where(c == 0, biases[:, 0:256].astype(F32), biases[:, 256:512].astype(F32))
     tail = jnp.where(line == 0, part, jnp.where(line == 1, gains[...].astype(F32), 0.0))
     half[512:528, :] = tail.astype(BF16)
-    for copy in copies[4:]:
-        copy.wait()
-    sends = [pltpu.make_async_copy(half, out.at[n], leave.at[n]) for n in range(4)]
-    for copy in sends:
-        copy.start()
-    for copy in copies[:2]:
-        copy.wait()
     zero = jnp.zeros((1, WIDE), F32)
     row, col = rows[...].astype(F32), cols[...].astype(F32)
     for m in range(4):
         taps[m] = jnp.concatenate([row[:, m, :], zero], 0).astype(BF16)
         group = jnp.concatenate([col[:, 4 * m + j, :] for j in range(4)], 1)
-        taps[4 + m] = jnp.concatenate([group, zero], 0).astype(BF16)
+        group = jnp.concatenate([group, zero], 0).astype(BF16)
+        taps[4 + m] = group
+        half[528 + 16 * (m // 2) : 544 + 16 * (m // 2), WIDE * (m % 2) : WIDE * (m % 2 + 1)] = group
+    for copy in copies[4:]:
+        copy.wait()
+    sends = [pltpu.make_async_copy(half, out.at[n], leave.at[n]) for n in range(4)]
     sends.append(pltpu.make_async_copy(taps, own, leave.at[4]))
-    sends[-1].start()
+    for copy in sends:
+        copy.start()
     for copy in sends:
         copy.wait()
 
@@ -201,18 +200,17 @@
         out[...] = chunk[z ^ k, 0 : out.shape[0], :]
 
 
-def tables_kernel(g0, g3, g2, g1, own_taps, sib_taps, taps, edges):
+def tables_kernel(g0, g3, g2, g1, sib_taps, taps, edges):
     _, c, z, _ = position()
     for k, g in enumerate((g0, g1, g2, g3)):
         taps[16 * k : 16 * (k + 1), :] = g[GROUP : GROUP + 16, :]
         if k != 2:
             edges[z ^ k] = g[GROUP + 16 : GROUP + 32, :]
-    edge = edges[(z + 3 + 2 * c) % 4]
-    for m in range(4):
-        core, chip = sib_taps[4 + (m + 2) % 4], edge[:, WIDE * (m % 2) : WIDE * (m % 2 + 1)]
-        margin = jnp.where(c == 0, chip, core) if m < 2 else jnp.where(c == 0, core, chip)
-        taps[64 + 16 * m : 80 + 16 * m, 0:WIDE] = own_taps[4 + m]
-        taps[64 + 16 * m : 80 + 16 * m, WIDE : 2 * WIDE] = margin
+    chip = edges[(z + 3 + 2 * c) % 4]
+    for n in range(2):
+        core = jnp.concatenate([sib_taps[4 + (2 * n + m + 2) % 4] for m in range(2)], 1)
+        left = c == n
+        taps[64 + 16 * n : 80 + 16 * n, :] = jnp.where(left, chip, core)
 
 
 def field_kernel(g0, g3, g2, g1, field):
@@ -221,31 +219,39 @@
         field[pl.ds(pl.multiple_of((z ^ k) * GROUP, GROUP), GROUP), :] = g[0:GROUP, :]
 
 
-def prepare_kernel(layers, last, q0, q3, q2, q1, *rest):
-    s, c, z, p = position()
-    outs, (turned, ordered, parts) = list(rest[:-3]), rest[-3:]
-
+def columns(groups, out, turned, ordered):
     tap_in, tap_out = iota((WIDE, 256), 0), iota((WIDE, 256), 1)
     expand = jnp.where((tap_in == tap_out // COLS) & (tap_in < TAPS), 1.0, 0.0).astype(BF16)
     lane, line = iota((COLS, 256), 1), iota((COLS, 256), 0)
     same = line == lane % COLS
-
-    def columns(table, out):
-        for m in range(4):
-            turned[128 * m : 128 * (m + 1), :] = jnp.concatenate(
-                [jnp.transpose(table[16 * m : 16 * (m + 1)]), jnp.zeros((128, WIDE - 16), F32)], 1
-            )
-        for i in range(ROWS):
-            ordered[COLS * i : COLS * (i + 1), :] = turned[pl.ds(i, COLS, stride=ROWS), :]
-        wide = jnp.dot(ordered[...].astype(BF16), expand, preferred_element_type=F32)
-        for i in range(ROWS):
-            row = i + lane // COLS - RADIUS
-            block = jnp.where(same & (row >= 0) & (row < ROWS), wide[COLS * i : COLS * (i + 1)], 0.0)
-            block = jnp.concatenate([block, jnp.zeros((COLS, CELLS - 256), F32)], 1)
-            shift = (COLS * (i - RADIUS)) % CELLS
-            if shift:
-                block = pltpu.roll(block, shift, 1)
-            out[COLS * i : COLS * (i + 1), :] = block.astype(BF16)
+    for m, group in enumerate(groups):
+        turned[128 * m : 128 * (m + 1), :] = jnp.concatenate(
+            [jnp.transpose(group), jnp.zeros((128, WIDE - 16), F32)], 1
+        )
+    for i in range(ROWS):
+        ordered[COLS * i : COLS * (i + 1), :] = turned[pl.ds(i, COLS, stride=ROWS), :]
+    wide = jnp.dot(ordered[...].astype(BF16), expand, preferred_element_type=F32)
+    for i in range(ROWS):
+        row = i + lane // COLS - RADIUS
+        block = jnp.where(same & (row >= 0) & (row < ROWS), wide[COLS * i : COLS * (i + 1)], 0.0)
+        block = jnp.concatenate([block, jnp.zeros((COLS, CELLS - 256), F32)], 1)
+        shift = (COLS * (i - RADIUS)) % CELLS
+        if shift:
+            block = pltpu.roll(block, shift, 1)
+        out[COLS * i : COLS * (i + 1), :] = block.astype(BF16)
+
+
+def own_columns_kernel(layers, weights, *rest):
+    outs, scratch = rest[:-2], rest[-2:]
+    for layer, out in zip(layers, outs):
+        table = weights[layer, 528:560, :].astype(F32)
+        groups = [table[16 * n : 16 * (n + 1), WIDE * m : WIDE * (m + 1)] for n in range(2) for m in range(2)]
+        columns(groups, out, *scratch)
+
+
+def prepare_kernel(layers, last, q0, q3, q2, q1, *rest):
+    s, c, z, p = position()
+    outs, (turned, ordered, parts) = list(rest[:-3]), rest[-3:]
 
     lane2, line2 = iota((GROUP, WIDE), 1), iota((GROUP, WIDE), 0)
     tap = (lane2 - line2 + RADIUS + WIDE) % WIDE
@@ -269,9 +275,10 @@
 
     for layer in layers:
         table = picked(s ^ layer, [q[...].astype(F32) for q in (q0, q1, q2, q3)])
-        columns(table[64:128, 0:WIDE], outs.pop(0))
         if layer % 2 == 0:
-            columns(table[64:128, WIDE : 2 * WIDE], outs.pop(0))
+            margin = table[64:96]
+            groups = [margin[16 * n : 16 * (n + 1), WIDE * m : WIDE * (m + 1)] for n in range(2) for m in range(2)]
+            columns(groups, outs.pop(0), turned, ordered)
         out = outs.pop(0)
         for k in range(4):
             parts[z ^ k] = table[16 * k : 16 * (k + 1)]
@@ -383,14 +390,14 @@
     window_sib = core(window)
     packed, own = call(
         stage_kernel,
-        (shaped((4, 528, 256)), shaped((8, 16, WIDE))),
+        (shaped((4, 560, 256)), shaped((8, 16, WIDE))),
         [ANY] * 6,
         [
             pltpu.VMEM(row_coef.shape[1:], BF16),
             pltpu.VMEM(col_coef.shape[1:], BF16),
             pltpu.VMEM((1, 512), BF16),
             pltpu.VMEM((1, 256), BF16),
-            pltpu.VMEM((528, 256), BF16),
+            pltpu.VMEM((560, 256), BF16),
             pltpu.VMEM((8, 16, WIDE), BF16),
             pltpu.SemaphoreType.DMA((6,)),
             pltpu.SemaphoreType.DMA((5,)),
@@ -412,19 +419,17 @@
     mine = lax.all_to_all(packed, "section", split_axis=0, concat_axis=0, tiled=True)
 
     taps = call(
-        tables_kernel, shaped((WIDE, 256)), [VMEM] * 6, [pltpu.VMEM((4, 16, 256), BF16)]
-    )(chunks[0], *chunks[:0:-1], own, sib)
+        tables_kernel, shaped((96, 256)), [VMEM] * 5, [pltpu.VMEM((4, 16, 256), BF16)]
+    )(chunks[0], *chunks[:0:-1], sib)
     field = call(field_kernel, shaped((CELLS, channels)), [VMEM] * 4)(after(chunks[0], taps), *chunks[:0:-1])
     field_core, field_chip = core(field), beside(field)
     tables = [section(taps, k) for k in (3, 2, 1)]
     tables = [taps] + tables[::-1]
-    theirs = [core(after(m, *tables[::-1], field_core, field_chip)) for m in (mine[:2], mine[2:])]
-
     def prepare(layers, tables):
         outs = []
         for layer in layers:
             even = layer % 2 == 0
-            outs += [shaped((CELLS, CELLS))] * (1 + even)
+            outs += [shaped((CELLS, CELLS))] * even
             outs.append(shaped((4, 2 * GROUP, 3 * WIDE) if even else (4, GROUP, 2 * WIDE)))
         return call(
             functools.partial(prepare_kernel, layers, spaces - 1),
@@ -432,6 +437,14 @@
             [VMEM] * 4,
             [pltpu.VMEM((CELLS, WIDE), F32), pltpu.VMEM((CELLS, WIDE), F32), pltpu.VMEM((4, 16, 256), F32)],
         )(tables[0], *tables[:0:-1])
+
+    def own_columns(layers, weights):
+        return call(
+            functools.partial(own_columns_kernel, layers),
+            (shaped((CELLS, CELLS)),) * len(layers),
+            [VMEM],
+            [pltpu.VMEM((CELLS, WIDE), F32), pltpu.VMEM((CELLS, WIDE), F32)],
+        )(weights)
 
     def run(layer, cells, bands, readers=()):
         wide = len(cells) == 3
@@ -444,13 +457,19 @@
             [pltpu.VMEM((CELLS, channels), BF16)] * (1 + wide),
         )(*cells, bands[-1], *bands[:-1], *readers, mine, theirs[layer // 2])
 
-    bands0 = prepare((0,), [after(tables[0], field_chip)] + tables[1:])
-    cells = run(0, (field, field_core, field_chip), bands0)
-    bands1 = prepare((1,), [after(tables[0], field_chip)] + tables[1:])
-    (state,) = run(1, cells, bands1)
-    bands23 = prepare((2, 3), [after(t, state) for t in tables])
-    cells = run(2, (state, core(state), beside(state)), bands23[:3])
-    (density,) = run(3, cells, bands23[3:], (readout.reshape(1, channels),))
+    own_cols = own_columns((0, 1), after(mine, taps))
+    theirs = [
+        core(after(m[:, :528], *tables[::-1], field_core, field_chip, own_cols[0])) for m in (mine[:2],)
+    ]
+
+    margin, rows0, rows1 = prepare((0, 1), [after(tables[0], field_chip)] + tables[1:])
+    theirs.append(core(after(mine[2:, :528], rows0)))
+    cells = run(0, (field, field_core, field_chip), (own_cols[0], margin, rows0))
+    (state,) = run(1, cells, (own_cols[1], rows1))
+    own_cols = own_columns((2, 3), after(mine, state))
+    margin, rows2, rows3 = prepare((2, 3), [after(t, state) for t in tables])
+    cells = run(2, (state, core(state), beside(state)), (own_cols[0], margin, rows2))
+    (density,) = run(3, cells, (own_cols[1], rows3), (readout.reshape(1, channels),))
 
     beside_density = core(density)
     pair = jnp.where(c == 0, jnp.stack([density, beside_density]), jnp.stack([beside_density, density]))

time: 51.8 us -> 51.3 us (level)
    pallas_call x2 -> x4, Pallas kernels: 2.28 us -> 3.66 us  [the longest x1 2.25 us: window_on_section(): call(stage_kernel, (shaped((4, 560, 256)), shaped((8, 16, WIDE))), [ANY]...]
    pallas_call x3 -> x2, Pallas kernels: 3.26 us -> 1.97 us  [prepare(): call(functools.partial(prepare_kernel, layers, spaces - 1), tuple(outs),...]
    ppermute x3, waiting for transfers between devices: 3.77 us -> 2.59 us  [section(): return lax.ppermute(array, 'section', [(i, i ^ k) for i in range(4)])]
  transfers between devices with their start and end apart: 19 -> 19, of which waited for: 8 -> 9; matrix products, arithmetic and copies ran while one was open for 0% -> 0% of each run, Pallas kernels for 12% -> 12%
where the time goes in v6:
time: 51.3 us; the launch traced here: 51.1 us
  starting transfers between devices  22.8 us (44%)
  waiting for transfers between devices  15.9 us (31%)
  Pallas kernels  12.1 us (24%)
    ppermute x6, starting transfers between devices, chip(): return lax.ppermute(array, 'space', [(i, i ^ 2 * k) for i in range(spaces)])  8.84 us
    ppermute x6, waiting for transfers between devices, chip(): return lax.ppermute(array, 'space', [(i, i ^ 2 * k) for i in range(spaces)])  7.77 us
    pallas_call x4, Pallas kernels, run(): call(functools.partial(layer_kernel, layer, len(cells), final), outs, [VM...  5.55 us
    all_to_all x1, starting transfers between devices, window_on_section(): lax.all_to_all(packed, 'section', split_axis=0, concat_axis=0, tiled=True)  5.18 us
    ppermute x2, starting transfers between devices, beside(): return lax.ppermute(array, ('section', 'space'), pairs)  3.77 us
    ppermute x3, starting transfers between devices, section(): return lax.ppermute(array, 'section', [(i, i ^ k) for i in range(4)])  3.49 us
    ppermute x2, waiting for transfers between devices, beside(): return lax.ppermute(array, ('section', 'space'), pairs)  2.97 us
    ppermute x3, waiting for transfers between devices, section(): return lax.ppermute(array, 'section', [(i, i ^ k) for i in range(4)])  2.59 us
  transfers between devices with their start and end apart: 19, of which 9 were waited for; matrix products, arithmetic and copies ran while one was open for 0% of the time, Pallas kernels for 12%

profile of v6, /device:TPU:0, one launch (start us, length us, event | category | flops | bytes accessed | tf_op | source)
XLA Modules:
  0.0 51.1 jit_solution(315785896147542974)
XLA Ops:
  0.0 2.2 %shard_map.82 = (bf16[4,560,256]{2,1,0:T(8,128)(2,1)}, bf16[8,16,128]{2,1,0:T(8,128)(2,1)}) custom-call(bf16[1,15,4,128]{3,2,1,0:T(4,128)(2,1)} %row_coef.1, bf16[1,15,16,32]{3,2,1,0:T(8,128)(2,1)} %col_coef.1, bf16[1,256,512]{2,1,0:T(8,128)(2,1)} %weight_in.1, bf16[1,512,256]{2,1,0:T(8,128)(2,1)} %weight_out.1, bf16[1,512]{1,0:T(2,128)(2,1)} %bias.1, ...), custom_call_target="tpu_custom_call" | custom-call | flops 1 | bytes 1 | tf_op jit(solution)/shard_map/pallas_call | solution.py:391
  2.3 5.2 %all-to-all-start = ((bf16[4,560,256]{2,1,0:T(8,128)(2,1)}), bf16[4,560,256]{2,1,0:T(8,128)(2,1)S(1)}, u32[]{:S(2)}, u32[]{:S(2)}) async-start(bf16[4,560,256]{2,1,0:T(8,128)(2,1)} %get-tuple-element.43), calls=%async_computation | async-start | bytes 2293760 | tf_op jit(solution)/shard_map/all_to_all | solution.py:419
  7.5 0.1 collective-permute-start.1
  7.6 0.5 collective-permute-start
  8.0 1.1 %collective-permute-done.sib_taps = bf16[8,16,128]{2,1,0:T(8,128)(2,1)S(1)} collective-permute-done((bf16[8,16,128]{2,1,0:T(8,128)(2,1)S(1)}, bf16[8,16,128]{2,1,0:T(8,128)(2,1)S(1)}, u32[]{:S(2)}, u32[]{:S(2)}) %collective-permute-start) | collective-permute-done | bytes 32800 | tf_op jit(solution)/shard_map/ppermute | solution.py:371
  9.1 0.0 collective-permute-done.1.sib
  9.1 0.1 shard_map.83
  9.3 3.7 %collective-permute-start.2 = (bf16[160,256]{1,0:T(8,128)(2,1)S(1)}, bf16[160,256]{1,0:T(8,128)(2,1)S(1)}, u32[]{:S(2)}, u32[]{:S(2)}) collective-permute-start(bf16[160,256]{1,0:T(8,128)(2,1)S(1)} %get-tuple-element.37), channel_id=1, source_target_pairs={{0,6},{1,7},{2,4},{3,5},{4,2},{5,3},{6,0},{7,1},{8,14},{9,15},{10,... | collective-permute-start | bytes 245768 | tf_op jit(solution)/shard_map/ppermute | solution.py:374
  12.9 0.0 collective-permute-start.4
  12.9 0.8 %collective-permute-start.3 = (bf16[144,256]{1,0:T(8,128)(2,1)S(1)}, bf16[144,256]{1,0:T(8,128)(2,1)S(1)}, u32[]{:S(2)}, u32[]{:S(2)}) collective-permute-start(bf16[144,256]{1,0:T(8,128)(2,1)S(1)} %get-tuple-element.38), channel_id=1, source_target_pairs={{0,4},{1,5},{2,6},{3,7},{4,0},{5,1},{6,2},{7,3},{8,12},{9,13},{10,... | collective-permute-start | bytes 221192 | tf_op jit(solution)/shard_map/ppermute | solution.py:374
  13.7 6.0 %collective-permute-done.3.g2 = bf16[144,256]{1,0:T(8,128)(2,1)S(1)} collective-permute-done((bf16[144,256]{1,0:T(8,128)(2,1)S(1)}, bf16[144,256]{1,0:T(8,128)(2,1)S(1)}, u32[]{:S(2)}, u32[]{:S(2)}) %collective-permute-start.3) | collective-permute-done | bytes 73760 | tf_op jit(solution)/shard_map/ppermute | solution.py:374
  19.8 0.0 collective-permute-done.2.g3
  19.8 0.1 collective-permute-start.5
  19.9 2.1 %collective-permute-start.6 = (bf16[512,256]{1,0:T(8,128)(2,1)S(1)}, bf16[512,256]{1,0:T(8,128)(2,1)S(1)}, u32[]{:S(2)}, u32[]{:S(2)}) collective-permute-start(bf16[512,256]{1,0:T(8,128)(2,1)S(1)} %shard_map.85.refs_0_), channel_id=1, source_target_pairs={{0,8},{1,2},{2,1},{3,4},{4,3},{5,6},{6,5},{7,15},{8,0},{9,10},{10,... | collective-permute-start | bytes 786440 | tf_op jit(solution)/shard_map/ppermute | solution.py:387
  22.0 1.5 %collective-permute-start.7 = (bf16[96,256]{1,0:T(8,128)(2,1)S(1)}, bf16[96,256]{1,0:T(8,128)(2,1)S(1)}, u32[]{:S(2)}, u32[]{:S(2)}) collective-permute-start(bf16[96,256]{1,0:T(8,128)(2,1)S(1)} %shard_map.84.q0), channel_id=1, source_target_pairs={{0,24},{8,16},{16,8},{24,0},{1,25},{9,17},{17,9},{25,1},{2,26},{10... | collective-permute-start | bytes 147464 | tf_op jit(solution)/shard_map/ppermute | solution.py:377
  23.5 0.1 collective-permute-start.8
  23.5 1.9 %collective-permute-start.9 = (bf16[96,256]{1,0:T(8,128)(2,1)S(1)}, bf16[96,256]{1,0:T(8,128)(2,1)S(1)}, u32[]{:S(2)}, u32[]{:S(2)}) collective-permute-start(bf16[96,256]{1,0:T(8,128)(2,1)S(1)} %shard_map.84.q0), channel_id=1, source_target_pairs={{0,8},{8,0},{16,24},{24,16},{1,9},{9,1},{17,25},{25,17},{2,10},{10... | collective-permute-start | bytes 147464 | tf_op jit(solution)/shard_map/ppermute | solution.py:377
  25.5 0.0 all-to-all-done.weights.refs_6_.refs_4_.refs_5_
  25.5 0.1 fusion
  25.6 0.7 %shard_map.87 = (bf16[512,512]{1,0:T(8,128)(2,1)S(1)}, bf16[512,512]{1,0:T(8,128)(2,1)S(1)}) custom-call(bf16[4,560,256]{2,1,0:T(8,128)(2,1)S(1)} %all-to-all-done.weights.refs_6_.refs_4_.refs_5_), custom_call_target="tpu_custom_call" | custom-call | flops 1 | bytes 1 | tf_op jit(solution)/shard_map/pallas_call | solution.py:442
  26.3 2.6 %collective-permute-done.7.q3 = bf16[96,256]{1,0:T(8,128)(2,1)S(1)} collective-permute-done((bf16[96,256]{1,0:T(8,128)(2,1)S(1)}, bf16[96,256]{1,0:T(8,128)(2,1)S(1)}, u32[]{:S(2)}, u32[]{:S(2)}) %collective-permute-start.7) | collective-permute-done | bytes 49184 | tf_op jit(solution)/shard_map/ppermute | solution.py:377
  28.9 0.0 collective-permute-done.9.q1
  28.9 0.0 collective-permute-done.5.refs_1_
  28.9 0.0 collective-permute-done.6.refs_2_
  28.9 0.1 collective-permute-start.10
  29.0 1.0 %shard_map.86 = (bf16[512,512]{1,0:T(8,128)(2,1)S(1)}, bf16[4,256,384]{2,1,0:T(8,128)(2,1)S(1)}, bf16[4,128,256]{2,1,0:T(8,128)(2,1)S(1)}) custom-call(bf16[96,256]{1,0:T(8,128)(2,1)S(1)} %shard_map.84.q0, bf16[96,256]{1,0:T(8,128)(2,1)S(1)} %collective-permute-done.7.q3, bf16[96,256]{1,0:T(8,128)(2,1)S(1)} %collective-permute-done.8.q2, ...), custom_call_target="tpu_custom_call" | custom-call | flops 1 | bytes 1 | tf_op jit(solution)/shard_map/pallas_call | solution.py:434
  30.0 0.6 %collective-permute-start.13 = (bf16[2,528,256]{2,1,0:T(8,128)(2,1)S(1)}, bf16[2,528,256]{2,1,0:T(8,128)(2,1)S(1)}, u32[]{:S(2)}, u32[]{:S(2)}) collective-permute-start(bf16[2,528,256]{2,1,0:T(8,128)(2,1)S(1)} %get-tuple-element.60), channel_id=1, source_target_pairs={{0,1},{1,0},{2,3},{3,2},{4,5},{5,4},{6,7},{7,6},{8,9},{9,8},{10,11... | collective-permute-start | bytes 1622024 | tf_op jit(solution)/shard_map/ppermute | solution.py:371
  30.5 0.4 collective-permute-done.10.refs_7_.refs_5_
  30.9 1.6 %shard_map.88 = (bf16[512,256]{1,0:T(8,128)(2,1)S(1)}, bf16[512,256]{1,0:T(8,128)(2,1)S(1)}) custom-call(bf16[512,256]{1,0:T(8,128)(2,1)S(1)} %shard_map.85.refs_0_, bf16[512,256]{1,0:T(8,128)(2,1)S(1)} %collective-permute-done.5.refs_1_, bf16[512,256]{1,0:T(8,128)(2,1)S(1)} %collective-permute-done.6.refs_2_, ...), custom_call_target="tpu_custom_call" | custom-call | flops 1 | bytes 1 | tf_op jit(solution)/shard_map/pallas_call | solution.py:453
  32.5 0.0 copy-start.2
  32.5 1.0 %shard_map.89.refs_0_ = bf16[512,256]{1,0:T(8,128)(2,1)S(1)} custom-call(bf16[512,256]{1,0:T(8,128)(2,1)S(1)} %get-tuple-element.48.refs_0_, bf16[512,256]{1,0:T(8,128)(2,1)S(1)} %get-tuple-element.49.refs_1_, bf16[4,128,256]{2,1,0:T(8,128)(2,1)S(1)} %get-tuple-element.50.refs_2_, bf16[512,512]{1,0:T(8,128)(2,1)S(1)} %get-tuple-element.51.refs_3_, ...), custom_call_target="tpu_custom_call" | custom-call | flops 1 | bytes 1 | tf_op jit(solution)/shard_map/pallas_call | solution.py:453
  33.6 0.2 collective-permute-start.11
  33.8 1.7 %collective-permute-start.12 = (bf16[512,256]{1,0:T(8,128)(2,1)S(1)}, bf16[512,256]{1,0:T(8,128)(2,1)S(1)}, u32[]{:S(2)}, u32[]{:S(2)}) collective-permute-start(bf16[512,256]{1,0:T(8,128)(2,1)S(1)} %shard_map.89.refs_0_), channel_id=1, source_target_pairs={{0,8},{1,2},{2,1},{3,4},{4,3},{5,6},{6,5},{7,15},{8,0},{9,10},{10,... | collective-permute-start | bytes 786440 | tf_op jit(solution)/shard_map/ppermute | solution.py:387
  35.5 0.7 %shard_map.91 = (bf16[512,512]{1,0:T(8,128)(2,1)S(1)}, bf16[512,512]{1,0:T(8,128)(2,1)S(1)}) custom-call(bf16[4,560,256]{2,1,0:T(8,128)(2,1)S(1)} %all-to-all-done.weights.refs_6_.refs_4_.refs_5_), custom_call_target="tpu_custom_call" | custom-call | flops 1 | bytes 1 | tf_op jit(solution)/shard_map/pallas_call | solution.py:442
  36.2 1.0 %shard_map.90 = (bf16[512,512]{1,0:T(8,128)(2,1)S(1)}, bf16[4,256,384]{2,1,0:T(8,128)(2,1)S(1)}, bf16[4,128,256]{2,1,0:T(8,128)(2,1)S(1)}) custom-call(bf16[96,256]{1,0:T(8,128)(2,1)S(1)} %shard_map.84.q0, bf16[96,256]{1,0:T(8,128)(2,1)S(1)} %collective-permute-done.7.q3, bf16[96,256]{1,0:T(8,128)(2,1)S(1)} %collective-permute-done.8.q2, ...), custom_call_target="tpu_custom_call" | custom-call | flops 1 | bytes 1 | tf_op jit(solution)/shard_map/pallas_call | solution.py:434
  37.2 0.0 collective-permute-done.13.refs_7_.refs_6_
  37.2 3.0 %collective-permute-done.12.refs_2_ = bf16[512,256]{1,0:T(8,128)(2,1)S(1)} collective-permute-done((bf16[512,256]{1,0:T(8,128)(2,1)S(1)}, bf16[512,256]{1,0:T(8,128)(2,1)S(1)}, u32[]{:S(2)}, u32[]{:S(2)}) %collective-permute-start.12) | collective-permute-done | bytes 262176 | tf_op jit(solution)/shard_map/ppermute | solution.py:387
  40.2 1.6 %shard_map.92 = (bf16[512,256]{1,0:T(8,128)(2,1)S(1)}, bf16[512,256]{1,0:T(8,128)(2,1)S(1)}) custom-call(bf16[512,256]{1,0:T(8,128)(2,1)S(1)} %shard_map.89.refs_0_, bf16[512,256]{1,0:T(8,128)(2,1)S(1)} %collective-permute-done.11.refs_1_, bf16[512,256]{1,0:T(8,128)(2,1)S(1)} %collective-permute-done.12.refs_2_, ...), custom_call_target="tpu_custom_call" | custom-call | flops 1 | bytes 1 | tf_op jit(solution)/shard_map/pallas_call | solution.py:453
  41.8 1.2 %shard_map.93 = f32[8,128]{1,0:T(8,128)S(1)} custom-call(bf16[512,256]{1,0:T(8,128)(2,1)S(1)} %get-tuple-element.61.refs_0_, bf16[512,256]{1,0:T(8,128)(2,1)S(1)} %get-tuple-element.62.refs_1_, bf16[4,128,256]{2,1,0:T(8,128)(2,1)S(1)} %get-tuple-element.63.refs_2_, bf16[512,512]{1,0:T(8,128)(2,1)S(1)} %get-tuple-element.64.refs_3_, ...), custom_call_target="tpu_custom_call" | custom-call | flops 1 | bytes 1 | tf_op jit(solution)/shard_map/pallas_call | solution.py:453
  43.1 0.1 collective-permute-start.14
  43.2 1.1 %collective-permute-done.14 = f32[8,128]{1,0:T(8,128)S(1)} collective-permute-done((f32[8,128]{1,0:T(8,128)S(1)}, f32[8,128]{1,0:T(8,128)S(1)}, u32[]{:S(2)}, u32[]{:S(2)}) %collective-permute-start.14) | collective-permute-done | bytes 4128 | tf_op jit(solution)/shard_map/ppermute | solution.py:371
  44.2 1.5 %collective-permute-start.15 = (f32[2,8,128]{2,1,0:T(8,128)S(1)}, f32[2,8,128]{2,1,0:T(8,128)S(1)}, u32[]{:S(2)}, u32[]{:S(2)}) collective-permute-start(f32[2,8,128]{2,1,0:T(8,128)S(1)} %maximum_select_fusion.g0), channel_id=1, source_target_pairs={{0,6},{1,7},{2,4},{3,5},{4,2},{5,3},{6,0},{7,1},{8,14},{9,15},{10,... | collective-permute-start | bytes 24584 | tf_op jit(solution)/shard_map/ppermute | solution.py:374
  45.7 0.1 collective-permute-start.16
  45.8 2.8 %collective-permute-start.17 = (f32[2,8,128]{2,1,0:T(8,128)S(1)}, f32[2,8,128]{2,1,0:T(8,128)S(1)}, u32[]{:S(2)}, u32[]{:S(2)}) collective-permute-start(f32[2,8,128]{2,1,0:T(8,128)S(1)} %maximum_select_fusion.g0), channel_id=1, source_target_pairs={{0,2},{1,3},{2,0},{3,1},{4,6},{5,7},{6,4},{7,5},{8,10},{9,11},{10,... | collective-permute-start | bytes 24584 | tf_op jit(solution)/shard_map/ppermute | solution.py:374
  48.6 1.1 %collective-permute-done.15.g3 = f32[2,8,128]{2,1,0:T(8,128)S(1)} collective-permute-done((f32[2,8,128]{2,1,0:T(8,128)S(1)}, f32[2,8,128]{2,1,0:T(8,128)S(1)}, u32[]{:S(2)}, u32[]{:S(2)}) %collective-permute-start.15) | collective-permute-done | bytes 8224 | tf_op jit(solution)/shard_map/ppermute | solution.py:374
  49.7 0.6 %collective-permute-done.16.g2 = f32[2,8,128]{2,1,0:T(8,128)S(1)} collective-permute-done((f32[2,8,128]{2,1,0:T(8,128)S(1)}, f32[2,8,128]{2,1,0:T(8,128)S(1)}, u32[]{:S(2)}, u32[]{:S(2)}) %collective-permute-start.16) | collective-permute-done | bytes 8224 | tf_op jit(solution)/shard_map/ppermute | solution.py:374
  50.3 0.1 collective-permute-done.17.g1
  50.3 0.7 %shard_map.94 = f32[1,4,128]{2,1,0:T(4,128)} custom-call(f32[2,8,128]{2,1,0:T(8,128)S(1)} %maximum_select_fusion.g0, f32[2,8,128]{2,1,0:T(8,128)S(1)} %collective-permute-done.15.g3, f32[2,8,128]{2,1,0:T(8,128)S(1)} %collective-permute-done.16.g2, f32[2,8,128]{2,1,0:T(8,128)S(1)} %collective-permute-done.17.g1), custom_call_target="tpu_custom_call" | custom-call | flops 1 | bytes 1 | tf_op jit(solution)/shard_map/pallas_call | solution.py:477
  (13 shorter events, 0.1 us)
Async XLA Ops:
  0.0 7.4 %copy-start = (bf16[4,4,128,256]{3,2,1,0:T(8,128)(2,1)S(1)}, bf16[4,4,128,256]{3,2,1,0:T(8,128)(2,1)}, u32[]{:S(2)}) copy-start(bf16[4,4,128,256]{3,2,1,0:T(8,128)(2,1)} %param.8) | copy-start | bytes 3145732
  2.3 5.3 %copy-start.1 = (bf16[8,16,128]{2,1,0:T(8,128)(2,1)S(1)}, bf16[8,16,128]{2,1,0:T(8,128)(2,1)}, u32[]{:S(2)}) copy-start(bf16[8,16,128]{2,1,0:T(8,128)(2,1)} %get-tuple-element.35.own_taps) | copy-start | bytes 98308
  2.3 23.2 %all-to-all-start = ((bf16[4,560,256]{2,1,0:T(8,128)(2,1)}), bf16[4,560,256]{2,1,0:T(8,128)(2,1)S(1)}, u32[]{:S(2)}, u32[]{:S(2)}) async-start(bf16[4,560,256]{2,1,0:T(8,128)(2,1)} %get-tuple-element.43), calls=%async_computation | async-start | bytes 2293760 | tf_op jit(solution)/shard_map/all_to_all | solution.py:419
  7.5 1.7 %collective-permute-start.1 = (bf16[4,128,256]{2,1,0:T(8,128)(2,1)S(1)}, bf16[4,128,256]{2,1,0:T(8,128)(2,1)S(1)}, u32[]{:S(2)}, u32[]{:S(2)}) collective-permute-start(bf16[4,128,256]{2,1,0:T(8,128)(2,1)S(1)} %dynamic-slice_bitcast_fusion.own), channel_id=1, source_target_pairs={{0,1},{1,0},{2,3},{3,2},{4,5},{5,4},{6,7},{7,6},{8,9},{9,8},{10,11... | collective-permute-start | bytes 786440 | tf_op jit(solution)/shard_map/ppermute | solution.py:371
  7.6 1.6 %collective-permute-start = (bf16[8,16,128]{2,1,0:T(8,128)(2,1)S(1)}, bf16[8,16,128]{2,1,0:T(8,128)(2,1)S(1)}, u32[]{:S(2)}, u32[]{:S(2)}) collective-permute-start(bf16[8,16,128]{2,1,0:T(8,128)(2,1)S(1)} %copy-done.1), channel_id=1, source_target_pairs={{0,1},{1,0},{2,3},{3,2},{4,5},{5,4},{6,7},{7,6},{8,9},{9,8},{10,11... | collective-permute-start | bytes 98312 | tf_op jit(solution)/shard_map/ppermute | solution.py:371
  9.3 10.5 %collective-permute-start.2 = (bf16[160,256]{1,0:T(8,128)(2,1)S(1)}, bf16[160,256]{1,0:T(8,128)(2,1)S(1)}, u32[]{:S(2)}, u32[]{:S(2)}) collective-permute-start(bf16[160,256]{1,0:T(8,128)(2,1)S(1)} %get-tuple-element.37), channel_id=1, source_target_pairs={{0,6},{1,7},{2,4},{3,5},{4,2},{5,3},{6,0},{7,1},{8,14},{9,15},{10,... | collective-permute-start | bytes 245768 | tf_op jit(solution)/shard_map/ppermute | solution.py:374
  12.9 6.8 %collective-permute-start.4 = (bf16[160,256]{1,0:T(8,128)(2,1)S(1)}, bf16[160,256]{1,0:T(8,128)(2,1)S(1)}, u32[]{:S(2)}, u32[]{:S(2)}) collective-permute-start(bf16[160,256]{1,0:T(8,128)(2,1)S(1)} %get-tuple-element.39), channel_id=1, source_target_pairs={{0,2},{1,3},{2,0},{3,1},{4,6},{5,7},{6,4},{7,5},{8,10},{9,11},{10,... | collective-permute-start | bytes 245768 | tf_op jit(solution)/shard_map/ppermute | solution.py:374
  12.9 6.8 %collective-permute-start.3 = (bf16[144,256]{1,0:T(8,128)(2,1)S(1)}, bf16[144,256]{1,0:T(8,128)(2,1)S(1)}, u32[]{:S(2)}, u32[]{:S(2)}) collective-permute-start(bf16[144,256]{1,0:T(8,128)(2,1)S(1)} %get-tuple-element.38), channel_id=1, source_target_pairs={{0,4},{1,5},{2,6},{3,7},{4,0},{5,1},{6,2},{7,3},{8,12},{9,13},{10,... | collective-permute-start | bytes 221192 | tf_op jit(solution)/shard_map/ppermute | solution.py:374
  19.8 9.0 %collective-permute-start.5 = (bf16[512,256]{1,0:T(8,128)(2,1)S(1)}, bf16[512,256]{1,0:T(8,128)(2,1)S(1)}, u32[]{:S(2)}, u32[]{:S(2)}) collective-permute-start(bf16[512,256]{1,0:T(8,128)(2,1)S(1)} %shard_map.85.refs_0_), channel_id=1, source_target_pairs={{0,1},{1,0},{2,3},{3,2},{4,5},{5,4},{6,7},{7,6},{8,9},{9,8},{10,11... | collective-permute-start | bytes 786440 | tf_op jit(solution)/shard_map/ppermute | solution.py:371
  19.9 9.0 %collective-permute-start.6 = (bf16[512,256]{1,0:T(8,128)(2,1)S(1)}, bf16[512,256]{1,0:T(8,128)(2,1)S(1)}, u32[]{:S(2)}, u32[]{:S(2)}) collective-permute-start(bf16[512,256]{1,0:T(8,128)(2,1)S(1)} %shard_map.85.refs_0_), channel_id=1, source_target_pairs={{0,8},{1,2},{2,1},{3,4},{4,3},{5,6},{6,5},{7,15},{8,0},{9,10},{10,... | collective-permute-start | bytes 786440 | tf_op jit(solution)/shard_map/ppermute | solution.py:387
  22.0 6.9 %collective-permute-start.7 = (bf16[96,256]{1,0:T(8,128)(2,1)S(1)}, bf16[96,256]{1,0:T(8,128)(2,1)S(1)}, u32[]{:S(2)}, u32[]{:S(2)}) collective-permute-start(bf16[96,256]{1,0:T(8,128)(2,1)S(1)} %shard_map.84.q0), channel_id=1, source_target_pairs={{0,24},{8,16},{16,8},{24,0},{1,25},{9,17},{17,9},{25,1},{2,26},{10... | collective-permute-start | bytes 147464 | tf_op jit(solution)/shard_map/ppermute | solution.py:377
  23.5 5.4 %collective-permute-start.8 = (bf16[96,256]{1,0:T(8,128)(2,1)S(1)}, bf16[96,256]{1,0:T(8,128)(2,1)S(1)}, u32[]{:S(2)}, u32[]{:S(2)}) collective-permute-start(bf16[96,256]{1,0:T(8,128)(2,1)S(1)} %shard_map.84.q0), channel_id=1, source_target_pairs={{0,16},{8,24},{16,0},{24,8},{1,17},{9,25},{17,1},{25,9},{2,18},{10... | collective-permute-start | bytes 147464 | tf_op jit(solution)/shard_map/ppermute | solution.py:377
  23.5 5.3 %collective-permute-start.9 = (bf16[96,256]{1,0:T(8,128)(2,1)S(1)}, bf16[96,256]{1,0:T(8,128)(2,1)S(1)}, u32[]{:S(2)}, u32[]{:S(2)}) collective-permute-start(bf16[96,256]{1,0:T(8,128)(2,1)S(1)} %shard_map.84.q0), channel_id=1, source_target_pairs={{0,8},{8,0},{16,24},{24,16},{1,9},{9,1},{17,25},{25,17},{2,10},{10... | collective-permute-start | bytes 147464 | tf_op jit(solution)/shard_map/ppermute | solution.py:377
  28.9 2.0 %collective-permute-start.10 = (bf16[2,528,256]{2,1,0:T(8,128)(2,1)S(1)}, bf16[2,528,256]{2,1,0:T(8,128)(2,1)S(1)}, u32[]{:S(2)}, u32[]{:S(2)}) collective-permute-start(bf16[2,528,256]{2,1,0:T(8,128)(2,1)S(1)} %get-tuple-element.47), channel_id=1, source_target_pairs={{0,1},{1,0},{2,3},{3,2},{4,5},{5,4},{6,7},{7,6},{8,9},{9,8},{10,11... | collective-permute-start | bytes 1622024 | tf_op jit(solution)/shard_map/ppermute | solution.py:371
  30.0 7.2 %collective-permute-start.13 = (bf16[2,528,256]{2,1,0:T(8,128)(2,1)S(1)}, bf16[2,528,256]{2,1,0:T(8,128)(2,1)S(1)}, u32[]{:S(2)}, u32[]{:S(2)}) collective-permute-start(bf16[2,528,256]{2,1,0:T(8,128)(2,1)S(1)} %get-tuple-element.60), channel_id=1, source_target_pairs={{0,1},{1,0},{2,3},{3,2},{4,5},{5,4},{6,7},{7,6},{8,9},{9,8},{10,11... | collective-permute-start | bytes 1622024 | tf_op jit(solution)/shard_map/ppermute | solution.py:371
  32.5 2.9 %copy-start.2 = (bf16[256]{0:T(256)(128)(2,1)S(1)}, bf16[256]{0:T(256)(128)(2,1)}, u32[]{:S(2)}) copy-start(bf16[256]{0:T(256)(128)(2,1)} %param.15) | copy-start | bytes 1540
  33.6 3.6 %collective-permute-start.11 = (bf16[512,256]{1,0:T(8,128)(2,1)S(1)}, bf16[512,256]{1,0:T(8,128)(2,1)S(1)}, u32[]{:S(2)}, u32[]{:S(2)}) collective-permute-start(bf16[512,256]{1,0:T(8,128)(2,1)S(1)} %shard_map.89.refs_0_), channel_id=1, source_target_pairs={{0,1},{1,0},{2,3},{3,2},{4,5},{5,4},{6,7},{7,6},{8,9},{9,8},{10,11... | collective-permute-start | bytes 786440 | tf_op jit(solution)/shard_map/ppermute | solution.py:371
  33.8 6.4 %collective-permute-start.12 = (bf16[512,256]{1,0:T(8,128)(2,1)S(1)}, bf16[512,256]{1,0:T(8,128)(2,1)S(1)}, u32[]{:S(2)}, u32[]{:S(2)}) collective-permute-start(bf16[512,256]{1,0:T(8,128)(2,1)S(1)} %shard_map.89.refs_0_), channel_id=1, source_target_pairs={{0,8},{1,2},{2,1},{3,4},{4,3},{5,6},{6,5},{7,15},{8,0},{9,10},{10,... | collective-permute-start | bytes 786440 | tf_op jit(solution)/shard_map/ppermute | solution.py:387
  43.1 1.2 %collective-permute-start.14 = (f32[8,128]{1,0:T(8,128)S(1)}, f32[8,128]{1,0:T(8,128)S(1)}, u32[]{:S(2)}, u32[]{:S(2)}) collective-permute-start(f32[8,128]{1,0:T(8,128)S(1)} %shard_map.93), channel_id=1, source_target_pairs={{0,1},{1,0},{2,3},{3,2},{4,5},{5,4},{6,7},{7,6},{8,9},{9,8},{10,11... | collective-permute-start | bytes 12296 | tf_op jit(solution)/shard_map/ppermute | solution.py:371
  44.2 5.4 %collective-permute-start.15 = (f32[2,8,128]{2,1,0:T(8,128)S(1)}, f32[2,8,128]{2,1,0:T(8,128)S(1)}, u32[]{:S(2)}, u32[]{:S(2)}) collective-permute-start(f32[2,8,128]{2,1,0:T(8,128)S(1)} %maximum_select_fusion.g0), channel_id=1, source_target_pairs={{0,6},{1,7},{2,4},{3,5},{4,2},{5,3},{6,0},{7,1},{8,14},{9,15},{10,... | collective-permute-start | bytes 24584 | tf_op jit(solution)/shard_map/ppermute | solution.py:374
  45.7 4.6 %collective-permute-start.16 = (f32[2,8,128]{2,1,0:T(8,128)S(1)}, f32[2,8,128]{2,1,0:T(8,128)S(1)}, u32[]{:S(2)}, u32[]{:S(2)}) collective-permute-start(f32[2,8,128]{2,1,0:T(8,128)S(1)} %maximum_select_fusion.g0), channel_id=1, source_target_pairs={{0,4},{1,5},{2,6},{3,7},{4,0},{5,1},{6,2},{7,3},{8,12},{9,13},{10,... | collective-permute-start | bytes 24584 | tf_op jit(solution)/shard_map/ppermute | solution.py:374
  45.8 4.5 %collective-permute-start.17 = (f32[2,8,128]{2,1,0:T(8,128)S(1)}, f32[2,8,128]{2,1,0:T(8,128)S(1)}, u32[]{:S(2)}, u32[]{:S(2)}) collective-permute-start(f32[2,8,128]{2,1,0:T(8,128)S(1)} %maximum_select_fusion.g0), channel_id=1, source_target_pairs={{0,2},{1,3},{2,0},{3,1},{4,6},{5,7},{6,4},{7,5},{8,10},{9,11},{10,... | collective-permute-start | bytes 24584 | tf_op jit(solution)/shard_map/ppermute | solution.py:374

commit v7 on v6

--- a/solution.py
+++ b/solution.py
@@ -271,7 +271,8 @@
         return jnp.concatenate([pltpu.roll(part, shift, 1, stride=1, stride_axis=0)] * 8, 0)
 
     def sides(left, right):
-        return jnp.where(c == 0, right, left).astype(BF16), jnp.where(c == 0, left, right).astype(BF16)
+        first = c == (0 if layer == 0 else 1)
+        return jnp.where(first, right, left).astype(BF16), jnp.where(first, left, right).astype(BF16)
 
     for layer in layers:
         table = picked(s ^ layer, [q[...].astype(F32) for q in (q0, q1, q2, q3)])
@@ -468,7 +469,7 @@
     (state,) = run(1, cells, (own_cols[1], rows1))
     own_cols = own_columns((2, 3), after(mine, state))
     margin, rows2, rows3 = prepare((2, 3), [after(t, state) for t in tables])
-    cells = run(2, (state, core(state), beside(state)), (own_cols[0], margin, rows2))
+    cells = run(2, (state, beside(state), core(state)), (own_cols[0], margin, rows2))
     (density,) = run(3, cells, (own_cols[1], rows3), (readout.reshape(1, channels),))
 
     beside_density = core(density)

time: 51.3 us -> 51.2 us (level)
  transfers between devices with their start and end apart: 19 -> 19, of which waited for: 9 -> 8; matrix products, arithmetic and copies ran while one was open for 0% -> 0% of each run, Pallas kernels for 12% -> 12%
where the time goes in v7:
time: 51.2 us; the launch traced here: 50.9 us
  starting transfers between devices  22.6 us (44%)
  waiting for transfers between devices  15.9 us (31%)
  Pallas kernels  12.1 us (24%)
    ppermute x6, starting transfers between devices, chip(): return lax.ppermute(array, 'space', [(i, i ^ 2 * k) for i in range(spaces)])  8.84 us
    ppermute x6, waiting for transfers between devices, chip(): return lax.ppermute(array, 'space', [(i, i ^ 2 * k) for i in range(spaces)])  7.77 us
    pallas_call x4, Pallas kernels, run(): call(functools.partial(layer_kernel, layer, len(cells), final), outs, [VM...  5.55 us
    all_to_all x1, starting transfers between devices, window_on_section(): lax.all_to_all(packed, 'section', split_axis=0, concat_axis=0, tiled=True)  5.18 us
    ppermute x2, starting transfers between devices, beside(): return lax.ppermute(array, ('section', 'space'), pairs)  3.84 us
    ppermute x3, starting transfers between devices, section(): return lax.ppermute(array, 'section', [(i, i ^ k) for i in range(4)])  3.49 us
    ppermute x2, waiting for transfers between devices, beside(): return lax.ppermute(array, ('section', 'space'), pairs)  2.97 us
    ppermute x7, waiting for transfers between devices, core(): return lax.ppermute(array, 'space', [(i, i ^ 1) for i in range(spaces)])  2.6 us
  transfers between devices with their start and end apart: 19, of which 8 were waited for; matrix products, arithmetic and copies ran while one was open for 0% of the time, Pallas kernels for 12%

profile of v7, /device:TPU:0, one launch (start us, length us, event | category | flops | bytes accessed | tf_op | source)
XLA Modules:
  0.0 50.9 jit_solution(2253093918946934586)
XLA Ops:
  0.0 2.2 %shard_map.82 = (bf16[4,560,256]{2,1,0:T(8,128)(2,1)}, bf16[8,16,128]{2,1,0:T(8,128)(2,1)}) custom-call(bf16[1,15,4,128]{3,2,1,0:T(4,128)(2,1)} %row_coef.1, bf16[1,15,16,32]{3,2,1,0:T(8,128)(2,1)} %col_coef.1, bf16[1,256,512]{2,1,0:T(8,128)(2,1)} %weight_in.1, bf16[1,512,256]{2,1,0:T(8,128)(2,1)} %weight_out.1, bf16[1,512]{1,0:T(2,128)(2,1)} %bias.1, ...), custom_call_target="tpu_custom_call" | custom-call | flops 1 | bytes 1 | tf_op jit(solution)/shard_map/pallas_call | solution.py:392
  2.3 5.2 %all-to-all-start = ((bf16[4,560,256]{2,1,0:T(8,128)(2,1)}), bf16[4,560,256]{2,1,0:T(8,128)(2,1)S(1)}, u32[]{:S(2)}, u32[]{:S(2)}) async-start(bf16[4,560,256]{2,1,0:T(8,128)(2,1)} %get-tuple-element.43), calls=%async_computation | async-start | bytes 2293760 | tf_op jit(solution)/shard_map/all_to_all | solution.py:420
  7.5 0.1 collective-permute-start.1
  7.6 0.5 collective-permute-start
  8.0 1.1 %collective-permute-done.sib_taps = bf16[8,16,128]{2,1,0:T(8,128)(2,1)S(1)} collective-permute-done((bf16[8,16,128]{2,1,0:T(8,128)(2,1)S(1)}, bf16[8,16,128]{2,1,0:T(8,128)(2,1)S(1)}, u32[]{:S(2)}, u32[]{:S(2)}) %collective-permute-start) | collective-permute-done | bytes 32800 | tf_op jit(solution)/shard_map/ppermute | solution.py:372
  9.1 0.0 collective-permute-done.1.sib
  9.1 0.1 shard_map.83
  9.3 3.7 %collective-permute-start.2 = (bf16[160,256]{1,0:T(8,128)(2,1)S(1)}, bf16[160,256]{1,0:T(8,128)(2,1)S(1)}, u32[]{:S(2)}, u32[]{:S(2)}) collective-permute-start(bf16[160,256]{1,0:T(8,128)(2,1)S(1)} %get-tuple-element.37), channel_id=1, source_target_pairs={{0,6},{1,7},{2,4},{3,5},{4,2},{5,3},{6,0},{7,1},{8,14},{9,15},{10,... | collective-permute-start | bytes 245768 | tf_op jit(solution)/shard_map/ppermute | solution.py:375
  12.9 0.0 collective-permute-start.4
  12.9 0.8 %collective-permute-start.3 = (bf16[144,256]{1,0:T(8,128)(2,1)S(1)}, bf16[144,256]{1,0:T(8,128)(2,1)S(1)}, u32[]{:S(2)}, u32[]{:S(2)}) collective-permute-start(bf16[144,256]{1,0:T(8,128)(2,1)S(1)} %get-tuple-element.38), channel_id=1, source_target_pairs={{0,4},{1,5},{2,6},{3,7},{4,0},{5,1},{6,2},{7,3},{8,12},{9,13},{10,... | collective-permute-start | bytes 221192 | tf_op jit(solution)/shard_map/ppermute | solution.py:375
  13.7 6.0 %collective-permute-done.3.g2 = bf16[144,256]{1,0:T(8,128)(2,1)S(1)} collective-permute-done((bf16[144,256]{1,0:T(8,128)(2,1)S(1)}, bf16[144,256]{1,0:T(8,128)(2,1)S(1)}, u32[]{:S(2)}, u32[]{:S(2)}) %collective-permute-start.3) | collective-permute-done | bytes 73760 | tf_op jit(solution)/shard_map/ppermute | solution.py:375
  19.8 0.0 collective-permute-done.2.g3
  19.8 0.0 collective-permute-done.4.g1
  19.8 0.1 collective-permute-start.5
  19.9 2.1 %collective-permute-start.6 = (bf16[512,256]{1,0:T(8,128)(2,1)S(1)}, bf16[512,256]{1,0:T(8,128)(2,1)S(1)}, u32[]{:S(2)}, u32[]{:S(2)}) collective-permute-start(bf16[512,256]{1,0:T(8,128)(2,1)S(1)} %shard_map.85.refs_0_), channel_id=1, source_target_pairs={{0,8},{1,2},{2,1},{3,4},{4,3},{5,6},{6,5},{7,15},{8,0},{9,10},{10,... | collective-permute-start | bytes 786440 | tf_op jit(solution)/shard_map/ppermute | solution.py:388
  22.0 1.5 %collective-permute-start.7 = (bf16[96,256]{1,0:T(8,128)(2,1)S(1)}, bf16[96,256]{1,0:T(8,128)(2,1)S(1)}, u32[]{:S(2)}, u32[]{:S(2)}) collective-permute-start(bf16[96,256]{1,0:T(8,128)(2,1)S(1)} %shard_map.84.q0), channel_id=1, source_target_pairs={{0,24},{8,16},{16,8},{24,0},{1,25},{9,17},{17,9},{25,1},{2,26},{10... | collective-permute-start | bytes 147464 | tf_op jit(solution)/shard_map/ppermute | solution.py:378
  23.5 0.1 collective-permute-start.8
  23.5 1.9 %collective-permute-start.9 = (bf16[96,256]{1,0:T(8,128)(2,1)S(1)}, bf16[96,256]{1,0:T(8,128)(2,1)S(1)}, u32[]{:S(2)}, u32[]{:S(2)}) collective-permute-start(bf16[96,256]{1,0:T(8,128)(2,1)S(1)} %shard_map.84.q0), channel_id=1, source_target_pairs={{0,8},{8,0},{16,24},{24,16},{1,9},{9,1},{17,25},{25,17},{2,10},{10... | collective-permute-start | bytes 147464 | tf_op jit(solution)/shard_map/ppermute | solution.py:378
  25.5 0.0 all-to-all-done.weights.refs_6_.refs_4_.refs_5_
  25.5 0.1 fusion
  25.6 0.7 %shard_map.87 = (bf16[512,512]{1,0:T(8,128)(2,1)S(1)}, bf16[512,512]{1,0:T(8,128)(2,1)S(1)}) custom-call(bf16[4,560,256]{2,1,0:T(8,128)(2,1)S(1)} %all-to-all-done.weights.refs_6_.refs_4_.refs_5_), custom_call_target="tpu_custom_call" | custom-call | flops 1 | bytes 1 | tf_op jit(solution)/shard_map/pallas_call | solution.py:443
  26.3 2.6 %collective-permute-done.7.q3 = bf16[96,256]{1,0:T(8,128)(2,1)S(1)} collective-permute-done((bf16[96,256]{1,0:T(8,128)(2,1)S(1)}, bf16[96,256]{1,0:T(8,128)(2,1)S(1)}, u32[]{:S(2)}, u32[]{:S(2)}) %collective-permute-start.7) | collective-permute-done | bytes 49184 | tf_op jit(solution)/shard_map/ppermute | solution.py:378
  28.9 0.0 collective-permute-done.8.q2
  28.9 0.0 collective-permute-done.9.q1
  28.9 0.0 collective-permute-done.5.refs_1_
  28.9 0.1 collective-permute-start.10
  29.0 1.0 %shard_map.86 = (bf16[512,512]{1,0:T(8,128)(2,1)S(1)}, bf16[4,256,384]{2,1,0:T(8,128)(2,1)S(1)}, bf16[4,128,256]{2,1,0:T(8,128)(2,1)S(1)}) custom-call(bf16[96,256]{1,0:T(8,128)(2,1)S(1)} %shard_map.84.q0, bf16[96,256]{1,0:T(8,128)(2,1)S(1)} %collective-permute-done.7.q3, bf16[96,256]{1,0:T(8,128)(2,1)S(1)} %collective-permute-done.8.q2, ...), custom_call_target="tpu_custom_call" | custom-call | flops 1 | bytes 1 | tf_op jit(solution)/shard_map/pallas_call | solution.py:435
  30.0 0.6 %collective-permute-start.13 = (bf16[2,528,256]{2,1,0:T(8,128)(2,1)S(1)}, bf16[2,528,256]{2,1,0:T(8,128)(2,1)S(1)}, u32[]{:S(2)}, u32[]{:S(2)}) collective-permute-start(bf16[2,528,256]{2,1,0:T(8,128)(2,1)S(1)} %get-tuple-element.60), channel_id=1, source_target_pairs={{0,1},{1,0},{2,3},{3,2},{4,5},{5,4},{6,7},{7,6},{8,9},{9,8},{10,11... | collective-permute-start | bytes 1622024 | tf_op jit(solution)/shard_map/ppermute | solution.py:372
  30.5 0.4 collective-permute-done.10.refs_7_.refs_5_
  30.9 1.6 %shard_map.88 = (bf16[512,256]{1,0:T(8,128)(2,1)S(1)}, bf16[512,256]{1,0:T(8,128)(2,1)S(1)}) custom-call(bf16[512,256]{1,0:T(8,128)(2,1)S(1)} %shard_map.85.refs_0_, bf16[512,256]{1,0:T(8,128)(2,1)S(1)} %collective-permute-done.5.refs_1_, bf16[512,256]{1,0:T(8,128)(2,1)S(1)} %collective-permute-done.6.refs_2_, ...), custom_call_target="tpu_custom_call" | custom-call | flops 1 | bytes 1 | tf_op jit(solution)/shard_map/pallas_call | solution.py:454
  32.5 0.0 copy-start.2
  32.5 1.0 %shard_map.89.refs_0_ = bf16[512,256]{1,0:T(8,128)(2,1)S(1)} custom-call(bf16[512,256]{1,0:T(8,128)(2,1)S(1)} %get-tuple-element.48.refs_0_, bf16[512,256]{1,0:T(8,128)(2,1)S(1)} %get-tuple-element.49.refs_1_, bf16[4,128,256]{2,1,0:T(8,128)(2,1)S(1)} %get-tuple-element.50.refs_2_, bf16[512,512]{1,0:T(8,128)(2,1)S(1)} %get-tuple-element.51.refs_3_, ...), custom_call_target="tpu_custom_call" | custom-call | flops 1 | bytes 1 | tf_op jit(solution)/shard_map/pallas_call | solution.py:454
  33.6 1.7 %collective-permute-start.11 = (bf16[512,256]{1,0:T(8,128)(2,1)S(1)}, bf16[512,256]{1,0:T(8,128)(2,1)S(1)}, u32[]{:S(2)}, u32[]{:S(2)}) collective-permute-start(bf16[512,256]{1,0:T(8,128)(2,1)S(1)} %shard_map.89.refs_0_), channel_id=1, source_target_pairs={{0,8},{1,2},{2,1},{3,4},{4,3},{5,6},{6,5},{7,15},{8,0},{9,10},{10,... | collective-permute-start | bytes 786440 | tf_op jit(solution)/shard_map/ppermute | solution.py:388
  35.3 0.0 collective-permute-start.12
  35.3 0.7 %shard_map.91 = (bf16[512,512]{1,0:T(8,128)(2,1)S(1)}, bf16[512,512]{1,0:T(8,128)(2,1)S(1)}) custom-call(bf16[4,560,256]{2,1,0:T(8,128)(2,1)S(1)} %all-to-all-done.weights.refs_6_.refs_4_.refs_5_), custom_call_target="tpu_custom_call" | custom-call | flops 1 | bytes 1 | tf_op jit(solution)/shard_map/pallas_call | solution.py:443
  36.0 1.0 %shard_map.90 = (bf16[512,512]{1,0:T(8,128)(2,1)S(1)}, bf16[4,256,384]{2,1,0:T(8,128)(2,1)S(1)}, bf16[4,128,256]{2,1,0:T(8,128)(2,1)S(1)}) custom-call(bf16[96,256]{1,0:T(8,128)(2,1)S(1)} %shard_map.84.q0, bf16[96,256]{1,0:T(8,128)(2,1)S(1)} %collective-permute-done.7.q3, bf16[96,256]{1,0:T(8,128)(2,1)S(1)} %collective-permute-done.8.q2, ...), custom_call_target="tpu_custom_call" | custom-call | flops 1 | bytes 1 | tf_op jit(solution)/shard_map/pallas_call | solution.py:435
  37.0 0.0 collective-permute-done.13.refs_7_.refs_6_
  37.0 3.0 %collective-permute-done.11.refs_1_ = bf16[512,256]{1,0:T(8,128)(2,1)S(1)} collective-permute-done((bf16[512,256]{1,0:T(8,128)(2,1)S(1)}, bf16[512,256]{1,0:T(8,128)(2,1)S(1)}, u32[]{:S(2)}, u32[]{:S(2)}) %collective-permute-start.11) | collective-permute-done | bytes 262176 | tf_op jit(solution)/shard_map/ppermute | solution.py:388
  40.0 1.6 %shard_map.92 = (bf16[512,256]{1,0:T(8,128)(2,1)S(1)}, bf16[512,256]{1,0:T(8,128)(2,1)S(1)}) custom-call(bf16[512,256]{1,0:T(8,128)(2,1)S(1)} %shard_map.89.refs_0_, bf16[512,256]{1,0:T(8,128)(2,1)S(1)} %collective-permute-done.11.refs_1_, bf16[512,256]{1,0:T(8,128)(2,1)S(1)} %collective-permute-done.12.refs_2_, ...), custom_call_target="tpu_custom_call" | custom-call | flops 1 | bytes 1 | tf_op jit(solution)/shard_map/pallas_call | solution.py:454
  41.7 1.2 %shard_map.93 = f32[8,128]{1,0:T(8,128)S(1)} custom-call(bf16[512,256]{1,0:T(8,128)(2,1)S(1)} %get-tuple-element.61.refs_0_, bf16[512,256]{1,0:T(8,128)(2,1)S(1)} %get-tuple-element.62.refs_1_, bf16[4,128,256]{2,1,0:T(8,128)(2,1)S(1)} %get-tuple-element.63.refs_2_, bf16[512,512]{1,0:T(8,128)(2,1)S(1)} %get-tuple-element.64.refs_3_, ...), custom_call_target="tpu_custom_call" | custom-call | flops 1 | bytes 1 | tf_op jit(solution)/shard_map/pallas_call | solution.py:454
  42.9 0.0 collective-permute-start.14
  42.9 1.1 %collective-permute-done.14 = f32[8,128]{1,0:T(8,128)S(1)} collective-permute-done((f32[8,128]{1,0:T(8,128)S(1)}, f32[8,128]{1,0:T(8,128)S(1)}, u32[]{:S(2)}, u32[]{:S(2)}) %collective-permute-start.14) | collective-permute-done | bytes 4128 | tf_op jit(solution)/shard_map/ppermute | solution.py:372
  44.1 1.5 %collective-permute-start.15 = (f32[2,8,128]{2,1,0:T(8,128)S(1)}, f32[2,8,128]{2,1,0:T(8,128)S(1)}, u32[]{:S(2)}, u32[]{:S(2)}) collective-permute-start(f32[2,8,128]{2,1,0:T(8,128)S(1)} %maximum_select_fusion.g0), channel_id=1, source_target_pairs={{0,6},{1,7},{2,4},{3,5},{4,2},{5,3},{6,0},{7,1},{8,14},{9,15},{10,... | collective-permute-start | bytes 24584 | tf_op jit(solution)/shard_map/ppermute | solution.py:375
  45.6 0.1 collective-permute-start.16
  45.7 2.8 %collective-permute-start.17 = (f32[2,8,128]{2,1,0:T(8,128)S(1)}, f32[2,8,128]{2,1,0:T(8,128)S(1)}, u32[]{:S(2)}, u32[]{:S(2)}) collective-permute-start(f32[2,8,128]{2,1,0:T(8,128)S(1)} %maximum_select_fusion.g0), channel_id=1, source_target_pairs={{0,2},{1,3},{2,0},{3,1},{4,6},{5,7},{6,4},{7,5},{8,10},{9,11},{10,... | collective-permute-start | bytes 24584 | tf_op jit(solution)/shard_map/ppermute | solution.py:375
  48.5 1.1 %collective-permute-done.15.g3 = f32[2,8,128]{2,1,0:T(8,128)S(1)} collective-permute-done((f32[2,8,128]{2,1,0:T(8,128)S(1)}, f32[2,8,128]{2,1,0:T(8,128)S(1)}, u32[]{:S(2)}, u32[]{:S(2)}) %collective-permute-start.15) | collective-permute-done | bytes 8224 | tf_op jit(solution)/shard_map/ppermute | solution.py:375
  49.5 0.7 %collective-permute-done.16.g2 = f32[2,8,128]{2,1,0:T(8,128)S(1)} collective-permute-done((f32[2,8,128]{2,1,0:T(8,128)S(1)}, f32[2,8,128]{2,1,0:T(8,128)S(1)}, u32[]{:S(2)}, u32[]{:S(2)}) %collective-permute-start.16) | collective-permute-done | bytes 8224 | tf_op jit(solution)/shard_map/ppermute | solution.py:375
  50.2 0.7 %shard_map.94 = f32[1,4,128]{2,1,0:T(4,128)} custom-call(f32[2,8,128]{2,1,0:T(8,128)S(1)} %maximum_select_fusion.g0, f32[2,8,128]{2,1,0:T(8,128)S(1)} %collective-permute-done.15.g3, f32[2,8,128]{2,1,0:T(8,128)S(1)} %collective-permute-done.16.g2, f32[2,8,128]{2,1,0:T(8,128)S(1)} %collective-permute-done.17.g1), custom_call_target="tpu_custom_call" | custom-call | flops 1 | bytes 1 | tf_op jit(solution)/shard_map/pallas_call | solution.py:478
  (13 shorter events, 0.1 us)
Async XLA Ops:
  0.0 7.4 %copy-start = (bf16[4,4,128,256]{3,2,1,0:T(8,128)(2,1)S(1)}, bf16[4,4,128,256]{3,2,1,0:T(8,128)(2,1)}, u32[]{:S(2)}) copy-start(bf16[4,4,128,256]{3,2,1,0:T(8,128)(2,1)} %param.8) | copy-start | bytes 3145732
  2.3 5.3 %copy-start.1 = (bf16[8,16,128]{2,1,0:T(8,128)(2,1)S(1)}, bf16[8,16,128]{2,1,0:T(8,128)(2,1)}, u32[]{:S(2)}) copy-start(bf16[8,16,128]{2,1,0:T(8,128)(2,1)} %get-tuple-element.35.own_taps) | copy-start | bytes 98308
  2.3 23.2 %all-to-all-start = ((bf16[4,560,256]{2,1,0:T(8,128)(2,1)}), bf16[4,560,256]{2,1,0:T(8,128)(2,1)S(1)}, u32[]{:S(2)}, u32[]{:S(2)}) async-start(bf16[4,560,256]{2,1,0:T(8,128)(2,1)} %get-tuple-element.43), calls=%async_computation | async-start | bytes 2293760 | tf_op jit(solution)/shard_map/all_to_all | solution.py:420
  7.5 1.7 %collective-permute-start.1 = (bf16[4,128,256]{2,1,0:T(8,128)(2,1)S(1)}, bf16[4,128,256]{2,1,0:T(8,128)(2,1)S(1)}, u32[]{:S(2)}, u32[]{:S(2)}) collective-permute-start(bf16[4,128,256]{2,1,0:T(8,128)(2,1)S(1)} %dynamic-slice_bitcast_fusion.own), channel_id=1, source_target_pairs={{0,1},{1,0},{2,3},{3,2},{4,5},{5,4},{6,7},{7,6},{8,9},{9,8},{10,11... | collective-permute-start | bytes 786440 | tf_op jit(solution)/shard_map/ppermute | solution.py:372
  7.6 1.6 %collective-permute-start = (bf16[8,16,128]{2,1,0:T(8,128)(2,1)S(1)}, bf16[8,16,128]{2,1,0:T(8,128)(2,1)S(1)}, u32[]{:S(2)}, u32[]{:S(2)}) collective-permute-start(bf16[8,16,128]{2,1,0:T(8,128)(2,1)S(1)} %copy-done.1), channel_id=1, source_target_pairs={{0,1},{1,0},{2,3},{3,2},{4,5},{5,4},{6,7},{7,6},{8,9},{9,8},{10,11... | collective-permute-start | bytes 98312 | tf_op jit(solution)/shard_map/ppermute | solution.py:372
  9.3 10.5 %collective-permute-start.2 = (bf16[160,256]{1,0:T(8,128)(2,1)S(1)}, bf16[160,256]{1,0:T(8,128)(2,1)S(1)}, u32[]{:S(2)}, u32[]{:S(2)}) collective-permute-start(bf16[160,256]{1,0:T(8,128)(2,1)S(1)} %get-tuple-element.37), channel_id=1, source_target_pairs={{0,6},{1,7},{2,4},{3,5},{4,2},{5,3},{6,0},{7,1},{8,14},{9,15},{10,... | collective-permute-start | bytes 245768 | tf_op jit(solution)/shard_map/ppermute | solution.py:375
  12.9 6.8 %collective-permute-start.4 = (bf16[160,256]{1,0:T(8,128)(2,1)S(1)}, bf16[160,256]{1,0:T(8,128)(2,1)S(1)}, u32[]{:S(2)}, u32[]{:S(2)}) collective-permute-start(bf16[160,256]{1,0:T(8,128)(2,1)S(1)} %get-tuple-element.39), channel_id=1, source_target_pairs={{0,2},{1,3},{2,0},{3,1},{4,6},{5,7},{6,4},{7,5},{8,10},{9,11},{10,... | collective-permute-start | bytes 245768 | tf_op jit(solution)/shard_map/ppermute | solution.py:375
  12.9 6.8 %collective-permute-start.3 = (bf16[144,256]{1,0:T(8,128)(2,1)S(1)}, bf16[144,256]{1,0:T(8,128)(2,1)S(1)}, u32[]{:S(2)}, u32[]{:S(2)}) collective-permute-start(bf16[144,256]{1,0:T(8,128)(2,1)S(1)} %get-tuple-element.38), channel_id=1, source_target_pairs={{0,4},{1,5},{2,6},{3,7},{4,0},{5,1},{6,2},{7,3},{8,12},{9,13},{10,... | collective-permute-start | bytes 221192 | tf_op jit(solution)/shard_map/ppermute | solution.py:375
  19.8 9.0 %collective-permute-start.5 = (bf16[512,256]{1,0:T(8,128)(2,1)S(1)}, bf16[512,256]{1,0:T(8,128)(2,1)S(1)}, u32[]{:S(2)}, u32[]{:S(2)}) collective-permute-start(bf16[512,256]{1,0:T(8,128)(2,1)S(1)} %shard_map.85.refs_0_), channel_id=1, source_target_pairs={{0,1},{1,0},{2,3},{3,2},{4,5},{5,4},{6,7},{7,6},{8,9},{9,8},{10,11... | collective-permute-start | bytes 786440 | tf_op jit(solution)/shard_map/ppermute | solution.py:372
  19.9 9.0 %collective-permute-start.6 = (bf16[512,256]{1,0:T(8,128)(2,1)S(1)}, bf16[512,256]{1,0:T(8,128)(2,1)S(1)}, u32[]{:S(2)}, u32[]{:S(2)}) collective-permute-start(bf16[512,256]{1,0:T(8,128)(2,1)S(1)} %shard_map.85.refs_0_), channel_id=1, source_target_pairs={{0,8},{1,2},{2,1},{3,4},{4,3},{5,6},{6,5},{7,15},{8,0},{9,10},{10,... | collective-permute-start | bytes 786440 | tf_op jit(solution)/shard_map/ppermute | solution.py:388
  22.0 6.9 %collective-permute-start.7 = (bf16[96,256]{1,0:T(8,128)(2,1)S(1)}, bf16[96,256]{1,0:T(8,128)(2,1)S(1)}, u32[]{:S(2)}, u32[]{:S(2)}) collective-permute-start(bf16[96,256]{1,0:T(8,128)(2,1)S(1)} %shard_map.84.q0), channel_id=1, source_target_pairs={{0,24},{8,16},{16,8},{24,0},{1,25},{9,17},{17,9},{25,1},{2,26},{10... | collective-permute-start | bytes 147464 | tf_op jit(solution)/shard_map/ppermute | solution.py:378
  23.5 5.4 %collective-permute-start.8 = (bf16[96,256]{1,0:T(8,128)(2,1)S(1)}, bf16[96,256]{1,0:T(8,128)(2,1)S(1)}, u32[]{:S(2)}, u32[]{:S(2)}) collective-permute-start(bf16[96,256]{1,0:T(8,128)(2,1)S(1)} %shard_map.84.q0), channel_id=1, source_target_pairs={{0,16},{8,24},{16,0},{24,8},{1,17},{9,25},{17,1},{25,9},{2,18},{10... | collective-permute-start | bytes 147464 | tf_op jit(solution)/shard_map/ppermute | solution.py:378
  23.5 5.3 %collective-permute-start.9 = (bf16[96,256]{1,0:T(8,128)(2,1)S(1)}, bf16[96,256]{1,0:T(8,128)(2,1)S(1)}, u32[]{:S(2)}, u32[]{:S(2)}) collective-permute-start(bf16[96,256]{1,0:T(8,128)(2,1)S(1)} %shard_map.84.q0), channel_id=1, source_target_pairs={{0,8},{8,0},{16,24},{24,16},{1,9},{9,1},{17,25},{25,17},{2,10},{10... | collective-permute-start | bytes 147464 | tf_op jit(solution)/shard_map/ppermute | solution.py:378
  28.9 2.0 %collective-permute-start.10 = (bf16[2,528,256]{2,1,0:T(8,128)(2,1)S(1)}, bf16[2,528,256]{2,1,0:T(8,128)(2,1)S(1)}, u32[]{:S(2)}, u32[]{:S(2)}) collective-permute-start(bf16[2,528,256]{2,1,0:T(8,128)(2,1)S(1)} %get-tuple-element.47), channel_id=1, source_target_pairs={{0,1},{1,0},{2,3},{3,2},{4,5},{5,4},{6,7},{7,6},{8,9},{9,8},{10,11... | collective-permute-start | bytes 1622024 | tf_op jit(solution)/shard_map/ppermute | solution.py:372
  30.0 7.1 %collective-permute-start.13 = (bf16[2,528,256]{2,1,0:T(8,128)(2,1)S(1)}, bf16[2,528,256]{2,1,0:T(8,128)(2,1)S(1)}, u32[]{:S(2)}, u32[]{:S(2)}) collective-permute-start(bf16[2,528,256]{2,1,0:T(8,128)(2,1)S(1)} %get-tuple-element.60), channel_id=1, source_target_pairs={{0,1},{1,0},{2,3},{3,2},{4,5},{5,4},{6,7},{7,6},{8,9},{9,8},{10,11... | collective-permute-start | bytes 1622024 | tf_op jit(solution)/shard_map/ppermute | solution.py:372
  32.5 2.8 %copy-start.2 = (bf16[256]{0:T(256)(128)(2,1)S(1)}, bf16[256]{0:T(256)(128)(2,1)}, u32[]{:S(2)}) copy-start(bf16[256]{0:T(256)(128)(2,1)} %param.15) | copy-start | bytes 1540
  33.6 6.4 %collective-permute-start.11 = (bf16[512,256]{1,0:T(8,128)(2,1)S(1)}, bf16[512,256]{1,0:T(8,128)(2,1)S(1)}, u32[]{:S(2)}, u32[]{:S(2)}) collective-permute-start(bf16[512,256]{1,0:T(8,128)(2,1)S(1)} %shard_map.89.refs_0_), channel_id=1, source_target_pairs={{0,8},{1,2},{2,1},{3,4},{4,3},{5,6},{6,5},{7,15},{8,0},{9,10},{10,... | collective-permute-start | bytes 786440 | tf_op jit(solution)/shard_map/ppermute | solution.py:388
  35.3 4.7 %collective-permute-start.12 = (bf16[512,256]{1,0:T(8,128)(2,1)S(1)}, bf16[512,256]{1,0:T(8,128)(2,1)S(1)}, u32[]{:S(2)}, u32[]{:S(2)}) collective-permute-start(bf16[512,256]{1,0:T(8,128)(2,1)S(1)} %shard_map.89.refs_0_), channel_id=1, source_target_pairs={{0,1},{1,0},{2,3},{3,2},{4,5},{5,4},{6,7},{7,6},{8,9},{9,8},{10,11... | collective-permute-start | bytes 786440 | tf_op jit(solution)/shard_map/ppermute | solution.py:372
  42.9 1.2 %collective-permute-start.14 = (f32[8,128]{1,0:T(8,128)S(1)}, f32[8,128]{1,0:T(8,128)S(1)}, u32[]{:S(2)}, u32[]{:S(2)}) collective-permute-start(f32[8,128]{1,0:T(8,128)S(1)} %shard_map.93), channel_id=1, source_target_pairs={{0,1},{1,0},{2,3},{3,2},{4,5},{5,4},{6,7},{7,6},{8,9},{9,8},{10,11... | collective-permute-start | bytes 12296 | tf_op jit(solution)/shard_map/ppermute | solution.py:372
  44.1 5.4 %collective-permute-start.15 = (f32[2,8,128]{2,1,0:T(8,128)S(1)}, f32[2,8,128]{2,1,0:T(8,128)S(1)}, u32[]{:S(2)}, u32[]{:S(2)}) collective-permute-start(f32[2,8,128]{2,1,0:T(8,128)S(1)} %maximum_select_fusion.g0), channel_id=1, source_target_pairs={{0,6},{1,7},{2,4},{3,5},{4,2},{5,3},{6,0},{7,1},{8,14},{9,15},{10,... | collective-permute-start | bytes 24584 | tf_op jit(solution)/shard_map/ppermute | solution.py:375
  45.6 4.6 %collective-permute-start.16 = (f32[2,8,128]{2,1,0:T(8,128)S(1)}, f32[2,8,128]{2,1,0:T(8,128)S(1)}, u32[]{:S(2)}, u32[]{:S(2)}) collective-permute-start(f32[2,8,128]{2,1,0:T(8,128)S(1)} %maximum_select_fusion.g0), channel_id=1, source_target_pairs={{0,4},{1,5},{2,6},{3,7},{4,0},{5,1},{6,2},{7,3},{8,12},{9,13},{10,... | collective-permute-start | bytes 24584 | tf_op jit(solution)/shard_map/ppermute | solution.py:375
  45.7 4.5 %collective-permute-start.17 = (f32[2,8,128]{2,1,0:T(8,128)S(1)}, f32[2,8,128]{2,1,0:T(8,128)S(1)}, u32[]{:S(2)}, u32[]{:S(2)}) collective-permute-start(f32[2,8,128]{2,1,0:T(8,128)S(1)} %maximum_select_fusion.g0), channel_id=1, source_target_pairs={{0,2},{1,3},{2,0},{3,1},{4,6},{5,7},{6,4},{7,5},{8,10},{9,11},{10,... | collective-permute-start | bytes 24584 | tf_op jit(solution)/shard_map/ppermute | solution.py:375

commit v8 on v7

--- a/solution.py
+++ b/solution.py
@@ -382,7 +382,7 @@
         for a in range(4):
             for q in range(spaces):
                 other = q - 1 if q % 2 == 0 else q + 1
-                to = a * spaces + other if 0 <= other < spaces else (a ^ 1) * spaces + q
+                to = a * spaces + other if 0 <= other < spaces else (a ^ 2) * spaces + q
                 if ends or 0 <= other < spaces:
                     pairs.append((a * spaces + q, to))
         return lax.ppermute(array, ("section", "space"), pairs)

time: 51.2 us -> 51.2 us (level)
  transfers between devices with their start and end apart: 19 -> 19, of which waited for: 8 -> 11; matrix products, arithmetic and copies ran while one was open for 0% -> 0% of each run, Pallas kernels for 12% -> 12%
where the time goes in v8:
time: 51.2 us; the launch traced here: 50.9 us
  starting transfers between devices  22.4 us (44%)
  waiting for transfers between devices  16.1 us (31%)
  Pallas kernels  12.1 us (24%)
    ppermute x6, starting transfers between devices, chip(): return lax.ppermute(array, 'space', [(i, i ^ 2 * k) for i in range(spaces)])  8.84 us
    ppermute x6, waiting for transfers between devices, chip(): return lax.ppermute(array, 'space', [(i, i ^ 2 * k) for i in range(spaces)])  7.68 us
    pallas_call x4, Pallas kernels, run(): call(functools.partial(layer_kernel, layer, len(cells), final), outs, [VM...  5.55 us
    all_to_all x1, starting transfers between devices, window_on_section(): lax.all_to_all(packed, 'section', split_axis=0, concat_axis=0, tiled=True)  5.18 us
    ppermute x2, starting transfers between devices, beside(): return lax.ppermute(array, ('section', 'space'), pairs)  3.69 us
    ppermute x3, starting transfers between devices, section(): return lax.ppermute(array, 'section', [(i, i ^ k) for i in range(4)])  3.49 us
    ppermute x2, waiting for transfers between devices, beside(): return lax.ppermute(array, ('section', 'space'), pairs)  3.12 us
    ppermute x3, waiting for transfers between devices, section(): return lax.ppermute(array, 'section', [(i, i ^ k) for i in range(4)])  2.74 us
  transfers between devices with their start and end apart: 19, of which 11 were waited for; matrix products, arithmetic and copies ran while one was open for 0% of the time, Pallas kernels for 12%

profile of v8, /device:TPU:0, one launch (start us, length us, event | category | flops | bytes accessed | tf_op | source)
XLA Modules:
  0.0 50.9 jit_solution(11531864858721909467)
XLA Ops:
  0.0 2.2 %shard_map.82 = (bf16[4,560,256]{2,1,0:T(8,128)(2,1)}, bf16[8,16,128]{2,1,0:T(8,128)(2,1)}) custom-call(bf16[1,15,4,128]{3,2,1,0:T(4,128)(2,1)} %row_coef.1, bf16[1,15,16,32]{3,2,1,0:T(8,128)(2,1)} %col_coef.1, bf16[1,256,512]{2,1,0:T(8,128)(2,1)} %weight_in.1, bf16[1,512,256]{2,1,0:T(8,128)(2,1)} %weight_out.1, bf16[1,512]{1,0:T(2,128)(2,1)} %bias.1, ...), custom_call_target="tpu_custom_call" | custom-call | flops 1 | bytes 1 | tf_op jit(solution)/shard_map/pallas_call | solution.py:392
  2.3 5.2 %all-to-all-start = ((bf16[4,560,256]{2,1,0:T(8,128)(2,1)}), bf16[4,560,256]{2,1,0:T(8,128)(2,1)S(1)}, u32[]{:S(2)}, u32[]{:S(2)}) async-start(bf16[4,560,256]{2,1,0:T(8,128)(2,1)} %get-tuple-element.43), calls=%async_computation | async-start | bytes 2293760 | tf_op jit(solution)/shard_map/all_to_all | solution.py:420
  7.5 0.1 collective-permute-start.1
  7.6 0.5 collective-permute-start
  8.0 1.1 %collective-permute-done.sib_taps = bf16[8,16,128]{2,1,0:T(8,128)(2,1)S(1)} collective-permute-done((bf16[8,16,128]{2,1,0:T(8,128)(2,1)S(1)}, bf16[8,16,128]{2,1,0:T(8,128)(2,1)S(1)}, u32[]{:S(2)}, u32[]{:S(2)}) %collective-permute-start) | collective-permute-done | bytes 32800 | tf_op jit(solution)/shard_map/ppermute | solution.py:372
  9.1 0.0 collective-permute-done.1.sib
  9.1 0.1 shard_map.83
  9.3 3.7 %collective-permute-start.2 = (bf16[160,256]{1,0:T(8,128)(2,1)S(1)}, bf16[160,256]{1,0:T(8,128)(2,1)S(1)}, u32[]{:S(2)}, u32[]{:S(2)}) collective-permute-start(bf16[160,256]{1,0:T(8,128)(2,1)S(1)} %get-tuple-element.37), channel_id=1, source_target_pairs={{0,6},{1,7},{2,4},{3,5},{4,2},{5,3},{6,0},{7,1},{8,14},{9,15},{10,... | collective-permute-start | bytes 245768 | tf_op jit(solution)/shard_map/ppermute | solution.py:375
  12.9 0.0 collective-permute-start.4
  12.9 0.8 %collective-permute-start.3 = (bf16[144,256]{1,0:T(8,128)(2,1)S(1)}, bf16[144,256]{1,0:T(8,128)(2,1)S(1)}, u32[]{:S(2)}, u32[]{:S(2)}) collective-permute-start(bf16[144,256]{1,0:T(8,128)(2,1)S(1)} %get-tuple-element.38), channel_id=1, source_target_pairs={{0,4},{1,5},{2,6},{3,7},{4,0},{5,1},{6,2},{7,3},{8,12},{9,13},{10,... | collective-permute-start | bytes 221192 | tf_op jit(solution)/shard_map/ppermute | solution.py:375
  13.7 6.0 %collective-permute-done.3.g2 = bf16[144,256]{1,0:T(8,128)(2,1)S(1)} collective-permute-done((bf16[144,256]{1,0:T(8,128)(2,1)S(1)}, bf16[144,256]{1,0:T(8,128)(2,1)S(1)}, u32[]{:S(2)}, u32[]{:S(2)}) %collective-permute-start.3) | collective-permute-done | bytes 73760 | tf_op jit(solution)/shard_map/ppermute | solution.py:375
  19.8 0.0 collective-permute-done.2.g3
  19.8 0.0 collective-permute-done.4.g1
  19.8 0.1 collective-permute-start.5
  19.9 2.1 %collective-permute-start.6 = (bf16[512,256]{1,0:T(8,128)(2,1)S(1)}, bf16[512,256]{1,0:T(8,128)(2,1)S(1)}, u32[]{:S(2)}, u32[]{:S(2)}) collective-permute-start(bf16[512,256]{1,0:T(8,128)(2,1)S(1)} %shard_map.85.refs_0_), channel_id=1, source_target_pairs={{0,16},{1,2},{2,1},{3,4},{4,3},{5,6},{6,5},{7,23},{8,24},{9,10},{1... | collective-permute-start | bytes 786440 | tf_op jit(solution)/shard_map/ppermute | solution.py:388
  22.0 1.5 %collective-permute-start.7 = (bf16[96,256]{1,0:T(8,128)(2,1)S(1)}, bf16[96,256]{1,0:T(8,128)(2,1)S(1)}, u32[]{:S(2)}, u32[]{:S(2)}) collective-permute-start(bf16[96,256]{1,0:T(8,128)(2,1)S(1)} %shard_map.84.q0), channel_id=1, source_target_pairs={{0,24},{8,16},{16,8},{24,0},{1,25},{9,17},{17,9},{25,1},{2,26},{10... | collective-permute-start | bytes 147464 | tf_op jit(solution)/shard_map/ppermute | solution.py:378
  23.5 1.5 %collective-permute-start.8 = (bf16[96,256]{1,0:T(8,128)(2,1)S(1)}, bf16[96,256]{1,0:T(8,128)(2,1)S(1)}, u32[]{:S(2)}, u32[]{:S(2)}) collective-permute-start(bf16[96,256]{1,0:T(8,128)(2,1)S(1)} %shard_map.84.q0), channel_id=1, source_target_pairs={{0,16},{8,24},{16,0},{24,8},{1,17},{9,25},{17,1},{25,9},{2,18},{10... | collective-permute-start | bytes 147464 | tf_op jit(solution)/shard_map/ppermute | solution.py:378
  24.9 0.6 %collective-permute-start.9 = (bf16[96,256]{1,0:T(8,128)(2,1)S(1)}, bf16[96,256]{1,0:T(8,128)(2,1)S(1)}, u32[]{:S(2)}, u32[]{:S(2)}) collective-permute-start(bf16[96,256]{1,0:T(8,128)(2,1)S(1)} %shard_map.84.q0), channel_id=1, source_target_pairs={{0,8},{8,0},{16,24},{24,16},{1,9},{9,1},{17,25},{25,17},{2,10},{10... | collective-permute-start | bytes 147464 | tf_op jit(solution)/shard_map/ppermute | solution.py:378
  25.5 0.0 all-to-all-done.weights.refs_6_.refs_4_.refs_5_
  25.5 0.1 fusion
  25.6 0.7 %shard_map.87 = (bf16[512,512]{1,0:T(8,128)(2,1)S(1)}, bf16[512,512]{1,0:T(8,128)(2,1)S(1)}) custom-call(bf16[4,560,256]{2,1,0:T(8,128)(2,1)S(1)} %all-to-all-done.weights.refs_6_.refs_4_.refs_5_), custom_call_target="tpu_custom_call" | custom-call | flops 1 | bytes 1 | tf_op jit(solution)/shard_map/pallas_call | solution.py:443
  26.3 0.8 %collective-permute-done.7.q3 = bf16[96,256]{1,0:T(8,128)(2,1)S(1)} collective-permute-done((bf16[96,256]{1,0:T(8,128)(2,1)S(1)}, bf16[96,256]{1,0:T(8,128)(2,1)S(1)}, u32[]{:S(2)}, u32[]{:S(2)}) %collective-permute-start.7) | collective-permute-done | bytes 49184 | tf_op jit(solution)/shard_map/ppermute | solution.py:378
  27.1 1.4 %collective-permute-done.8.q2 = bf16[96,256]{1,0:T(8,128)(2,1)S(1)} collective-permute-done((bf16[96,256]{1,0:T(8,128)(2,1)S(1)}, bf16[96,256]{1,0:T(8,128)(2,1)S(1)}, u32[]{:S(2)}, u32[]{:S(2)}) %collective-permute-start.8) | collective-permute-done | bytes 49184 | tf_op jit(solution)/shard_map/ppermute | solution.py:378
  28.5 0.6 %collective-permute-done.9.q1 = bf16[96,256]{1,0:T(8,128)(2,1)S(1)} collective-permute-done((bf16[96,256]{1,0:T(8,128)(2,1)S(1)}, bf16[96,256]{1,0:T(8,128)(2,1)S(1)}, u32[]{:S(2)}, u32[]{:S(2)}) %collective-permute-start.9) | collective-permute-done | bytes 49184 | tf_op jit(solution)/shard_map/ppermute | solution.py:378
  29.0 0.0 collective-permute-done.5.refs_1_
  29.0 0.0 collective-permute-done.6.refs_2_
  29.0 1.0 %shard_map.86 = (bf16[512,512]{1,0:T(8,128)(2,1)S(1)}, bf16[4,256,384]{2,1,0:T(8,128)(2,1)S(1)}, bf16[4,128,256]{2,1,0:T(8,128)(2,1)S(1)}) custom-call(bf16[96,256]{1,0:T(8,128)(2,1)S(1)} %shard_map.84.q0, bf16[96,256]{1,0:T(8,128)(2,1)S(1)} %collective-permute-done.7.q3, bf16[96,256]{1,0:T(8,128)(2,1)S(1)} %collective-permute-done.8.q2, ...), custom_call_target="tpu_custom_call" | custom-call | flops 1 | bytes 1 | tf_op jit(solution)/shard_map/pallas_call | solution.py:435
  30.0 0.6 %collective-permute-start.13 = (bf16[2,528,256]{2,1,0:T(8,128)(2,1)S(1)}, bf16[2,528,256]{2,1,0:T(8,128)(2,1)S(1)}, u32[]{:S(2)}, u32[]{:S(2)}) collective-permute-start(bf16[2,528,256]{2,1,0:T(8,128)(2,1)S(1)} %get-tuple-element.60), channel_id=1, source_target_pairs={{0,1},{1,0},{2,3},{3,2},{4,5},{5,4},{6,7},{7,6},{8,9},{9,8},{10,11... | collective-permute-start | bytes 1622024 | tf_op jit(solution)/shard_map/ppermute | solution.py:372
  30.6 0.4 collective-permute-done.10.refs_7_.refs_5_
  31.0 1.6 %shard_map.88 = (bf16[512,256]{1,0:T(8,128)(2,1)S(1)}, bf16[512,256]{1,0:T(8,128)(2,1)S(1)}) custom-call(bf16[512,256]{1,0:T(8,128)(2,1)S(1)} %shard_map.85.refs_0_, bf16[512,256]{1,0:T(8,128)(2,1)S(1)} %collective-permute-done.5.refs_1_, bf16[512,256]{1,0:T(8,128)(2,1)S(1)} %collective-permute-done.6.refs_2_, ...), custom_call_target="tpu_custom_call" | custom-call | flops 1 | bytes 1 | tf_op jit(solution)/shard_map/pallas_call | solution.py:454
  32.6 0.0 copy-start.2
  32.6 1.0 %shard_map.89.refs_0_ = bf16[512,256]{1,0:T(8,128)(2,1)S(1)} custom-call(bf16[512,256]{1,0:T(8,128)(2,1)S(1)} %get-tuple-element.48.refs_0_, bf16[512,256]{1,0:T(8,128)(2,1)S(1)} %get-tuple-element.49.refs_1_, bf16[4,128,256]{2,1,0:T(8,128)(2,1)S(1)} %get-tuple-element.50.refs_2_, bf16[512,512]{1,0:T(8,128)(2,1)S(1)} %get-tuple-element.51.refs_3_, ...), custom_call_target="tpu_custom_call" | custom-call | flops 1 | bytes 1 | tf_op jit(solution)/shard_map/pallas_call | solution.py:454
  33.7 1.6 %collective-permute-start.11 = (bf16[512,256]{1,0:T(8,128)(2,1)S(1)}, bf16[512,256]{1,0:T(8,128)(2,1)S(1)}, u32[]{:S(2)}, u32[]{:S(2)}) collective-permute-start(bf16[512,256]{1,0:T(8,128)(2,1)S(1)} %shard_map.89.refs_0_), channel_id=1, source_target_pairs={{0,16},{1,2},{2,1},{3,4},{4,3},{5,6},{6,5},{7,23},{8,24},{9,10},{1... | collective-permute-start | bytes 786440 | tf_op jit(solution)/shard_map/ppermute | solution.py:388
  35.3 0.0 collective-permute-start.12
  35.3 0.7 %shard_map.91 = (bf16[512,512]{1,0:T(8,128)(2,1)S(1)}, bf16[512,512]{1,0:T(8,128)(2,1)S(1)}) custom-call(bf16[4,560,256]{2,1,0:T(8,128)(2,1)S(1)} %all-to-all-done.weights.refs_6_.refs_4_.refs_5_), custom_call_target="tpu_custom_call" | custom-call | flops 1 | bytes 1 | tf_op jit(solution)/shard_map/pallas_call | solution.py:443
  36.0 1.0 %shard_map.90 = (bf16[512,512]{1,0:T(8,128)(2,1)S(1)}, bf16[4,256,384]{2,1,0:T(8,128)(2,1)S(1)}, bf16[4,128,256]{2,1,0:T(8,128)(2,1)S(1)}) custom-call(bf16[96,256]{1,0:T(8,128)(2,1)S(1)} %shard_map.84.q0, bf16[96,256]{1,0:T(8,128)(2,1)S(1)} %collective-permute-done.7.q3, bf16[96,256]{1,0:T(8,128)(2,1)S(1)} %collective-permute-done.8.q2, ...), custom_call_target="tpu_custom_call" | custom-call | flops 1 | bytes 1 | tf_op jit(solution)/shard_map/pallas_call | solution.py:435
  37.0 3.1 %collective-permute-done.11.refs_1_ = bf16[512,256]{1,0:T(8,128)(2,1)S(1)} collective-permute-done((bf16[512,256]{1,0:T(8,128)(2,1)S(1)}, bf16[512,256]{1,0:T(8,128)(2,1)S(1)}, u32[]{:S(2)}, u32[]{:S(2)}) %collective-permute-start.11) | collective-permute-done | bytes 262176 | tf_op jit(solution)/shard_map/ppermute | solution.py:388
  40.1 1.7 %shard_map.92 = (bf16[512,256]{1,0:T(8,128)(2,1)S(1)}, bf16[512,256]{1,0:T(8,128)(2,1)S(1)}) custom-call(bf16[512,256]{1,0:T(8,128)(2,1)S(1)} %shard_map.89.refs_0_, bf16[512,256]{1,0:T(8,128)(2,1)S(1)} %collective-permute-done.11.refs_1_, bf16[512,256]{1,0:T(8,128)(2,1)S(1)} %collective-permute-done.12.refs_2_, ...), custom_call_target="tpu_custom_call" | custom-call | flops 1 | bytes 1 | tf_op jit(solution)/shard_map/pallas_call | solution.py:454
  41.8 1.2 %shard_map.93 = f32[8,128]{1,0:T(8,128)S(1)} custom-call(bf16[512,256]{1,0:T(8,128)(2,1)S(1)} %get-tuple-element.61.refs_0_, bf16[512,256]{1,0:T(8,128)(2,1)S(1)} %get-tuple-element.62.refs_1_, bf16[4,128,256]{2,1,0:T(8,128)(2,1)S(1)} %get-tuple-element.63.refs_2_, bf16[512,512]{1,0:T(8,128)(2,1)S(1)} %get-tuple-element.64.refs_3_, ...), custom_call_target="tpu_custom_call" | custom-call | flops 1 | bytes 1 | tf_op jit(solution)/shard_map/pallas_call | solution.py:454
  43.0 0.0 collective-permute-start.14
  43.0 1.1 %collective-permute-done.14 = f32[8,128]{1,0:T(8,128)S(1)} collective-permute-done((f32[8,128]{1,0:T(8,128)S(1)}, f32[8,128]{1,0:T(8,128)S(1)}, u32[]{:S(2)}, u32[]{:S(2)}) %collective-permute-start.14) | collective-permute-done | bytes 4128 | tf_op jit(solution)/shard_map/ppermute | solution.py:372
  44.2 1.3 %collective-permute-start.15 = (f32[2,8,128]{2,1,0:T(8,128)S(1)}, f32[2,8,128]{2,1,0:T(8,128)S(1)}, u32[]{:S(2)}, u32[]{:S(2)}) collective-permute-start(f32[2,8,128]{2,1,0:T(8,128)S(1)} %maximum_select_fusion.g0), channel_id=1, source_target_pairs={{0,6},{1,7},{2,4},{3,5},{4,2},{5,3},{6,0},{7,1},{8,14},{9,15},{10,... | collective-permute-start | bytes 24584 | tf_op jit(solution)/shard_map/ppermute | solution.py:375
  45.5 0.1 collective-permute-start.16
  45.7 2.9 %collective-permute-start.17 = (f32[2,8,128]{2,1,0:T(8,128)S(1)}, f32[2,8,128]{2,1,0:T(8,128)S(1)}, u32[]{:S(2)}, u32[]{:S(2)}) collective-permute-start(f32[2,8,128]{2,1,0:T(8,128)S(1)} %maximum_select_fusion.g0), channel_id=1, source_target_pairs={{0,2},{1,3},{2,0},{3,1},{4,6},{5,7},{6,4},{7,5},{8,10},{9,11},{10,... | collective-permute-start | bytes 24584 | tf_op jit(solution)/shard_map/ppermute | solution.py:375
  48.6 1.1 %collective-permute-done.15.g3 = f32[2,8,128]{2,1,0:T(8,128)S(1)} collective-permute-done((f32[2,8,128]{2,1,0:T(8,128)S(1)}, f32[2,8,128]{2,1,0:T(8,128)S(1)}, u32[]{:S(2)}, u32[]{:S(2)}) %collective-permute-start.15) | collective-permute-done | bytes 8224 | tf_op jit(solution)/shard_map/ppermute | solution.py:375
  49.6 0.4 collective-permute-done.16.g2
  50.1 0.1 collective-permute-done.17.g1
  50.2 0.7 %shard_map.94 = f32[1,4,128]{2,1,0:T(4,128)} custom-call(f32[2,8,128]{2,1,0:T(8,128)S(1)} %maximum_select_fusion.g0, f32[2,8,128]{2,1,0:T(8,128)S(1)} %collective-permute-done.15.g3, f32[2,8,128]{2,1,0:T(8,128)S(1)} %collective-permute-done.16.g2, f32[2,8,128]{2,1,0:T(8,128)S(1)} %collective-permute-done.17.g1), custom_call_target="tpu_custom_call" | custom-call | flops 1 | bytes 1 | tf_op jit(solution)/shard_map/pallas_call | solution.py:478
  (13 shorter events, 0.1 us)
Async XLA Ops:
  0.0 7.4 %copy-start = (bf16[4,4,128,256]{3,2,1,0:T(8,128)(2,1)S(1)}, bf16[4,4,128,256]{3,2,1,0:T(8,128)(2,1)}, u32[]{:S(2)}) copy-start(bf16[4,4,128,256]{3,2,1,0:T(8,128)(2,1)} %param.8) | copy-start | bytes 3145732
  2.3 5.3 %copy-start.1 = (bf16[8,16,128]{2,1,0:T(8,128)(2,1)S(1)}, bf16[8,16,128]{2,1,0:T(8,128)(2,1)}, u32[]{:S(2)}) copy-start(bf16[8,16,128]{2,1,0:T(8,128)(2,1)} %get-tuple-element.35.own_taps) | copy-start | bytes 98308
  2.3 23.2 %all-to-all-start = ((bf16[4,560,256]{2,1,0:T(8,128)(2,1)}), bf16[4,560,256]{2,1,0:T(8,128)(2,1)S(1)}, u32[]{:S(2)}, u32[]{:S(2)}) async-start(bf16[4,560,256]{2,1,0:T(8,128)(2,1)} %get-tuple-element.43), calls=%async_computation | async-start | bytes 2293760 | tf_op jit(solution)/shard_map/all_to_all | solution.py:420
  7.5 1.7 %collective-permute-start.1 = (bf16[4,128,256]{2,1,0:T(8,128)(2,1)S(1)}, bf16[4,128,256]{2,1,0:T(8,128)(2,1)S(1)}, u32[]{:S(2)}, u32[]{:S(2)}) collective-permute-start(bf16[4,128,256]{2,1,0:T(8,128)(2,1)S(1)} %dynamic-slice_bitcast_fusion.own), channel_id=1, source_target_pairs={{0,1},{1,0},{2,3},{3,2},{4,5},{5,4},{6,7},{7,6},{8,9},{9,8},{10,11... | collective-permute-start | bytes 786440 | tf_op jit(solution)/shard_map/ppermute | solution.py:372
  7.6 1.6 %collective-permute-start = (bf16[8,16,128]{2,1,0:T(8,128)(2,1)S(1)}, bf16[8,16,128]{2,1,0:T(8,128)(2,1)S(1)}, u32[]{:S(2)}, u32[]{:S(2)}) collective-permute-start(bf16[8,16,128]{2,1,0:T(8,128)(2,1)S(1)} %copy-done.1), channel_id=1, source_target_pairs={{0,1},{1,0},{2,3},{3,2},{4,5},{5,4},{6,7},{7,6},{8,9},{9,8},{10,11... | collective-permute-start | bytes 98312 | tf_op jit(solution)/shard_map/ppermute | solution.py:372
  9.3 10.5 %collective-permute-start.2 = (bf16[160,256]{1,0:T(8,128)(2,1)S(1)}, bf16[160,256]{1,0:T(8,128)(2,1)S(1)}, u32[]{:S(2)}, u32[]{:S(2)}) collective-permute-start(bf16[160,256]{1,0:T(8,128)(2,1)S(1)} %get-tuple-element.37), channel_id=1, source_target_pairs={{0,6},{1,7},{2,4},{3,5},{4,2},{5,3},{6,0},{7,1},{8,14},{9,15},{10,... | collective-permute-start | bytes 245768 | tf_op jit(solution)/shard_map/ppermute | solution.py:375
  12.9 6.8 %collective-permute-start.4 = (bf16[160,256]{1,0:T(8,128)(2,1)S(1)}, bf16[160,256]{1,0:T(8,128)(2,1)S(1)}, u32[]{:S(2)}, u32[]{:S(2)}) collective-permute-start(bf16[160,256]{1,0:T(8,128)(2,1)S(1)} %get-tuple-element.39), channel_id=1, source_target_pairs={{0,2},{1,3},{2,0},{3,1},{4,6},{5,7},{6,4},{7,5},{8,10},{9,11},{10,... | collective-permute-start | bytes 245768 | tf_op jit(solution)/shard_map/ppermute | solution.py:375
  12.9 6.8 %collective-permute-start.3 = (bf16[144,256]{1,0:T(8,128)(2,1)S(1)}, bf16[144,256]{1,0:T(8,128)(2,1)S(1)}, u32[]{:S(2)}, u32[]{:S(2)}) collective-permute-start(bf16[144,256]{1,0:T(8,128)(2,1)S(1)} %get-tuple-element.38), channel_id=1, source_target_pairs={{0,4},{1,5},{2,6},{3,7},{4,0},{5,1},{6,2},{7,3},{8,12},{9,13},{10,... | collective-permute-start | bytes 221192 | tf_op jit(solution)/shard_map/ppermute | solution.py:375
  19.8 9.2 %collective-permute-start.5 = (bf16[512,256]{1,0:T(8,128)(2,1)S(1)}, bf16[512,256]{1,0:T(8,128)(2,1)S(1)}, u32[]{:S(2)}, u32[]{:S(2)}) collective-permute-start(bf16[512,256]{1,0:T(8,128)(2,1)S(1)} %shard_map.85.refs_0_), channel_id=1, source_target_pairs={{0,1},{1,0},{2,3},{3,2},{4,5},{5,4},{6,7},{7,6},{8,9},{9,8},{10,11... | collective-permute-start | bytes 786440 | tf_op jit(solution)/shard_map/ppermute | solution.py:372
  19.9 9.1 %collective-permute-start.6 = (bf16[512,256]{1,0:T(8,128)(2,1)S(1)}, bf16[512,256]{1,0:T(8,128)(2,1)S(1)}, u32[]{:S(2)}, u32[]{:S(2)}) collective-permute-start(bf16[512,256]{1,0:T(8,128)(2,1)S(1)} %shard_map.85.refs_0_), channel_id=1, source_target_pairs={{0,16},{1,2},{2,1},{3,4},{4,3},{5,6},{6,5},{7,23},{8,24},{9,10},{1... | collective-permute-start | bytes 786440 | tf_op jit(solution)/shard_map/ppermute | solution.py:388
  22.0 5.1 %collective-permute-start.7 = (bf16[96,256]{1,0:T(8,128)(2,1)S(1)}, bf16[96,256]{1,0:T(8,128)(2,1)S(1)}, u32[]{:S(2)}, u32[]{:S(2)}) collective-permute-start(bf16[96,256]{1,0:T(8,128)(2,1)S(1)} %shard_map.84.q0), channel_id=1, source_target_pairs={{0,24},{8,16},{16,8},{24,0},{1,25},{9,17},{17,9},{25,1},{2,26},{10... | collective-permute-start | bytes 147464 | tf_op jit(solution)/shard_map/ppermute | solution.py:378
  23.5 5.0 %collective-permute-start.8 = (bf16[96,256]{1,0:T(8,128)(2,1)S(1)}, bf16[96,256]{1,0:T(8,128)(2,1)S(1)}, u32[]{:S(2)}, u32[]{:S(2)}) collective-permute-start(bf16[96,256]{1,0:T(8,128)(2,1)S(1)} %shard_map.84.q0), channel_id=1, source_target_pairs={{0,16},{8,24},{16,0},{24,8},{1,17},{9,25},{17,1},{25,9},{2,18},{10... | collective-permute-start | bytes 147464 | tf_op jit(solution)/shard_map/ppermute | solution.py:378
  24.9 4.1 %collective-permute-start.9 = (bf16[96,256]{1,0:T(8,128)(2,1)S(1)}, bf16[96,256]{1,0:T(8,128)(2,1)S(1)}, u32[]{:S(2)}, u32[]{:S(2)}) collective-permute-start(bf16[96,256]{1,0:T(8,128)(2,1)S(1)} %shard_map.84.q0), channel_id=1, source_target_pairs={{0,8},{8,0},{16,24},{24,16},{1,9},{9,1},{17,25},{25,17},{2,10},{10... | collective-permute-start | bytes 147464 | tf_op jit(solution)/shard_map/ppermute | solution.py:378
  29.0 1.9 %collective-permute-start.10 = (bf16[2,528,256]{2,1,0:T(8,128)(2,1)S(1)}, bf16[2,528,256]{2,1,0:T(8,128)(2,1)S(1)}, u32[]{:S(2)}, u32[]{:S(2)}) collective-permute-start(bf16[2,528,256]{2,1,0:T(8,128)(2,1)S(1)} %get-tuple-element.47), channel_id=1, source_target_pairs={{0,1},{1,0},{2,3},{3,2},{4,5},{5,4},{6,7},{7,6},{8,9},{9,8},{10,11... | collective-permute-start | bytes 1622024 | tf_op jit(solution)/shard_map/ppermute | solution.py:372
  30.0 6.9 %collective-permute-start.13 = (bf16[2,528,256]{2,1,0:T(8,128)(2,1)S(1)}, bf16[2,528,256]{2,1,0:T(8,128)(2,1)S(1)}, u32[]{:S(2)}, u32[]{:S(2)}) collective-permute-start(bf16[2,528,256]{2,1,0:T(8,128)(2,1)S(1)} %get-tuple-element.60), channel_id=1, source_target_pairs={{0,1},{1,0},{2,3},{3,2},{4,5},{5,4},{6,7},{7,6},{8,9},{9,8},{10,11... | collective-permute-start | bytes 1622024 | tf_op jit(solution)/shard_map/ppermute | solution.py:372
  32.6 2.7 %copy-start.2 = (bf16[256]{0:T(256)(128)(2,1)S(1)}, bf16[256]{0:T(256)(128)(2,1)}, u32[]{:S(2)}) copy-start(bf16[256]{0:T(256)(128)(2,1)} %param.15) | copy-start | bytes 1540
  33.7 6.4 %collective-permute-start.11 = (bf16[512,256]{1,0:T(8,128)(2,1)S(1)}, bf16[512,256]{1,0:T(8,128)(2,1)S(1)}, u32[]{:S(2)}, u32[]{:S(2)}) collective-permute-start(bf16[512,256]{1,0:T(8,128)(2,1)S(1)} %shard_map.89.refs_0_), channel_id=1, source_target_pairs={{0,16},{1,2},{2,1},{3,4},{4,3},{5,6},{6,5},{7,23},{8,24},{9,10},{1... | collective-permute-start | bytes 786440 | tf_op jit(solution)/shard_map/ppermute | solution.py:388
  35.3 4.8 %collective-permute-start.12 = (bf16[512,256]{1,0:T(8,128)(2,1)S(1)}, bf16[512,256]{1,0:T(8,128)(2,1)S(1)}, u32[]{:S(2)}, u32[]{:S(2)}) collective-permute-start(bf16[512,256]{1,0:T(8,128)(2,1)S(1)} %shard_map.89.refs_0_), channel_id=1, source_target_pairs={{0,1},{1,0},{2,3},{3,2},{4,5},{5,4},{6,7},{7,6},{8,9},{9,8},{10,11... | collective-permute-start | bytes 786440 | tf_op jit(solution)/shard_map/ppermute | solution.py:372
  43.0 1.2 %collective-permute-start.14 = (f32[8,128]{1,0:T(8,128)S(1)}, f32[8,128]{1,0:T(8,128)S(1)}, u32[]{:S(2)}, u32[]{:S(2)}) collective-permute-start(f32[8,128]{1,0:T(8,128)S(1)} %shard_map.93), channel_id=1, source_target_pairs={{0,1},{1,0},{2,3},{3,2},{4,5},{5,4},{6,7},{7,6},{8,9},{9,8},{10,11... | collective-permute-start | bytes 12296 | tf_op jit(solution)/shard_map/ppermute | solution.py:372
  44.2 5.4 %collective-permute-start.15 = (f32[2,8,128]{2,1,0:T(8,128)S(1)}, f32[2,8,128]{2,1,0:T(8,128)S(1)}, u32[]{:S(2)}, u32[]{:S(2)}) collective-permute-start(f32[2,8,128]{2,1,0:T(8,128)S(1)} %maximum_select_fusion.g0), channel_id=1, source_target_pairs={{0,6},{1,7},{2,4},{3,5},{4,2},{5,3},{6,0},{7,1},{8,14},{9,15},{10,... | collective-permute-start | bytes 24584 | tf_op jit(solution)/shard_map/ppermute | solution.py:375
  45.5 4.5 %collective-permute-start.16 = (f32[2,8,128]{2,1,0:T(8,128)S(1)}, f32[2,8,128]{2,1,0:T(8,128)S(1)}, u32[]{:S(2)}, u32[]{:S(2)}) collective-permute-start(f32[2,8,128]{2,1,0:T(8,128)S(1)} %maximum_select_fusion.g0), channel_id=1, source_target_pairs={{0,4},{1,5},{2,6},{3,7},{4,0},{5,1},{6,2},{7,3},{8,12},{9,13},{10,... | collective-permute-start | bytes 24584 | tf_op jit(solution)/shard_map/ppermute | solution.py:375
  45.7 4.5 %collective-permute-start.17 = (f32[2,8,128]{2,1,0:T(8,128)S(1)}, f32[2,8,128]{2,1,0:T(8,128)S(1)}, u32[]{:S(2)}, u32[]{:S(2)}) collective-permute-start(f32[2,8,128]{2,1,0:T(8,128)S(1)} %maximum_select_fusion.g0), channel_id=1, source_target_pairs={{0,2},{1,3},{2,0},{3,1},{4,6},{5,7},{6,4},{7,5},{8,10},{9,11},{10,... | collective-permute-start | bytes 24584 | tf_op jit(solution)/shard_map/ppermute | solution.py:375
